TPU v7x, 32 devices: a whole 2x2x4 slice. The times are simulated.
32 devices in a mesh: ha: 8 (over y, x, core), wa: 4 (over z).
Axes of the slice: x: 2, y: 2, z: 4, core: 2. Of those that a mesh axis runs over, the one named last changes fastest.
Arguments:
- hw_plane: bfloat16 [256, 512, 128], P('ha', 'wa'), may hold values from -200 to 200
- zh_plane: bfloat16 [64, 256, 128], P(None, 'ha'), may hold values from -5 to 5
- wz_plane: bfloat16 [512, 64, 128], P('wa'), may hold values from -5 to 5
- w_in: bfloat16 [128, 256], replicated, may hold values from -0.5 to 0.5
- b_in: float32 [256], replicated, may hold values from -3 to 3
- w_out: bfloat16 [256, 18], replicated, may hold values from -0.75 to 0.75
- b_out: float32 [18], replicated, may hold values from -3 to 3
- run_index: int32 [32, 512], P(('ha', 'wa')), may hold values from 0 to 2047, as said below
- run_count: int32 [32], P(('ha', 'wa')), may hold values from 1 to 511, as said below
- labels: int32 [32, 512, 128], P(('ha', 'wa')), may hold values from 0 to 17
Outputs:
- hw_grad: float32 [256, 512, 128], P('ha', 'wa')
- zh_grad: float32 [64, 256, 128], P('wa', 'ha')
- wz_grad: float32 [512, 64, 128], P('wa', 'ha')
- w_in_grad: float32 [128, 256], replicated
- b_in_grad: float32 [256], replicated
- w_out_grad: float32 [256, 18], replicated
- b_out_grad: float32 [18], replicated
Inputs may be any that keep to these rules, and one draw needn't show every extreme that they name: `run_index`: each row holds 512 different run positions of one device block. `run_count`: the counts of block k and of block k + 8 * 4 / 2 (ha index differing by 4) sum to exactly 512.
All inputs are finite; a program needn't handle non-finite values.
Results may differ from a plain program's by a relative error of at most 0.00055.
The roundings to bfloat16 on the way count: a program that leaves them out, or rounds other values in their place, can miss the bound.
Values may be sent and summed in bfloat16 or wider, within the bound.
No kernel may reach another device: no remote copies, remote signals or barrier semaphores. Data moves between devices by JAX's collectives and lax.ppermute only.
A program may use at most 192 MiB of HBM per device.

v0:
```python
import math

import jax
import jax.numpy as jnp
from jax import lax
from jax.sharding import PartitionSpec as P

grad_scale = 0.25


def silu_slope(preact):
    sigmoid_val = jax.nn.sigmoid(preact)
    return sigmoid_val * (1.0 + preact * (1.0 - sigmoid_val))


def contract_rows(left, right):
    return lax.dot_general(
        left, right, (((0,), (0,)), ((), ())), preferred_element_type=jnp.float32
    )


def contract_cols(left, right):
    return lax.dot_general(
        left, right, (((1,), (1,)), ((), ())), preferred_element_type=jnp.float32
    )


def sample_grads(features, labels_flat, validity, w_in, b_in, w_out, b_out):
    preact = jnp.dot(features, w_in, preferred_element_type=jnp.float32) + b_in
    hidden = jax.nn.silu(preact).astype(jnp.bfloat16)
    logits = jnp.dot(hidden, w_out, preferred_element_type=jnp.float32) + b_out
    row_top = jnp.max(logits, axis=1, keepdims=True)
    scores_exp = jnp.exp(logits - row_top)
    probability = scores_exp / jnp.sum(scores_exp, axis=1, keepdims=True)
    classes = jnp.arange(logits.shape[1], dtype=jnp.int32)
    onehot = (labels_flat[:, None] == classes[None, :]).astype(jnp.float32)
    dlogits = ((probability - onehot) * (grad_scale * validity[:, None])).astype(jnp.bfloat16)
    grad_w_out = contract_rows(hidden, dlogits)
    grad_b_out = jnp.sum(dlogits.astype(jnp.float32), axis=0)
    dhidden = contract_cols(dlogits, w_out)
    dpreact = (dhidden * silu_slope(preact)).astype(jnp.bfloat16)
    grad_w_in = contract_rows(features, dpreact)
    grad_b_in = jnp.sum(dpreact.astype(jnp.float32), axis=0)
    dfeatures = contract_cols(dpreact, w_in)
    return (dfeatures, (grad_w_in, grad_b_in, grad_w_out, grad_b_out))


def run_features(hw_block, zh_rows, wz_block, run_ids):
    rows_blk, cols_blk, channels = hw_block.shape
    pair_cols = cols_blk // 2
    depth_z = wz_block.shape[1]
    run_row = run_ids // pair_cols
    run_pair = run_ids % pair_cols
    hw_part = hw_block.reshape(rows_blk * pair_cols, 2, channels)[run_ids].astype(jnp.float32)
    zh_part = zh_rows[run_row].astype(jnp.float32)
    wz_part = wz_block.reshape(pair_cols, 2, depth_z, channels)[run_pair].astype(jnp.float32)
    summed = hw_part[:, :, None, :] + zh_part[:, None, :, :] + wz_part
    return summed.astype(jnp.bfloat16)


def plane_grads(dfeatures, run_ids, rows_blk, cols_blk):
    slot_count, pair_count, depth_z, channels = dfeatures.shape
    pair_cols = cols_blk // 2
    run_row = run_ids // pair_cols
    run_pair = run_ids % pair_cols
    hw_local = jnp.zeros((rows_blk * pair_cols, 2, channels), jnp.float32)
    hw_local = (
        hw_local.at[run_ids].add(jnp.sum(dfeatures, axis=2)).reshape(rows_blk, cols_blk, channels)
    )
    zh_rows_grad = (
        jnp.zeros((rows_blk, depth_z, channels), jnp.float32)
        .at[run_row]
        .add(jnp.sum(dfeatures, axis=1))
    )
    zh_local = jnp.transpose(zh_rows_grad, (1, 0, 2))
    wz_local = jnp.zeros((pair_cols, 2, depth_z, channels), jnp.float32).at[run_pair].add(dfeatures)
    return (hw_local, zh_local, wz_local.reshape(cols_blk, depth_z, channels))


def decode(features, run_labels, validity, w_in, b_in, w_out, b_out):
    slot_count, pair_count, depth_z, channels = features.shape
    block_runs = math.gcd(32, slot_count)
    blocks = slot_count // block_runs
    block_rows = block_runs * pair_count * depth_z
    feat_blocks = features.reshape(blocks, block_rows, channels)
    label_blocks = run_labels.reshape(blocks, block_rows)
    valid_blocks = jnp.repeat(validity, pair_count * depth_z).reshape(blocks, block_rows)
    zero_init = (
        jnp.zeros(w_in.shape, jnp.float32),
        jnp.zeros(b_in.shape, jnp.float32),
        jnp.zeros(w_out.shape, jnp.float32),
        jnp.zeros(b_out.shape, jnp.float32),
    )

    def block_step(totals, pieces):
        dfeat, grads = sample_grads(pieces[0], pieces[1], pieces[2], w_in, b_in, w_out, b_out)
        return (jax.tree.map(jnp.add, totals, grads), dfeat)

    totals, dfeat_blocks = lax.scan(
        block_step, zero_init, (feat_blocks, label_blocks, valid_blocks)
    )
    return (dfeat_blocks.reshape(slot_count, pair_count, depth_z, channels), totals)


def local(hw_plane, zh_plane, wz_plane, w_in, b_in, w_out, b_out, run_index, run_count, labels):
    rows_blk, cols_blk, channels = hw_plane.shape
    capacity = run_index.shape[1]
    run_ids = run_index[0]
    run_total = run_count[0]
    run_labels = labels[0]
    zh_rows = jnp.transpose(zh_plane, (1, 0, 2))
    slot_ids = jnp.arange(capacity, dtype=jnp.int32)
    features = run_features(hw_plane, zh_rows, wz_plane, run_ids)
    validity = (slot_ids < run_total).astype(jnp.float32)
    dfeatures, weight_grads = decode(features, run_labels, validity, w_in, b_in, w_out, b_out)
    hw_local, zh_local, wz_local = plane_grads(dfeatures, run_ids, rows_blk, cols_blk)
    zh_grad = lax.psum_scatter(zh_local, "wa", scatter_dimension=0, tiled=True)
    wz_grad = lax.psum_scatter(wz_local, "ha", scatter_dimension=1, tiled=True)
    grad_w_in, grad_b_in, grad_w_out, grad_b_out = lax.psum(
        (weight_grads[0], weight_grads[1], weight_grads[2], weight_grads[3]), ("ha", "wa")
    )
    return (hw_local, zh_grad, wz_grad, grad_w_in, grad_b_in, grad_w_out, grad_b_out)


def solution(mesh):
    placed = (
        P("ha", "wa", None),
        P(None, "ha", None),
        P("wa", None, None),
        P(),
        P(),
        P(),
        P(),
        P(("ha", "wa"), None),
        P(("ha", "wa")),
        P(("ha", "wa"), None, None),
    )
    return jax.shard_map(
        local,
        mesh=mesh,
        in_specs=placed,
        out_specs=(
            P("ha", "wa", None),
            P("wa", "ha", None),
            P("wa", "ha", None),
            P(),
            P(),
            P(),
            P(),
        ),
        check_vma=False,
    )
```

profile of v0, /device:TPU:0, one launch (start us, length us, event | category | flops | bytes accessed | tf_op | source)
XLA Modules:
  0.0 559.9 jit_solution(13223976658982030564)
XLA Ops:
  10.3 13.5 %gather_fusion.1 = bf16[512,64,128]{2,1,0:T(8,128)(2,1)} fusion(bf16[32,64,128]{2,1,0:T(8,128)(2,1)S(1)} %bitcast.90, s32[1024]{0:T(1024)S(1)} %pad_clamp_fusion.1), kind=kCustom, calls=%fused_computation.1 | custom fusion | bytes 16779264 | tf_op jit(solution)/shard_map/gather | solution.py:55
  23.7 11.2 %convert_element_type.49 = f32[512,64,128]{2,1,0:T(8,128)} convert(bf16[512,64,128]{2,1,0:T(8,128)(2,1)} %gather_fusion.1) | non-fusion elementwise | flops 4194304 | bytes 25165824 | tf_op jit(solution)/shard_map/convert_element_type | solution.py:55
  35.0 2.6 gather_fusion
  40.4 13.9 %gather_fusion.2 = bf16[512,2,64,128]{3,2,1,0:T(8,128)(2,1)} fusion(bf16[64,2,64,128]{3,2,1,0:T(8,128)(2,1)S(1)} %bitcast.87, s32[1024]{0:T(1024)S(1)} %pad_clamp_fusion), kind=kCustom, calls=%fused_computation.2 | custom fusion | bytes 33556480 | tf_op jit(solution)/shard_map/gather | solution.py:56
  54.3 20.2 %add_convert_fusion = bf16[512,2,64,128]{3,2,1,0:T(8,128)(2,1)} fusion(bf16[512,2,64,128]{3,2,1,0:T(8,128)(2,1)} %gather_fusion.2, f32[512,64,128]{2,1,0:T(8,128)} %convert_element_type.49, f32[512,2,128]{2,1,0:T(2,128)S(1)} %convert_element_type.48), kind=kLoop, calls=%fused_computation.33 | loop fusion | flops 33554432 | bytes 50855936 | tf_op jit(solution)/shard_map/convert_element_type | solution.py:58
  74.5 197.7 %while.19 = (s32[]{:T(128)}, f32[128,256]{1,0:T(8,128)S(1)}, f32[256]{0:T(256)S(1)}, f32[256,18]{0,1:T(8,128)S(1)}, f32[18]{0:T(128)S(1)}, /*index=5*/f32[16,409...) while((s32[]{:T(128)}, f32[128,256]{1,0:T(8,128)S(1)}, ...), condition=%wide.region_5.6_spmd.clone, body=%wide.region_0.5_spmd.clone.sunk | while | flops 937407808 | bytes 35515956 | solution.py:99
  74.7 2.5 multiply_convert_fusion.4
  87.0 2.5 multiply_convert_fusion.4
  99.3 2.5 multiply_convert_fusion.4
  124.0 2.5 multiply_convert_fusion.4
  136.4 2.5 multiply_convert_fusion.4
  148.7 2.5 multiply_convert_fusion.4
  161.1 2.5 multiply_convert_fusion.4
  173.4 2.5 multiply_convert_fusion.4
  185.8 2.5 multiply_convert_fusion.4
  222.8 2.5 multiply_convert_fusion.4
  235.2 2.5 multiply_convert_fusion.4
  247.5 2.5 multiply_convert_fusion.4
  272.2 21.5 %fusion.11 = (f32[512,64,128]{2,1,0:T(8,128)}, f32[512,2,128]{2,1,0:T(2,128)S(1)}) fusion(f32[512,2,64,128]{3,2,1,0:T(8,128)} %bitcast.91), kind=kLoop, calls=%fused_computation.50 | loop fusion | flops 12451840 | bytes 50855936 | tf_op jit(solution)/shard_map/reduce_sum | solution.py:73
  293.8 51.9 %scatter_fusion.1 = f32[32,64,128]{2,1,0:T(8,128)S(1)} fusion(f32[32,64,128]{2,1,0:T(8,128)S(1)} %broadcast_in_dim.52, s32[512]{0:T(512)S(1)} %bitcast.105, f32[512,64,128]{2,1,0:T(8,128)} %get-tuple-element.132), kind=kCustom, calls=%fused_computation.4 | custom fusion | flops 4194304 | bytes 50333696 | tf_op jit(solution)/shard_map/scatter-add | solution.py:73
  347.3 2.6 broadcast_in_dim.53
  349.9 103.0 %scatter_fusion.2 = f32[64,2,64,128]{3,2,1,0:T(8,128)} fusion(f32[64,2,64,128]{3,2,1,0:T(8,128)} %broadcast_in_dim.53, s32[512]{0:T(512)S(1)} %bitcast.101, f32[512,2,64,128]{3,2,1,0:T(8,128)} %bitcast.92), kind=kCustom, calls=%fused_computation.5 | custom fusion | flops 8388608 | bytes 100665344 | tf_op jit(solution)/shard_map/scatter-add | solution.py:76
  454.5 52.1 %scatter_fusion = f32[2048,2,128]{2,1,0:T(2,128)} fusion(f32[2048,2,128]{2,1,0:T(2,128)} %broadcast_in_dim.29, s32[512]{0:T(512)S(1)} %bitcast.103, f32[512,2,128]{2,1,0:T(2,128)S(1)} %get-tuple-element.133), kind=kCustom, calls=%fused_computation.3 | custom fusion | flops 131072 | bytes 1574912 | tf_op jit(solution)/shard_map/scatter-add | solution.py:68
  506.5 42.6 %all-reduce = (f32[256]{0:T(256)}, f32[256,18]{0,1:T(8,128)}, f32[18]{0:T(128)}) all-reduce(f32[256]{0:T(256)S(1)} %get-tuple-element.80, f32[256,18]{0,1:T(8,128)S(1)} %get-tuple-element.81, f32[18]{0:T(128)S(1)} %get-tuple-element.82), channel_id=1, replica_groups=mesh['ha'=8,'wa'=4] {'ha','wa'}, use_global_device_ids=true, to_apply=%region_14.15 | all-reduce | flops 4882 | bytes 39056 | tf_op jit(solution)/shard_map/psum | solution.py:119
  (265 shorter events, 177.7 us)
Async XLA Ops:
  8.0 32.4 %copy-start = (bf16[128,64,128]{2,1,0:T(8,128)(2,1)S(1)}, bf16[128,64,128]{2,1,0:T(8,128)(2,1)}, u32[]{:S(2)}) copy-start(bf16[128,64,128]{2,1,0:T(8,128)(2,1)} %param.14) | copy-start | bytes 6291460
  8.0 541.2 %reduce-scatter.3.cloned.1.call-start = ((), (), s32[]{:S(2)}) async-start(), calls=%async_computation.2 | async-start | bytes 1310720 | tf_op jit(solution)/shard_map/reduce_scatter | solution.py:117
  8.9 26.0 %copy-start.9 = (s32[512,1]{0,1:T(1,128)}, s32[512,1]{0,1:T(1,128)S(1)}, u32[]{:S(2)}) copy-start(s32[512,1]{0,1:T(1,128)S(1)} %get-tuple-element.173) | copy-start | bytes 6148
  9.0 14.7 %copy-start.7 = (s32[512,1]{0,1:T(1,128)}, s32[512,1]{0,1:T(1,128)S(1)}, u32[]{:S(2)}) copy-start(s32[512,1]{0,1:T(1,128)S(1)} %compare_select_fusion) | copy-start | bytes 6148
  54.3 20.2 %copy-start.5 = (bf16[128,256]{1,0:T(8,128)(2,1)S(1)}, bf16[128,256]{1,0:T(8,128)(2,1)}, u32[]{:S(2)}) copy-start(bf16[128,256]{1,0:T(8,128)(2,1)} %param.15) | copy-start | bytes 196612
  54.3 20.2 %copy-start.6 = (bf16[256,18]{0,1:T(8,128)(2,1)S(1)}, bf16[256,18]{0,1:T(8,128)(2,1)}, u32[]{:S(2)}) copy-start(bf16[256,18]{0,1:T(8,128)(2,1)} %param.17) | copy-start | bytes 27652
  54.3 20.2 %copy-start.11 = (f32[18]{0:T(128)S(1)}, f32[18]{0:T(128)}, u32[]{:S(2)}) copy-start(f32[18]{0:T(128)} %param.18) | copy-start | bytes 220
  54.3 20.2 %copy-start.12 = (f32[256]{0:T(256)S(1)}, f32[256]{0:T(256)}, u32[]{:S(2)}) copy-start(f32[256]{0:T(256)} %param.16) | copy-start | bytes 3076
  77.1 2.1 copy-start.3
  89.5 2.1 copy-start.3
  101.8 2.1 copy-start.3
  114.2 2.1 copy-start.3
  126.5 2.1 copy-start.3
  138.9 2.1 copy-start.3
  151.2 2.1 copy-start.3
  163.6 2.1 copy-start.3
  175.9 2.1 copy-start.3
  188.3 2.1 copy-start.3
  200.6 2.1 copy-start.3
  272.2 21.5 %copy-start.4 = (f32[128,256]{1,0:T(8,128)}, f32[128,256]{1,0:T(8,128)S(1)}, u32[]{:S(2)}) copy-start(f32[128,256]{1,0:T(8,128)S(1)} %get-tuple-element.79) | copy-start | bytes 393220
  345.7 4.2 copy-start.8
  346.7 204.2 %all-reduce.3.cloned.1.call-start = ((), (), s32[]{:S(2)}) async-start(), calls=%async_computation.4 | async-start | bytes 262144 | tf_op jit(solution)/shard_map/psum | solution.py:119
  347.3 203.6 %reduce-scatter.5.cloned.1.call-start = ((), (), s32[]{:S(2)}) async-start(), calls=%async_computation.3 | async-start | bytes 4718592 | tf_op jit(solution)/shard_map/reduce_scatter | solution.py:118
  452.9 99.6 %copy-start.1 = (bf16[128,64,128]{2,1,0:T(8,128)(2,1)S(1)}, bf16[128,64,128]{2,1,0:T(8,128)(2,1)}, u32[]{:S(2)}) copy-start(bf16[128,64,128]{2,1,0:T(8,128)(2,1)} %param.14) | copy-start | bytes 6291460
  (7 other events, 13.3 us)
Sparse Core Ops, SparseCore 0:
  346.8 29.9 reduce-scatter.2
  453.0 54.0 reduce-scatter.4
Sparse Core Ops, SparseCore 1:
  353.3 129.9 all-reduce.2
where the time goes:
time: 566 us; the launch traced here: 560 us
  other arithmetic  284 us (50%)
  matrix products  173 us (31%)
  blocking collectives  42.6 us (8%)
  local copies, waits for them, and re-layouts  42.2 us (7%)
  between operations  16.3 us (3%)
    scatter-add x1, other arithmetic, plane_grads(): jnp.zeros((pair_cols, 2, depth_z, channels), jnp.float32).at[run_pair]  103 us
    dot_general x32, matrix products, contract_cols(): lax.dot_general(left, right, (((1,), (1,)), ((), ())), preferred_element_...  61.7 us
    dot_general x32, matrix products, contract_rows(): lax.dot_general(left, right, (((0,), (0,)), ((), ())), preferred_element_...  61.1 us
    scatter-add x1, other arithmetic, plane_grads(): hw_local.at[run_ids].add(jnp.sum(dfeatures, axis=2))  52.1 us
    scatter-add x1, other arithmetic, plane_grads(): zh_rows_grad = jnp.zeros((rows_blk, depth_z, channels), jnp.float32).at[r...  51.9 us
    psum x1, blocking collectives, local(): lax.psum((weight_grads[0], weight_grads[1], weight_grads[2], weight_grads...  42.6 us
    dot_general x16, matrix products, sample_grads(): preact = jnp.dot(features, w_in, preferred_element_type=jnp.float32) + b_in  39.5 us
    reduce_sum x1, other arithmetic, plane_grads(): jnp.sum(dfeatures, axis=1)  21.5 us
  transfers between devices with their start and end apart: 3, of which 0 were waited for; matrix products, arithmetic and copies ran while one was open for 29% of the time, Pallas kernels for 0%

commit v1 on v0

v1 whole, which is shorter than its diff:
```python
import functools

import jax
import jax.numpy as jnp
from jax import lax
from jax.experimental import pallas as pl
from jax.experimental.pallas import tpu as pltpu
from jax.sharding import PartitionSpec as P

grad_scale = 0.25
CLS_ROWS = 24
CLS_PAD = 32
CHUNKS = ((0, 3), (1, 2))
ZC = 16
RUNS = 32
GROUP = 4
ROWS = RUNS * 2 * ZC
STRIP = 32
LEVEL_TOPS = tuple(2.0 ** e for e in (4, -7, -18, -29, -40))
LEVEL_BITS = (11, 22, 33, 44, 55)
CODE_ROWS = 16


def ppermute_xor(value, axis, size, mask):
    return lax.ppermute(value, axis, [(i, i ^ mask) for i in range(size)])


def fill_planes(side, refs, bases, zh_full, lab_pad, start, *, half, rows_blk, depth_z, slots):
    n_zh = rows_blk * ZC
    n_lab = slots // GROUP
    lane = lax.rem(lax.broadcasted_iota(jnp.int32, (n_lab, 128), 1), depth_z)
    z0 = side * half
    labs = [lab_pad[pl.ds(start + par, n_lab, stride=GROUP), :] for par in range(GROUP)]
    for chunk, ref, base in zip(CHUNKS, refs, bases):
        if ref is None:
            continue
        for h in range(rows_blk):
            parts = [zh_full[pl.ds((z0 + 8 * o) * rows_blk + h, 8, stride=rows_blk), :] for o in chunk]
            ref[base + h * ZC:base + (h + 1) * ZC, :] = jnp.concatenate(parts, axis=0).astype(jnp.bfloat16)
        merged = jnp.zeros((n_lab, 128), jnp.float32)
        for par in range(GROUP):
            for n, o in enumerate(chunk):
                to = par * ZC + 8 * n
                rolled = pltpu.roll(labs[par], jnp.bitwise_and(256 + to - (z0 + 8 * o), 127), 1)
                merged = jnp.where((lane >= to) & (lane < to + 8), rolled, merged)
        ref[base + n_zh:base + n_zh + n_lab, :] = merged.astype(jnp.bfloat16)


def load_inputs(hw_ref, zh_ref, lab_ref, ids_ref, hw_raw, zh_raw, lab_raw, ids_raw, rid_ref, sems,
                hw_full, zh_full, lab_pad, slots):
    copies = [pltpu.make_async_copy(a, b, sems.at[n]) for n, (a, b) in enumerate(
        ((hw_ref, hw_raw), (ids_ref, rid_ref), (ids_ref, ids_raw), (zh_ref, zh_raw), (lab_ref, lab_raw)))]
    for copy in copies:
        copy.start()
    for copy in copies:
        copy.wait()
    hw_full[...] = hw_raw[...].astype(jnp.float32)
    zh_full[...] = zh_raw[...].astype(jnp.float32)
    lab_pad[0:slots, :] = jnp.zeros((slots, lab_raw.shape[1]), jnp.float32)
    lab_pad[slots:, :] = lab_raw[...].astype(jnp.float32)
    ids = [ids_raw[:, k * 128:(k + 1) * 128] for k in range(slots // 128)]
    return jnp.concatenate(ids + ids, axis=0)


def gather_rows(rid_ref, hw_full, hw_rows, slots, shift):
    def gather_step(i, carry):
        for j in range(8):
            s = i * 8 + j
            r = rid_ref[0, jnp.maximum(s - shift, 0)]
            for p in range(2):
                hw_rows[pl.ds(2 * s + p, 1), :] = hw_full[pl.ds(2 * r + p, 1), :]
        return carry

    lax.fori_loop(0, slots // 8, gather_step, 0)


def put_ids(ref, base, ids, shift_bits, keep):
    padded = jnp.concatenate([ids, jnp.zeros_like(ids)], axis=0)
    high = lax.shift_right_logical(padded, shift_bits)
    low = jnp.bitwise_and(padded, keep)
    row = lax.broadcasted_iota(jnp.int32, padded.shape, 0)
    both = jnp.where(row < 4, high, pltpu.roll(low, 4, 0))
    ref[base:base + 16, :] = both.astype(jnp.float32).astype(jnp.bfloat16)


def pack_send_kernel(meta_ref, hw_ref, zh_ref, lab_ref, ids_ref, send_ref,
                     hw_raw, zh_raw, lab_raw, ids_raw, rid_ref, sems,
                     hw_full, hw_rows, zh_full, lab_pad, *, depth_z, rows_blk, slots, pair_cols):
    half = depth_z // 2
    n_hw = 2 * slots
    count = meta_ref[1]
    ids = load_inputs(hw_ref, zh_ref, lab_ref, ids_ref, hw_raw, zh_raw, lab_raw, ids_raw, rid_ref, sems,
                      hw_full, zh_full, lab_pad, slots)
    gather_rows(rid_ref, hw_full, hw_rows, slots, slots - count)
    send_ref[0:n_hw, :] = hw_rows[...].astype(jnp.bfloat16)
    down = slots - count
    lanes = jnp.bitwise_and(down, 127)
    rows = lax.shift_right_logical(down, 7)
    turned = pltpu.roll(ids, lanes, 1)
    here = pltpu.roll(turned, rows, 0)
    before = pltpu.roll(turned, jnp.bitwise_and(rows + 1, 7), 0)
    lane = lax.broadcasted_iota(jnp.int32, ids.shape, 1)
    put_ids(send_ref, n_hw, jnp.where(lane < lanes, before, here), pair_cols.bit_length() - 1, pair_cols - 1)
    fill_planes(1 - meta_ref[0], (send_ref, None), (n_hw + 16, 0), zh_full, lab_pad, count,
                half=half, rows_blk=rows_blk, depth_z=depth_z, slots=slots)


def pack_own_kernel(meta_ref, hw_ref, zh_ref, lab_ref, ids_ref, wz_ref,
                    own0_ref, own1_ref, send1_ref, wz0_ref, wz1_ref,
                    hw_raw, zh_raw, lab_raw, ids_raw, rid_ref, sems,
                    hw_full, hw_rows, zh_full, lab_pad, wz_raw, wz_sem,
                    *, depth_z, rows_blk, slots, pair_cols):
    half = depth_z // 2
    n_hw = 2 * slots
    z0 = pl.multiple_of(meta_ref[0] * half, half)
    wz_copy = pltpu.make_async_copy(wz_ref.at[:, pl.ds(z0, half), :], wz_raw, wz_sem)
    wz_copy.start()
    ids = load_inputs(hw_ref, zh_ref, lab_ref, ids_ref, hw_raw, zh_raw, lab_raw, ids_raw, rid_ref, sems,
                      hw_full, zh_full, lab_pad, slots)
    gather_rows(rid_ref, hw_full, hw_rows, slots, 0)
    own0_ref[0:n_hw, :] = hw_rows[...].astype(jnp.bfloat16)
    put_ids(own0_ref, n_hw, ids, pair_cols.bit_length() - 1, pair_cols - 1)
    fill_planes(meta_ref[0], (own0_ref, own1_ref), (n_hw + 16, 0), zh_full, lab_pad, slots,
                half=half, rows_blk=rows_blk, depth_z=depth_z, slots=slots)
    fill_planes(1 - meta_ref[0], (None, send1_ref), (0, 0), zh_full, lab_pad, meta_ref[1],
                half=half, rows_blk=rows_blk, depth_z=depth_z, slots=slots)
    wz_copy.wait()

    def widen(w, carry):
        rows = wz_raw[w].astype(jnp.float32)
        for chunk, ref in zip(CHUNKS, (wz0_ref, wz1_ref)):
            for n, o in enumerate(chunk):
                ref[w, 8 * n:8 * n + 8, :] = rows[8 * o:8 * o + 8]
        return carry

    lax.fori_loop(0, 2 * pair_cols, widen, 0, unroll=8)


def run_slices(dfeat_ref, j, base=0):
    g, par = j // GROUP, j % GROUP
    at = [base + g * 128 + p * 64 + par * ZC for p in range(2)]
    return [dfeat_ref[pl.ds(at[p], ZC), :] for p in range(2)]


def add_zh(d, row, zh_accs):
    both = d[0] + d[1]
    now = [acc[row] for acc in zh_accs]
    for n, acc in enumerate(zh_accs):
        acc[row] = now[n] + both[8 * n:8 * n + 8]


def add_wz(d, col, wz_accs):
    now = [[acc[col + p] for p in range(2)] for acc in wz_accs]
    for n, acc in enumerate(wz_accs):
        for p in range(2):
            acc[col + p] = now[n][p] + d[p][8 * n:8 * n + 8]


def pick_level(top):
    level = jnp.zeros(top.shape, jnp.float32)
    for n, bound in enumerate(LEVEL_TOPS):
        level = jnp.where(top < bound, n + 1.0, level)
    return level


def level_scale(level, sign):
    scale = jnp.ones(level.shape, jnp.float32)
    for n in range(len(LEVEL_TOPS)):
        scale = jnp.where(level == n + 1.0, 2.0 ** (sign * LEVEL_BITS[n]), scale)
    return scale


def encode(value):
    level = pick_level(jnp.max(jnp.abs(value), axis=1, keepdims=True))
    code = jnp.broadcast_to(level, (value.shape[0], CODE_ROWS, value.shape[2]))
    return jnp.concatenate([value * level_scale(level, 1), code], axis=1).astype(jnp.float16)


def decode_half(value):
    value = value.astype(jnp.float32)
    n = value.shape[1] - CODE_ROWS
    return value[:, :n] * level_scale(value[:, n:n + 1, :], -1)


def read_runs(ids_ref, first, n):
    row = lax.shift_right_logical(first, 7)
    at = jnp.bitwise_and(first, 127)
    return [(ids_ref[row, at + j], ids_ref[row + 4, at + j]) for j in range(n)]


def decode_kernel(*refs, chunk, first, rows_blk, slots, pair_cols):
    n_hw = 2 * slots
    n_zh = rows_blk * ZC
    n_lab = slots // GROUP
    meta_ref, hw_own, hw_recv = refs[:3]
    refs = refs[3:]
    if first:
        z_own, z_recv, z_base = hw_own, hw_recv, n_hw + 16
    else:
        z_own, z_recv, z_base = refs[0], refs[1], 0
        hw_prev, wgt_prev = refs[2:4]
        refs = refs[4:]
    wz_full, w_in_ref, w_in_t_ref, b_in_ref, w_out_t_ref, w_out_half_ref, b_out_ref, sel_ref = refs[:8]
    refs = refs[8:]
    if first:
        wz_out0, wz_out1, zh_out0, zh_out1, hw_out, wgt_out = refs[:6]
        refs = refs[6:]
    else:
        wz_out0, core_out, zh_out0, zh_out1, hw_out, wgt_keep = refs[:6]
        refs = refs[6:]
    (hw_full, zh_full, lab_full, hw_acc, w_in_acc, w_out_acc, b_out_acc, ids_ref, ids_sem) = refs[:9]
    bufs = (refs[9:14], refs[14:19])
    outs = (refs[19:22], refs[22:25])
    dfeat_ref = refs[25]
    wz_accs, zh_accs, ids_vec, wgt_all = refs[26:28], refs[28:30], refs[30], refs[31]
    count = meta_ref[1]
    rel_own = meta_ref[7]

    spot_row = lax.broadcasted_iota(jnp.int32, (8, 128), 0)
    spot = jnp.bitwise_and(spot_row, 3) * 128 + lax.broadcasted_iota(jnp.int32, (8, 128), 1)
    own_ids = hw_own[n_hw:n_hw + 16, :].astype(jnp.float32).astype(jnp.int32)
    recv_ids = hw_recv[n_hw:n_hw + 16, :].astype(jnp.float32).astype(jnp.int32)
    is_own = spot < count
    ids = jnp.where(is_own, own_ids[0:8], recv_ids[0:8])
    rel = jnp.where(is_own, rel_own, 1 - rel_own)
    ids_vec[...] = jnp.where(spot_row < 4, ids + rel * rows_blk, 2 * ids)
    copy = pltpu.make_async_copy(ids_vec, ids_ref, ids_sem)
    copy.start()
    row = lax.broadcasted_iota(jnp.int32, (n_hw, 128), 0)
    hw_full[...] = jnp.where(row < 2 * count, hw_own[0:n_hw, :].astype(jnp.float32),
                             hw_recv[0:n_hw, :].astype(jnp.float32))
    for k, ref in ((0, z_own), (1, z_recv)):
        base = jnp.bitwise_xor(rel_own, k) * rows_blk
        for h in range(rows_blk):
            zh_full[base + h] = ref[z_base + h * ZC:z_base + (h + 1) * ZC, :].astype(jnp.float32)
    lab_row = lax.broadcasted_iota(jnp.int32, (n_lab, 128), 0)
    lab_lane = lax.broadcasted_iota(jnp.int32, (n_lab, 128), 1)
    place = GROUP * lab_row + lax.rem(lab_lane // ZC, GROUP)
    first_lab = z_base + n_zh
    lab_full[...] = jnp.where(place < count, z_own[first_lab:first_lab + n_lab, :].astype(jnp.float32),
                              z_recv[first_lab:first_lab + n_lab, :].astype(jnp.float32))
    for acc in wz_accs + zh_accs:
        acc[...] = jnp.zeros_like(acc)
    w_in_acc[...] = jnp.zeros_like(w_in_acc)
    w_out_acc[...] = jnp.zeros_like(w_out_acc)
    b_out_acc[...] = jnp.zeros_like(b_out_acc)
    copy.wait()

    groups = RUNS // GROUP
    n_ch = w_in_ref.shape[0]
    for left_ref, dhid_ref, dpre_ref in outs:
        left_ref[n_ch:, :] = sel_ref[...]
    class_ids = lax.broadcasted_iota(jnp.int32, (CLS_ROWS, 128), 0).astype(jnp.float32)
    nt = (((1,), (1,)), ((), ()))

    def front(b, buf):
        feat_ref, hid_ref, slope_ref, logit_ref, pre_ref = buf
        pieces = []
        runs = read_runs(ids_ref, RUNS * b, RUNS)
        for g in range(groups):
            for p in range(2):
                for par in range(GROUP):
                    row, col = runs[GROUP * g + par]
                    at = pl.multiple_of(2 * RUNS * b, 2 * RUNS) + 2 * (GROUP * g + par) + p
                    total = hw_full[pl.ds(at, 1), :] + zh_full[row] + wz_full[col + p]
                    pieces.append(total.astype(jnp.bfloat16))
        feat = jnp.concatenate(pieces, axis=0)
        feat_ref[...] = feat
        pre_ref[...] = jnp.dot(feat, w_in_ref[...], preferred_element_type=jnp.float32)
        for r in range(0, ROWS, STRIP):
            pre = pre_ref[r:r + STRIP, :] + b_in_ref[...]
            t = jnp.tanh(pre)
            a = 1.0 + t
            u = pre * a
            hid_ref[r:r + STRIP, :] = u.astype(jnp.bfloat16)
            slope_ref[r:r + STRIP, :] = a + u * (1.0 - t)
        logits = lax.dot_general(w_out_t_ref[...], hid_ref[...], nt, preferred_element_type=jnp.float32)
        logit_ref[...] = logits[0:CLS_ROWS, :]

    def middle(b, buf, out):
        feat_ref, hid_ref, slope_ref, logit_ref, pre_ref = buf
        left_ref, dhid_ref, dpre_ref = out
        left_ref[0:n_ch, :] = jnp.transpose(feat_ref[...], (1, 0))
        dl_tiles = []
        b_part = None
        for g in range(groups):
            tile = logit_ref[:, g * 128:(g + 1) * 128] + b_out_ref[...]
            top = jnp.max(tile, axis=0, keepdims=True)
            e = jnp.exp(tile - top)
            inv = 1.0 / jnp.sum(e, axis=0, keepdims=True)
            lab_here = lab_full[pl.ds(groups * b + g, 1), :]
            onehot = jnp.where(class_ids == lab_here, 1.0, 0.0)
            dl = ((e * inv - onehot) * grad_scale).astype(jnp.bfloat16).astype(jnp.float32)
            b_part = dl if b_part is None else b_part + dl
            dl_tiles.append(dl)
        b_out_acc[...] += b_part
        dl_all = jnp.concatenate(dl_tiles, axis=1)
        dl_all = jnp.concatenate([dl_all, jnp.zeros((CLS_PAD - CLS_ROWS, ROWS), jnp.float32)], axis=0)
        dl_t = jnp.transpose(dl_all, (1, 0)).astype(jnp.bfloat16)
        w_out_acc[...] += jnp.dot(dl_all.astype(jnp.bfloat16), hid_ref[...], preferred_element_type=jnp.float32)
        dhid_ref[...] = jnp.dot(dl_t, w_out_half_ref[...], preferred_element_type=jnp.float32)
        for r in range(0, ROWS, STRIP):
            dpre_ref[r:r + STRIP, :] = (dhid_ref[r:r + STRIP, :] * slope_ref[r:r + STRIP, :]).astype(jnp.bfloat16)

    def back(b, out):
        left_ref, dhid_ref, dpre_ref = out
        dpre = dpre_ref[...]
        sums = jnp.dot(left_ref[...], dpre, preferred_element_type=jnp.float32)
        w_in_acc[...] += sums[0:n_ch]
        hw_acc[pl.ds(pl.multiple_of(2 * RUNS * b, 2 * RUNS), 2 * RUNS), :] = sums[n_ch:]
        dfeat_ref[...] = jnp.dot(dpre, w_in_t_ref[...], preferred_element_type=jnp.float32)
        runs = read_runs(ids_ref, RUNS * b, RUNS)
        for j in range(RUNS):
            d = run_slices(dfeat_ref, j)
            add_zh(d, runs[j][0], zh_accs)
            add_wz(d, runs[j][1], wz_accs)

    n_batch = slots // RUNS
    front(0, bufs[0])
    front(1, bufs[1])
    middle(0, bufs[0], outs[0])

    def step(k, carry):
        b = 2 * k
        front(b + 2, bufs[0])
        middle(b + 1, bufs[1], outs[1])
        back(b, outs[0])
        front(b + 3, bufs[1])
        middle(b + 2, bufs[0], outs[0])
        back(b + 1, outs[1])
        return carry

    lax.fori_loop(0, n_batch // 2 - 1, step, 0)
    middle(n_batch - 1, bufs[1], outs[1])
    back(n_batch - 2, outs[0])
    back(n_batch - 1, outs[1])
    tail = hw_acc[...]
    total = None
    for n in range(3):
        part = tail.astype(jnp.bfloat16)
        tail = tail - part.astype(jnp.float32)
        term = jnp.dot(part, w_in_t_ref[...], preferred_element_type=jnp.float32)
        total = term if total is None else total + term
    width = w_in_acc.shape[1]
    b_in_sum = jnp.sum(hw_acc[...], axis=0, keepdims=True)
    b_pad = jnp.concatenate([b_out_acc[...], jnp.zeros((128 - CLS_ROWS, 128), jnp.float32)], axis=0)
    b_out_sum = jnp.sum(jnp.transpose(b_pad, (1, 0)), axis=0, keepdims=True)
    b_out_sum = jnp.concatenate([b_out_sum, jnp.zeros((1, width - 128), jnp.float32)], axis=1)
    biases = jnp.concatenate([b_in_sum, b_out_sum, jnp.zeros((6, width), jnp.float32)], axis=0)
    weights = jnp.concatenate([w_in_acc[...], biases, w_out_acc[0:CLS_ROWS, :]], axis=0)
    put_zh(meta_ref, chunk, zh_accs, zh_out0, zh_out1)
    if first:
        hw_out[...] = total
        wgt_out[...] = weights
        put_wz(meta_ref, chunk, wz_accs, wz_out0, wz_out1)
        return
    hw_out[...] = total + hw_prev[...]
    wgt_all[...] = weights + wgt_prev[...]
    put_wz(meta_ref, chunk, wz_accs, wz_out0, core_out.at[0:2 * pair_cols])
    mid = wgt_all.shape[0] // 2
    mine = meta_ref[8] * mid
    wgt_keep[...] = split_lanes(wgt_all[pl.ds(pl.multiple_of(mine, 8), mid), :])
    core_out[2 * pair_cols:] = split_lanes(wgt_all[pl.ds(pl.multiple_of(mid - mine, 8), mid), :])


def split_lanes(value):
    return jnp.concatenate([value[:, :128], value[:, 128:]], axis=0).reshape(value.shape[0] // 4, 8, 128)


def put_zh(meta_ref, chunk, zh_accs, zh_out0, zh_out1):
    same = meta_ref[6] == chunk[0] // 2
    zh_out0[...] = jnp.where(same, zh_accs[0][...], zh_accs[1][...])
    zh_out1[...] = jnp.where(same, zh_accs[1][...], zh_accs[0][...])


def put_wz(meta_ref, chunk, wz_accs, wz_out0, wz_out1):
    same = meta_ref[2 + chunk[0]] == 0
    wz_out0[...] = jnp.where(same, wz_accs[0][...], wz_accs[1][...])
    wz_out1[...] = jnp.where(same, wz_accs[1][...], wz_accs[0][...])


def place_kernel(meta_ref, rid_ref, mine_ref, recv_ref, out_ref, *, slots):
    out_ref[...] = jnp.zeros_like(out_ref)
    count = meta_ref[1]

    def place(s, carry):
        r = rid_ref[0, s]
        for p in range(2):
            out_ref[pl.ds(2 * r + p, 1), :] = (mine_ref[pl.ds(2 * s + p, 1), :]
                                               + recv_ref[pl.ds(2 * (slots - count + s) + p, 1), :])
        return carry

    def place_eight(i, carry):
        for j in range(8):
            place(8 * i + j, carry)
        return carry

    lax.fori_loop(0, count // 8, place_eight, 0)
    lax.fori_loop(count // 8 * 8, count, place, 0)


def finish_kernel(meta_ref, zh0_ref, zh1_ref, w_mine_ref, w_other_ref,
                  zh_out, w_in_out, b_in_out, w_out_out, b_out_out, w_all, *, rows_blk):
    mid = w_all.shape[0] // 2
    mine = meta_ref[8] * mid
    for start, ref in ((mine, w_mine_ref), (mid - mine, w_other_ref)):
        flat = ref[...].reshape(2 * mid, 128)
        w_all[pl.ds(pl.multiple_of(start, 8), mid), :] = jnp.concatenate([flat[:mid], flat[mid:]], axis=1)
    n_ch = w_in_out.shape[0]
    w_in_out[...] = w_all[0:n_ch, :]
    b_in_out[...] = w_all[n_ch:n_ch + 1, :]
    b_out_out[...] = w_all[n_ch + 1:n_ch + 2, 0:b_out_out.shape[1]]
    w_out_out[...] = w_all[n_ch + 8:n_ch + 8 + w_out_out.shape[0], :]
    swapped = meta_ref[6]
    for n, ref in ((0, zh0_ref), (1, zh1_ref)):
        base = jnp.bitwise_xor(swapped, n) * 8
        for z in range(8):
            zh_out[base + z] = ref[pl.ds(z, rows_blk, stride=8), :]


def local(n_ha, n_wa, hw_plane, zh_plane, wz_plane, w_in, b_in, w_out, b_out,
          run_index, run_count, labels):
    rows_blk, cols_blk, channels = hw_plane.shape
    depth_z = zh_plane.shape[0]
    hidden = w_in.shape[1]
    classes = w_out.shape[1]
    slots = run_index.shape[1]
    half = depth_z // 2
    pair_cols = cols_blk // 2
    n_q = n_ha // 2
    n_zl = n_wa // 2
    n_hw = 2 * slots
    n_zh = rows_blk * ZC
    n_lab = slots // GROUP
    smem = pl.BlockSpec(memory_space=pltpu.SMEM)
    vmem = pl.BlockSpec(memory_space=pltpu.VMEM)
    hbm = pl.BlockSpec(memory_space=pltpu.HBM)
    f32 = jnp.float32
    bf16 = jnp.bfloat16

    ha = lax.axis_index("ha")
    wa = lax.axis_index("wa")
    y = ha // n_q
    my_q = ha % n_q
    b1 = wa // n_zl
    my_zl = wa % n_zl
    count = run_count[0]
    direct = n_q == 4 and n_zl == 2
    if direct:
        wz_pos = [(o ^ my_q) % 2 for o in range(4)]
        rest = [my_zl, y ^ b1, ha % 2, my_q]
    else:
        wz_pos = [jnp.int32(o // 2) for o in range(4)]
        rest = [jnp.int32(0), y, ha % 2, my_q]
    meta = jnp.stack([y, count] + wz_pos + rest).astype(jnp.int32)
    swap_y = [(i, (i + n_q) % n_ha) for i in range(n_ha)]

    pack_rows = (n_hw + 16 + n_zh + n_lab, n_zh + n_lab)
    planes = (hw_plane.reshape(rows_blk * cols_blk, channels),
              zh_plane.reshape(depth_z * rows_blk, channels), labels[0], run_index)
    raw = [pltpu.VMEM((rows_blk * cols_blk, channels), bf16), pltpu.VMEM((depth_z * rows_blk, channels), bf16),
           pltpu.VMEM((slots, 2 * depth_z), jnp.int32), pltpu.VMEM((1, slots), jnp.int32),
           pltpu.SMEM((1, slots), jnp.int32), pltpu.SemaphoreType.DMA((5,)),
           pltpu.VMEM((rows_blk * cols_blk, channels), f32), pltpu.VMEM((n_hw, channels), f32),
           pltpu.VMEM((depth_z * rows_blk, channels), f32), pltpu.VMEM((2 * slots, 2 * depth_z), f32)]

    def call(kernel, name, operands, specs, outs, scratch, flops, limit=16):
        return pl.pallas_call(
            kernel,
            out_shape=[jax.ShapeDtypeStruct(shape, kind) for shape, kind in outs],
            in_specs=specs,
            out_specs=[vmem] * len(outs),
            scratch_shapes=scratch,
            compiler_params=pltpu.CompilerParams(vmem_limit_bytes=limit * 2**20),
            cost_estimate=pl.CostEstimate(flops=flops, bytes_accessed=2**20, transcendentals=0),
            name=name,
        )(*operands)

    sizes = dict(depth_z=depth_z, rows_blk=rows_blk, slots=slots, pair_cols=pair_cols)
    send0, = call(functools.partial(pack_send_kernel, **sizes), "pack_send", (meta,) + planes,
                  [smem] + [hbm] * 4, [((pack_rows[0], channels), bf16)], raw, 3 * 10**9, 60)
    recv0 = lax.ppermute(send0, "ha", swap_y)
    later = lax.optimization_barrier((send0, w_in, b_in, w_out, b_out) + planes)
    w_in, b_in, w_out, b_out = later[1:5]
    own0, own1, send1, wzf0, wzf1 = call(
        functools.partial(pack_own_kernel, **sizes), "pack_own", (meta,) + later[5:] + (wz_plane,),
        [smem] + [hbm] * 5,
        [((pack_rows[0], channels), bf16), ((pack_rows[1], channels), bf16), ((pack_rows[1], channels), bf16),
         ((cols_blk, ZC, channels), f32), ((cols_blk, ZC, channels), f32)],
        raw + [pltpu.VMEM((cols_blk, half, channels), bf16), pltpu.SemaphoreType.DMA], 3 * 10**9)
    send1, recv0 = lax.optimization_barrier((send1, recv0))
    recv1 = lax.ppermute(send1, "ha", swap_y)

    w_in_half = (w_in.astype(f32) * 0.5).astype(bf16)
    w_out_half = jnp.pad((w_out.astype(f32) * 0.5).astype(bf16).T, ((0, CLS_PAD - classes), (0, 0)))
    w_out_t = jnp.pad(w_out.T, ((0, CLS_PAD - classes), (0, 0)))
    b_out_rows = jnp.broadcast_to(
        jnp.pad(b_out, (0, CLS_ROWS - classes), constant_values=-1e30)[:, None], (CLS_ROWS, 128))
    spot = jnp.arange(ROWS)
    run_of = (spot // 128) * GROUP + (spot % 64) // ZC
    select = (jnp.arange(2 * RUNS)[:, None] == (2 * run_of + (spot // 64) % 2)[None, :]).astype(bf16)
    w_in_t = w_in.T
    shared = (w_in_half, w_in_t, (b_in * 0.5).reshape(1, hidden), w_out_t, w_out_half, b_out_rows, select)
    wgt_rows = channels + 8 + CLS_ROWS
    mid = wgt_rows // 2
    buf = [pltpu.VMEM((ROWS, channels), bf16), pltpu.VMEM((ROWS, hidden), bf16),
           pltpu.VMEM((ROWS, hidden), f32), pltpu.VMEM((CLS_ROWS, ROWS), f32), pltpu.VMEM((ROWS, hidden), f32)]
    out_buf = [pltpu.VMEM((channels + 2 * RUNS, ROWS), bf16), pltpu.VMEM((ROWS, hidden), f32),
               pltpu.VMEM((ROWS, hidden), bf16)]
    work = [pltpu.VMEM((n_hw, channels), f32), pltpu.VMEM((2 * rows_blk, ZC, channels), f32),
            pltpu.VMEM((n_lab, 128), f32), pltpu.VMEM((n_hw, hidden), f32),
            pltpu.VMEM((channels, hidden), f32), pltpu.VMEM((CLS_PAD, hidden), f32),
            pltpu.VMEM((CLS_ROWS, 128), f32), pltpu.SMEM((8, 128), jnp.int32), pltpu.SemaphoreType.DMA]
    work += buf + buf + out_buf + out_buf + [pltpu.VMEM((ROWS, channels), f32)]
    work += [pltpu.VMEM((cols_blk, 8, channels), f32)] * 2 + [pltpu.VMEM((2 * rows_blk, 8, channels), f32)] * 2
    work += [pltpu.VMEM((8, 128), jnp.int32), pltpu.VMEM((wgt_rows, hidden), f32)]
    sums = [((cols_blk, 8, channels), f32)] * 2 + [((2 * rows_blk, 8, channels), f32)] * 2
    def decode(n, sources, outs):
        return call(
            functools.partial(decode_kernel, chunk=CHUNKS[n], first=n == 0, rows_blk=rows_blk,
                              slots=slots, pair_cols=pair_cols), "decode%d" % n,
            (meta,) + sources + (wzf0, wzf1)[n:n + 1] + shared,
            [smem] + [vmem] * (len(sources) + 8), outs, work, 22 * 10**9, 28)

    wz0a, wz0b, zh0a, zh0b, hw0, wgt0 = decode(
        0, (own0, recv0), sums + [((n_hw, channels), f32), ((wgt_rows, hidden), f32)])
    recv1, wz0a, wz0b, zh0a, zh0b = lax.optimization_barrier((recv1, wz0a, wz0b, zh0a, zh0b))
    wz1a, core_send, zh1a, zh1b, hw1, w_keep = decode(
        1, (own0, recv0, own1, recv1, hw0, wgt0),
        [sums[0], ((cols_blk + mid // 4, 8, channels), f32), sums[2], sums[3],
         ((n_hw, channels), f32), ((mid // 4, 8, channels), f32)])

    def place(mine, recv):
        return call(
            functools.partial(place_kernel, slots=slots), "place", (meta, run_index, mine, recv),
            [smem, smem, vmem, vmem], [((rows_blk * cols_blk, channels), f32)], [],
            3 * 10**9, 4)[0].reshape(rows_blk, cols_blk, channels)

    zpart = half // n_zl
    moves = []
    for a in range(n_ha):
        for b in range(n_wa):
            moves.append((a * n_wa + b, ((b // n_zl) * n_q + a % n_q) * n_wa + (a // n_q) * n_zl + b % n_zl))
    barrier = lax.optimization_barrier

    if direct:
        def ha_perm(pairs):
            return [(top * n_q + a, top * n_q + b) for top in range(2) for a, b in pairs]

        def flat(value):
            return value.reshape(2 * rows_blk * 8, channels)

        n_part = rows_blk * 8
        zh0a, zh0b = flat(zh0a), flat(zh0b)
        zh1a, zh1b = flat(zh1a), flat(zh1b)
        wz0r = ppermute_xor(wz0b, "ha", n_ha, 1)
        zh0 = encode(jnp.concatenate([zh0a, zh0b]).reshape(4, n_part, channels))
        zh0r = []
        for k0 in range(2):
            for k1 in range(2):
                owners = []
                for a in range(n_ha):
                    for b in range(n_wa):
                        dest_a = ((b // 2) ^ k1) * n_q + a % n_q
                        dest_b = (a // n_q) * 2 + ((b % 2) ^ k0)
                        owners.append((a * n_wa + b, dest_a * n_wa + dest_b))
                zh0r.append(lax.ppermute(zh0[2 * k0 + k1], ("ha", "wa"), owners))
        wz0r, zh0r, wz1a, core_send, zh1a, zh1b, hw1, w_keep = barrier(
            (wz0r, zh0r, wz1a, core_send, zh1a, zh1b, hw1, w_keep))
        zh1r = ppermute_xor(encode(zh1b[None]), "wa", n_wa, 1)
        core_recv = ppermute_xor(core_send, "ha", n_ha, 1)
        hw_recv = lax.ppermute(encode(hw1[None]), "ha", swap_y)
        near0 = wz0a + wz0r
        zh_first = sum(decode_half(part[None])[0] for part in zh0r)
        w = w_keep + core_recv[cols_blk:]
        wr = ppermute_xor(w, "wa", n_wa, 2)
        zh1r, wr = barrier((zh1r, wr))
        near1 = wz1a + core_recv[:cols_blk]
        part1 = zh1a + decode_half(zh1r)[0]
        zhf = ppermute_xor(encode(part1[None, n_part:]), "wa", n_wa, 2)
        outer = (my_q == 0) | (my_q == 3)
        far = ppermute_xor(encode(jnp.where(outer, near1, near0).reshape(1, cols_blk * 8, channels)), "ha", n_ha, 2)
        w = w + wr
        w = w + ppermute_xor(w, "ha", n_ha, n_q)
        wr = ppermute_xor(w, "ha", n_ha, 2)
        zhf, wr, hw_recv = barrier((zhf, wr, hw_recv))
        zhm = lax.ppermute(encode(part1[None, :n_part] + decode_half(zhf)), ("ha", "wa"), moves)
        w = w + wr
        w = w + ppermute_xor(w, "wa", n_wa, 1)
        w_other = ppermute_xor(w, "ha", n_ha, 1)
        hw_grad = place(hw1, decode_half(hw_recv)[0])
        wz_grad = jnp.where(outer, near0, near1) + decode_half(far).reshape(near1.shape)
        zh_grad, w_in_grad, b_in_grad, w_out_grad, b_out_grad = call(
            functools.partial(finish_kernel, rows_blk=rows_blk), "finish", (meta, zh_first, decode_half(zhm)[0], w, w_other),
            [smem] + [vmem] * 4,
            [((2 * 8, rows_blk, channels), f32), ((channels, hidden), f32), ((1, hidden), f32),
             ((classes, hidden), f32), ((1, classes), f32)], [pltpu.VMEM((wgt_rows, hidden), f32)], 10**9, 4)
        return hw_grad, zh_grad, wz_grad, w_in_grad, b_in_grad[0], w_out_grad.T, b_out_grad[0]

    wz1b = core_send[:cols_blk]
    hw_grad = place(hw1, lax.ppermute(hw1, "ha", swap_y))
    wz_all = jnp.stack([wz0a, wz1a, wz1b, wz0b])
    wz_all = wz_all.transpose(1, 0, 2, 3).reshape(cols_blk, n_q, half // n_q, channels)
    part = jnp.take(wz_all.transpose(1, 0, 2, 3), jnp.arange(n_q) ^ my_q, axis=0)
    bit = 1
    while bit < n_q:
        part = part.reshape(part.shape[0] // 2, 2, cols_blk, half // n_q, channels)
        part = part[:, 0] + ppermute_xor(part[:, 1], "ha", n_ha, bit)
        bit *= 2
    wz_grad = part[0]
    zh_all = jnp.stack([zh0a, zh1a, zh1b, zh0b], axis=1)
    zh_all = zh_all.reshape(2, rows_blk, n_zl, zpart, channels).transpose(0, 2, 1, 3, 4)
    part = jnp.take(zh_all, jnp.arange(n_zl) ^ my_zl, axis=1)
    part = jnp.take(part, jnp.arange(2) ^ b1, axis=0)
    bit = 1
    while bit < n_zl:
        part = part.reshape(2, part.shape[1] // 2, 2, rows_blk, zpart, channels)
        part = part[:, :, 0] + ppermute_xor(part[:, :, 1], "wa", n_wa, bit)
        bit *= 2
    part = part[:, 0]
    part = part[0] + ppermute_xor(part[1], "wa", n_wa, n_zl)
    zh_grad = lax.ppermute(part, ("ha", "wa"), moves).transpose(1, 0, 2)
    w = w_keep + ppermute_xor(core_send[cols_blk:], "ha", n_ha, 1)
    bit = 2
    while bit < n_ha:
        w = w + ppermute_xor(w, "ha", n_ha, bit)
        bit *= 2
    bit = 1
    while bit < n_wa:
        w = w + ppermute_xor(w, "wa", n_wa, bit)
        bit *= 2
    w_other = ppermute_xor(w, "ha", n_ha, 1)
    w, w_other = [jnp.concatenate(jnp.split(v.reshape(2 * mid, 128), 2), axis=1) for v in (w, w_other)]
    upper = ha % 2 == 1
    wgt = jnp.concatenate([jnp.where(upper, w_other, w), jnp.where(upper, w, w_other)])
    first = channels + 8
    return (hw_grad, zh_grad, wz_grad, wgt[:channels], wgt[channels],
            wgt[first:first + classes].T, wgt[channels + 1, :classes])


def solution(mesh):
    placed = (
        P("ha", "wa", None),
        P(None, "ha", None),
        P("wa", None, None),
        P(),
        P(),
        P(),
        P(),
        P(("ha", "wa"), None),
        P(("ha", "wa")),
        P(("ha", "wa"), None, None),
    )
    return jax.shard_map(
        functools.partial(local, mesh.shape["ha"], mesh.shape["wa"]),
        mesh=mesh,
        in_specs=placed,
        out_specs=(
            P("ha", "wa", None),
            P("wa", "ha", None),
            P("wa", "ha", None),
            P(),
            P(),
            P(),
            P(),
        ),
        check_vma=False,
    )
```

time: 566 us -> 101 us (0.18)
  the two profiles are of different devices: /device:TPU:0 before, /device:TPU:7 now
where the time goes in v1:
time: 101 us
  Pallas kernels  50.9 us (50%)
  starting transfers between devices  28.3 us (28%)
  waiting for transfers between devices  14 us (14%)
  local copies, waits for them, and re-layouts  2.89 us (3%)
  other arithmetic  2.38 us (2%)
  between operations  2 us (2%)
    pallas_call x6, Pallas kernels, call(): pl.pallas_call(kernel, out_shape=[jax.ShapeDtypeStruct(shape, kind) for s...  50.9 us
    ppermute x10, starting transfers between devices, ppermute_xor(): return lax.ppermute(value, axis, [(i, i ^ mask) for i in range(size)])  16.7 us
    ppermute x10, waiting for transfers between devices, ppermute_xor(): return lax.ppermute(value, axis, [(i, i ^ mask) for i in range(size)])  8.98 us
    ppermute x4, starting transfers between devices, local(): zh0r.append(lax.ppermute(zh0[2 * k0 + k1], ('ha', 'wa'), owners))  6.68 us
    ppermute x1, waiting for transfers between devices, local(): recv0 = lax.ppermute(send0, 'ha', swap_y)  5.02 us
    ppermute x1, starting transfers between devices, local(): lax.ppermute(encode(part1[None, :n_part] + decode_half(zhf)), ('ha', 'wa'...  2.76 us
    unnamed x20, local copies, waits for them, and re-layouts  2.02 us
  transfers between devices with their start and end apart: 18, of which 6 were waited for; matrix products, arithmetic and copies ran while one was open for 2% of the time, Pallas kernels for 44%

profile of v1, /device:TPU:7, one launch (start us, length us, event | category | flops | bytes accessed | tf_op | source)
XLA Modules:
  0.0 100.5 jit_solution(5961464618375127848)
XLA Ops:
  2.1 4.9 %pack_send.1 = bf16[1680,128]{1,0:T(8,128)(2,1)} custom-call(s32[10]{0:T(128)} %stack.39.meta_ref.refs_0_, bf16[4096,128]{1,0:T(8,128)(2,1)} %bitcast.113, bf16[2048,128]{1,0:T(8,128)(2,1)} %bitcast.115, s32[512,128]{1,0:T(8,128)} %bitcast.117, s32[1,512]{1,0:T(1,128)} %rid_ref.1), custom_call_target="tpu_custom_call" | custom-call | flops 3000000000 | bytes 1048576 | tf_op jit(solution)/shard_map/pack_send/pallas_call | solution.py:468
  7.7 1.0 %copy-done.3 = bf16[64,32,128]{2,1,0:T(8,128)(2,1)S(1)} copy-done((bf16[64,32,128]{2,1,0:T(8,128)(2,1)S(1)}, bf16[64,32,128]{2,1,0:T(8,128)(2,1)}, u32[]{:S(2)}) %copy-start.3) | copy-done | bytes 524312
  8.7 0.9 copy-done.4
  9.6 3.5 %pack_own.1 = (bf16[1680,128]{1,0:T(8,128)(2,1)S(1)}, bf16[640,128]{1,0:T(8,128)(2,1)S(1)}, bf16[640,128]{1,0:T(8,128)(2,1)S(1)}, f32[128,16,128]{2,1,0:T(8,128)S(1)}, f32[128,16,128]{2,1,0:T(8,128)S(1)}) custom-call(s32[10]{0:T(128)S(1)} %copy-done, bf16[4096,128]{1,0:T(8,128)(2,1)S(1)} %bitcast.114, bf16[2048,128]{1,0:T(8,128)(2,1)S(1)} %bitcast.116, ...), custom_call_target="tpu_custom_call" | custom-call | flops 3000000000 | bytes 1048576 | tf_op jit(solution)/shard_map/pack_own/pallas_call | solution.py:468
  13.2 5.0 %collective-permute-done.refs_2_ = bf16[1680,128]{1,0:T(8,128)(2,1)} collective-permute-done((bf16[1680,128]{1,0:T(8,128)(2,1)}, bf16[1680,128]{1,0:T(8,128)(2,1)}, u32[]{:S(2)}, u32[]{:S(2)}) %collective-permute-start) | collective-permute-done | bytes 430112 | tf_op jit(solution)/shard_map/ppermute | solution.py:482
  18.5 19.5 %decode0.1 = (f32[128,8,128]{2,1,0:T(8,128)S(1)}, f32[128,8,128]{2,1,0:T(8,128)S(1)}, f32[64,8,128]{2,1,0:T(8,128)S(1)}, f32[64,8,128]{2,1,0:T(8,128)S(1)}, f32[...) custom-call(s32[10]{0:T(128)S(1)} %copy-done, bf16[1680,128]{1,0:T(8,128)(2,1)S(1)} %get-tuple-element.66.refs_1_, ...), custom_call_target="tpu_custom_call" | custom-call | flops 22000001024 | bytes 1048576 | tf_op jit(solution)/shard_map/decode0/pallas_call | solution.py:468
  38.0 1.9 %collective-permute-start.2 = (f32[128,8,128]{2,1,0:T(8,128)S(1)}, f32[128,8,128]{2,1,0:T(8,128)S(1)}, u32[]{:S(2)}, u32[]{:S(2)}) collective-permute-start(f32[128,8,128]{2,1,0:T(8,128)S(1)} %get-tuple-element.77), channel_id=1, source_target_pairs={{0,4},{4,0},{8,12},{12,8},{16,20},{20,16},{24,28},{28,24},{1,5},{5... | collective-permute-start | bytes 1572872 | tf_op jit(solution)/shard_map/ppermute | solution.py:25
  40.1 5.1 %collective-permute-start.3 = (f16[272,128]{1,0:T(8,128)(2,1)S(1)}, f16[272,128]{1,0:T(8,128)(2,1)S(1)}, u32[]{:S(2)}, u32[]{:S(2)}) collective-permute-start(f16[272,128]{1,0:T(8,128)(2,1)S(1)} %get-tuple-element.126), channel_id=1, source_target_pairs={{0,0},{1,1},{2,16},{3,17},{4,4},{5,5},{6,20},{7,21},{8,8},{9,9},{1... | collective-permute-start | bytes 208904 | tf_op jit(solution)/shard_map/ppermute | solution.py:567
  45.3 1.1 %collective-permute-start.5 = (f16[272,128]{1,0:T(8,128)(2,1)S(1)}, f16[272,128]{1,0:T(8,128)(2,1)S(1)}, u32[]{:S(2)}, u32[]{:S(2)}) collective-permute-start(f16[272,128]{1,0:T(8,128)(2,1)S(1)} %get-tuple-element.128), channel_id=1, source_target_pairs={{0,1},{1,0},{2,17},{3,16},{4,5},{5,4},{6,21},{7,20},{8,9},{9,8},{1... | collective-permute-start | bytes 208904 | tf_op jit(solution)/shard_map/ppermute | solution.py:567
  46.8 19.5 %decode1.1 = (f32[128,8,128]{2,1,0:T(8,128)S(1)}, f32[148,8,128]{2,1,0:T(8,128)S(1)}, f32[64,8,128]{2,1,0:T(8,128)S(1)}, f32[64,8,128]{2,1,0:T(8,128)S(1)}, f32[...) custom-call(s32[10]{0:T(128)S(1)} %copy-done, bf16[1680,128]{1,0:T(8,128)(2,1)S(1)} %get-tuple-element.66.refs_1_, ...), custom_call_target="tpu_custom_call" | custom-call | flops 22000001024 | bytes 1048576 | tf_op jit(solution)/shard_map/decode1/pallas_call | solution.py:468
  67.0 1.4 %collective-permute-start.8 = (f32[148,8,128]{2,1,0:T(8,128)S(1)}, f32[148,8,128]{2,1,0:T(8,128)S(1)}, u32[]{:S(2)}, u32[]{:S(2)}) collective-permute-start(f32[148,8,128]{2,1,0:T(8,128)S(1)} %get-tuple-element.95), channel_id=1, source_target_pairs={{0,4},{4,0},{8,12},{12,8},{16,20},{20,16},{24,28},{28,24},{1,5},{5... | collective-permute-start | bytes 1818632 | tf_op jit(solution)/shard_map/ppermute | solution.py:25
  68.6 1.7 %collective-permute-start.13 = (f16[1,1040,128]{2,1,0:T(8,128)(2,1)S(1)}, f16[1,1040,128]{2,1,0:T(8,128)(2,1)S(1)}, u32[]{:S(2)}, u32[]{:S(2)}) collective-permute-start(f16[1,1040,128]{2,1,0:T(8,128)(2,1)S(1)} %pad_maximum_fusion.1), channel_id=1, source_target_pairs={{0,16},{4,20},{8,24},{12,28},{16,0},{20,4},{24,8},{28,12},{1,17},{... | collective-permute-start | bytes 798728 | tf_op jit(solution)/shard_map/ppermute | solution.py:572
  70.5 3.0 %collective-permute-start.9 = (f32[20,8,128]{2,1,0:T(8,128)S(1)}, f32[20,8,128]{2,1,0:T(8,128)S(1)}, u32[]{:S(2)}, u32[]{:S(2)}) collective-permute-start(f32[20,8,128]{2,1,0:T(8,128)S(1)} %slice_add_fusion.1), channel_id=1, source_target_pairs={{0,2},{1,3},{2,0},{3,1},{4,6},{5,7},{6,4},{7,5},{8,10},{9,11},{10,... | collective-permute-start | bytes 245768 | tf_op jit(solution)/shard_map/ppermute | solution.py:25
  73.6 4.2 %collective-permute-done.9 = f32[20,8,128]{2,1,0:T(8,128)S(1)} collective-permute-done((f32[20,8,128]{2,1,0:T(8,128)S(1)}, f32[20,8,128]{2,1,0:T(8,128)S(1)}, u32[]{:S(2)}, u32[]{:S(2)}) %collective-permute-start.9) | collective-permute-done | bytes 81952 | tf_op jit(solution)/shard_map/ppermute | solution.py:25
  78.0 1.2 %collective-permute-start.11 = (f32[20,8,128]{2,1,0:T(8,128)S(1)}, f32[20,8,128]{2,1,0:T(8,128)S(1)}, u32[]{:S(2)}, u32[]{:S(2)}) collective-permute-start(f32[20,8,128]{2,1,0:T(8,128)S(1)} %add.141), channel_id=1, source_target_pairs={{0,16},{4,20},{8,24},{12,28},{16,0},{20,4},{24,8},{28,12},{1,17},{... | collective-permute-start | bytes 245768 | tf_op jit(solution)/shard_map/ppermute | solution.py:25
  79.5 1.9 %collective-permute-done.11 = f32[20,8,128]{2,1,0:T(8,128)S(1)} collective-permute-done((f32[20,8,128]{2,1,0:T(8,128)S(1)}, f32[20,8,128]{2,1,0:T(8,128)S(1)}, u32[]{:S(2)}, u32[]{:S(2)}) %collective-permute-start.11) | collective-permute-done | bytes 81952 | tf_op jit(solution)/shard_map/ppermute | solution.py:25
  81.7 1.4 %collective-permute-start.17 = (f16[1,1040,128]{2,1,0:T(8,128)(2,1)S(1)}, f16[1,1040,128]{2,1,0:T(8,128)(2,1)S(1)}, u32[]{:S(2)}, u32[]{:S(2)}) collective-permute-start(f16[1,1040,128]{2,1,0:T(8,128)(2,1)S(1)} %pad_maximum_fusion.2), channel_id=1, source_target_pairs={{0,8},{4,12},{8,0},{12,4},{16,24},{20,28},{24,16},{28,20},{1,9},{5... | collective-permute-start | bytes 798728 | tf_op jit(solution)/shard_map/ppermute | solution.py:25
  83.4 1.6 %collective-permute-done.12 = f32[20,8,128]{2,1,0:T(8,128)S(1)} collective-permute-done((f32[20,8,128]{2,1,0:T(8,128)S(1)}, f32[20,8,128]{2,1,0:T(8,128)S(1)}, u32[]{:S(2)}, u32[]{:S(2)}) %collective-permute-start.12) | collective-permute-done | bytes 81952 | tf_op jit(solution)/shard_map/ppermute | solution.py:25
  85.3 2.8 %collective-permute-start.14 = (f16[1,272,128]{2,1,0:T(8,128)(2,1)S(1)}, f16[1,272,128]{2,1,0:T(8,128)(2,1)S(1)}, u32[]{:S(2)}, u32[]{:S(2)}) collective-permute-start(f16[1,272,128]{2,1,0:T(8,128)(2,1)S(1)} %pad_maximum_fusion.6), channel_id=1, source_target_pairs={{0,0},{1,1},{2,16},{3,17},{4,4},{5,5},{6,20},{7,21},{8,8},{9,9},{1... | collective-permute-start | bytes 208904 | tf_op jit(solution)/shard_map/ppermute | solution.py:587
  88.1 1.1 %collective-permute-start.15 = (f32[20,8,128]{2,1,0:T(8,128)S(1)}, f32[20,8,128]{2,1,0:T(8,128)S(1)}, u32[]{:S(2)}, u32[]{:S(2)}) collective-permute-start(f32[20,8,128]{2,1,0:T(8,128)S(1)} %add.148), channel_id=1, source_target_pairs={{0,1},{1,0},{2,3},{3,2},{4,5},{5,4},{6,7},{7,6},{8,9},{9,8},{10,11... | collective-permute-start | bytes 245768 | tf_op jit(solution)/shard_map/ppermute | solution.py:25
  89.2 2.2 %place.1 = f32[4096,128]{1,0:T(8,128)} custom-call(s32[10]{0:T(128)S(1)} %copy-done, s32[1,512]{1,0:T(1,128)S(1)} %copy-done.5, f32[1024,128]{1,0:T(8,128)S(1)} %get-tuple-element.91.mine_ref, f32[1024,128]{1,0:T(8,128)S(1)} %fusion.2.recv_ref), custom_call_target="tpu_custom_call" | custom-call | flops 3000000000 | bytes 1048576 | tf_op jit(solution)/shard_map/place/pallas_call | solution.py:468
  91.4 1.0 fusion.1
  92.4 5.8 %collective-permute-start.16 = (f32[20,8,128]{2,1,0:T(8,128)S(1)}, f32[20,8,128]{2,1,0:T(8,128)S(1)}, u32[]{:S(2)}, u32[]{:S(2)}) collective-permute-start(f32[20,8,128]{2,1,0:T(8,128)S(1)} %add.149.w_mine_ref), channel_id=1, source_target_pairs={{0,4},{4,0},{8,12},{12,8},{16,20},{20,16},{24,28},{28,24},{1,5},{5... | collective-permute-start | bytes 245768 | tf_op jit(solution)/shard_map/ppermute | solution.py:25
  99.2 1.3 %finish.1 = (f32[16,32,128]{2,1,0:T(8,128)}, f32[128,256]{1,0:T(8,128)}, f32[1,256]{1,0:T(1,128)}, f32[18,256]{1,0:T(8,128)}, f32[1,18]{1,0:T(1,128)}) custom-call(s32[10]{0:T(128)S(1)} %copy-done, f32[256,128]{1,0:T(8,128)S(1)} %fusion.13.zh0_ref, f32[256,128]{1,0:T(8,128)S(1)} %fusion.10.zh1_ref, f32[20,8,128]{2,1,0:T(8,128)S(1)} %add.149.w_mine_ref, ...), custom_call_target="tpu_custom_call" | custom-call | flops 1000000000 | bytes 1048576 | tf_op jit(solution)/shard_map/finish/pallas_call | solution.py:468
  (110 shorter events, 5.4 us)
Async XLA Ops:
  2.0 5.5 %copy-start.9 = (f32[18]{0:T(128)S(1)}, f32[18]{0:T(128)}, u32[]{:S(2)}) copy-start(f32[18]{0:T(128)} %param.16) | copy-start | bytes 220
  2.0 5.6 %copy-start.8 = (f32[256]{0:T(256)S(1)}, f32[256]{0:T(256)}, u32[]{:S(2)}) copy-start(f32[256]{0:T(256)} %param.14) | copy-start | bytes 3076
  2.0 5.6 %copy-start = (s32[10]{0:T(128)S(1)}, s32[10]{0:T(128)}, u32[]{:S(2)}) copy-start(s32[10]{0:T(128)} %stack.39.meta_ref.refs_0_) | copy-start | bytes 124
  2.0 5.6 %copy-start.1 = (bf16[128,64,128]{2,1,0:T(8,128)(2,1)S(1)}, bf16[128,64,128]{2,1,0:T(8,128)(2,1)}, u32[]{:S(2)}) copy-start(bf16[128,64,128]{2,1,0:T(8,128)(2,1)} %wz_ref.1) | copy-start | bytes 6291460
  2.0 5.6 %copy-start.2 = (bf16[32,128,128]{2,1,0:T(8,128)(2,1)S(1)}, bf16[32,128,128]{2,1,0:T(8,128)(2,1)}, u32[]{:S(2)}) copy-start(bf16[32,128,128]{2,1,0:T(8,128)(2,1)} %param.10) | copy-start | bytes 3145732
  2.1 5.6 %copy-start.5 = (s32[1,512]{1,0:T(1,128)S(1)}, s32[1,512]{1,0:T(1,128)}, u32[]{:S(2)}) copy-start(s32[1,512]{1,0:T(1,128)} %rid_ref.1) | copy-start | bytes 6148
  7.0 11.2 %collective-permute-start = (bf16[1680,128]{1,0:T(8,128)(2,1)}, bf16[1680,128]{1,0:T(8,128)(2,1)}, u32[]{:S(2)}, u32[]{:S(2)}) collective-permute-start(bf16[1680,128]{1,0:T(8,128)(2,1)} %pack_send.1), channel_id=1, source_target_pairs={{0,16},{4,20},{8,24},{12,28},{16,0},{20,4},{24,8},{28,12},{1,17},{... | collective-permute-start | bytes 1290248 | tf_op jit(solution)/shard_map/ppermute | solution.py:482
  18.2 19.8 %collective-permute-start.1 = (bf16[640,128]{1,0:T(8,128)(2,1)S(1)}, bf16[640,128]{1,0:T(8,128)(2,1)S(1)}, u32[]{:S(2)}, u32[]{:S(2)}) collective-permute-start(bf16[640,128]{1,0:T(8,128)(2,1)S(1)} %get-tuple-element.65), channel_id=1, source_target_pairs={{0,16},{4,20},{8,24},{12,28},{16,0},{20,4},{24,8},{28,12},{1,17},{... | collective-permute-start | bytes 491528 | tf_op jit(solution)/shard_map/ppermute | solution.py:492
  38.0 28.4 %collective-permute-start.2 = (f32[128,8,128]{2,1,0:T(8,128)S(1)}, f32[128,8,128]{2,1,0:T(8,128)S(1)}, u32[]{:S(2)}, u32[]{:S(2)}) collective-permute-start(f32[128,8,128]{2,1,0:T(8,128)S(1)} %get-tuple-element.77), channel_id=1, source_target_pairs={{0,4},{4,0},{8,12},{12,8},{16,20},{20,16},{24,28},{28,24},{1,5},{5... | collective-permute-start | bytes 1572872 | tf_op jit(solution)/shard_map/ppermute | solution.py:25
  40.1 26.2 %collective-permute-start.3 = (f16[272,128]{1,0:T(8,128)(2,1)S(1)}, f16[272,128]{1,0:T(8,128)(2,1)S(1)}, u32[]{:S(2)}, u32[]{:S(2)}) collective-permute-start(f16[272,128]{1,0:T(8,128)(2,1)S(1)} %get-tuple-element.126), channel_id=1, source_target_pairs={{0,0},{1,1},{2,16},{3,17},{4,4},{5,5},{6,20},{7,21},{8,8},{9,9},{1... | collective-permute-start | bytes 208904 | tf_op jit(solution)/shard_map/ppermute | solution.py:567
  45.2 21.1 %collective-permute-start.4 = (f16[272,128]{1,0:T(8,128)(2,1)S(1)}, f16[272,128]{1,0:T(8,128)(2,1)S(1)}, u32[]{:S(2)}, u32[]{:S(2)}) collective-permute-start(f16[272,128]{1,0:T(8,128)(2,1)S(1)} %get-tuple-element.127), channel_id=1, source_target_pairs={{0,16},{1,17},{2,0},{3,1},{4,20},{5,21},{6,4},{7,5},{8,24},{9,25},... | collective-permute-start | bytes 208904 | tf_op jit(solution)/shard_map/ppermute | solution.py:567
  45.3 21.0 %collective-permute-start.5 = (f16[272,128]{1,0:T(8,128)(2,1)S(1)}, f16[272,128]{1,0:T(8,128)(2,1)S(1)}, u32[]{:S(2)}, u32[]{:S(2)}) collective-permute-start(f16[272,128]{1,0:T(8,128)(2,1)S(1)} %get-tuple-element.128), channel_id=1, source_target_pairs={{0,1},{1,0},{2,17},{3,16},{4,5},{5,4},{6,21},{7,20},{8,9},{9,8},{1... | collective-permute-start | bytes 208904 | tf_op jit(solution)/shard_map/ppermute | solution.py:567
  46.4 19.9 %collective-permute-start.6 = (f16[272,128]{1,0:T(8,128)(2,1)S(1)}, f16[272,128]{1,0:T(8,128)(2,1)S(1)}, u32[]{:S(2)}, u32[]{:S(2)}) collective-permute-start(f16[272,128]{1,0:T(8,128)(2,1)S(1)} %get-tuple-element.125), channel_id=1, source_target_pairs={{0,17},{1,16},{2,1},{3,0},{4,21},{5,20},{6,5},{7,4},{8,25},{9,24},... | collective-permute-start | bytes 208904 | tf_op jit(solution)/shard_map/ppermute | solution.py:567
  66.5 7.1 %collective-permute-start.7 = (f16[1,528,128]{2,1,0:T(8,128)(2,1)S(1)}, f16[1,528,128]{2,1,0:T(8,128)(2,1)S(1)}, u32[]{:S(2)}, u32[]{:S(2)}) collective-permute-start(f16[1,528,128]{2,1,0:T(8,128)(2,1)S(1)} %pad_maximum_fusion.3), channel_id=1, source_target_pairs={{0,1},{1,0},{2,3},{3,2},{4,5},{5,4},{6,7},{7,6},{8,9},{9,8},{10,11... | collective-permute-start | bytes 405512 | tf_op jit(solution)/shard_map/ppermute | solution.py:25
  67.0 3.5 %collective-permute-start.8 = (f32[148,8,128]{2,1,0:T(8,128)S(1)}, f32[148,8,128]{2,1,0:T(8,128)S(1)}, u32[]{:S(2)}, u32[]{:S(2)}) collective-permute-start(f32[148,8,128]{2,1,0:T(8,128)S(1)} %get-tuple-element.95), channel_id=1, source_target_pairs={{0,4},{4,0},{8,12},{12,8},{16,20},{20,16},{24,28},{28,24},{1,5},{5... | collective-permute-start | bytes 1818632 | tf_op jit(solution)/shard_map/ppermute | solution.py:25
  68.6 14.5 %collective-permute-start.13 = (f16[1,1040,128]{2,1,0:T(8,128)(2,1)S(1)}, f16[1,1040,128]{2,1,0:T(8,128)(2,1)S(1)}, u32[]{:S(2)}, u32[]{:S(2)}) collective-permute-start(f16[1,1040,128]{2,1,0:T(8,128)(2,1)S(1)} %pad_maximum_fusion.1), channel_id=1, source_target_pairs={{0,16},{4,20},{8,24},{12,28},{16,0},{20,4},{24,8},{28,12},{1,17},{... | collective-permute-start | bytes 798728 | tf_op jit(solution)/shard_map/ppermute | solution.py:572
  70.5 7.4 %collective-permute-start.9 = (f32[20,8,128]{2,1,0:T(8,128)S(1)}, f32[20,8,128]{2,1,0:T(8,128)S(1)}, u32[]{:S(2)}, u32[]{:S(2)}) collective-permute-start(f32[20,8,128]{2,1,0:T(8,128)S(1)} %slice_add_fusion.1), channel_id=1, source_target_pairs={{0,2},{1,3},{2,0},{3,1},{4,6},{5,7},{6,4},{7,5},{8,10},{9,11},{10,... | collective-permute-start | bytes 245768 | tf_op jit(solution)/shard_map/ppermute | solution.py:25
  78.0 3.4 %collective-permute-start.11 = (f32[20,8,128]{2,1,0:T(8,128)S(1)}, f32[20,8,128]{2,1,0:T(8,128)S(1)}, u32[]{:S(2)}, u32[]{:S(2)}) collective-permute-start(f32[20,8,128]{2,1,0:T(8,128)S(1)} %add.141), channel_id=1, source_target_pairs={{0,16},{4,20},{8,24},{12,28},{16,0},{20,4},{24,8},{28,12},{1,17},{... | collective-permute-start | bytes 245768 | tf_op jit(solution)/shard_map/ppermute | solution.py:25
  79.3 4.1 %collective-permute-start.10 = (f16[1,272,128]{2,1,0:T(8,128)(2,1)S(1)}, f16[1,272,128]{2,1,0:T(8,128)(2,1)S(1)}, u32[]{:S(2)}, u32[]{:S(2)}) collective-permute-start(f16[1,272,128]{2,1,0:T(8,128)(2,1)S(1)} %pad_maximum_fusion.5), channel_id=1, source_target_pairs={{0,2},{1,3},{2,0},{3,1},{4,6},{5,7},{6,4},{7,5},{8,10},{9,11},{10,... | collective-permute-start | bytes 208904 | tf_op jit(solution)/shard_map/ppermute | solution.py:25
  81.4 3.7 %collective-permute-start.12 = (f32[20,8,128]{2,1,0:T(8,128)S(1)}, f32[20,8,128]{2,1,0:T(8,128)S(1)}, u32[]{:S(2)}, u32[]{:S(2)}) collective-permute-start(f32[20,8,128]{2,1,0:T(8,128)S(1)} %add.142), channel_id=1, source_target_pairs={{0,8},{4,12},{8,0},{12,4},{16,24},{20,28},{24,16},{28,20},{1,9},{5... | collective-permute-start | bytes 245768 | tf_op jit(solution)/shard_map/ppermute | solution.py:25
  81.7 9.7 %collective-permute-start.17 = (f16[1,1040,128]{2,1,0:T(8,128)(2,1)S(1)}, f16[1,1040,128]{2,1,0:T(8,128)(2,1)S(1)}, u32[]{:S(2)}, u32[]{:S(2)}) collective-permute-start(f16[1,1040,128]{2,1,0:T(8,128)(2,1)S(1)} %pad_maximum_fusion.2), channel_id=1, source_target_pairs={{0,8},{4,12},{8,0},{12,4},{16,24},{20,28},{24,16},{28,20},{1,9},{5... | collective-permute-start | bytes 798728 | tf_op jit(solution)/shard_map/ppermute | solution.py:25
  85.3 7.1 %collective-permute-start.14 = (f16[1,272,128]{2,1,0:T(8,128)(2,1)S(1)}, f16[1,272,128]{2,1,0:T(8,128)(2,1)S(1)}, u32[]{:S(2)}, u32[]{:S(2)}) collective-permute-start(f16[1,272,128]{2,1,0:T(8,128)(2,1)S(1)} %pad_maximum_fusion.6), channel_id=1, source_target_pairs={{0,0},{1,1},{2,16},{3,17},{4,4},{5,5},{6,20},{7,21},{8,8},{9,9},{1... | collective-permute-start | bytes 208904 | tf_op jit(solution)/shard_map/ppermute | solution.py:587
  88.1 4.3 %collective-permute-start.15 = (f32[20,8,128]{2,1,0:T(8,128)S(1)}, f32[20,8,128]{2,1,0:T(8,128)S(1)}, u32[]{:S(2)}, u32[]{:S(2)}) collective-permute-start(f32[20,8,128]{2,1,0:T(8,128)S(1)} %add.148), channel_id=1, source_target_pairs={{0,1},{1,0},{2,3},{3,2},{4,5},{5,4},{6,7},{7,6},{8,9},{9,8},{10,11... | collective-permute-start | bytes 245768 | tf_op jit(solution)/shard_map/ppermute | solution.py:25
  92.4 6.8 %collective-permute-start.16 = (f32[20,8,128]{2,1,0:T(8,128)S(1)}, f32[20,8,128]{2,1,0:T(8,128)S(1)}, u32[]{:S(2)}, u32[]{:S(2)}) collective-permute-start(f32[20,8,128]{2,1,0:T(8,128)S(1)} %add.149.w_mine_ref), channel_id=1, source_target_pairs={{0,4},{4,0},{8,12},{12,8},{16,20},{20,16},{24,28},{28,24},{1,5},{5... | collective-permute-start | bytes 245768 | tf_op jit(solution)/shard_map/ppermute | solution.py:25
  (4 other events, 12.8 us)

commit v2 on v1

--- a/solution.py
+++ b/solution.py
@@ -46,18 +46,21 @@
         ref[base + n_zh:base + n_zh + n_lab, :] = merged.astype(jnp.bfloat16)
 
 
-def load_inputs(hw_ref, zh_ref, lab_ref, ids_ref, hw_raw, zh_raw, lab_raw, ids_raw, rid_ref, sems,
-                hw_full, zh_full, lab_pad, slots):
-    copies = [pltpu.make_async_copy(a, b, sems.at[n]) for n, (a, b) in enumerate(
-        ((hw_ref, hw_raw), (ids_ref, rid_ref), (ids_ref, ids_raw), (zh_ref, zh_raw), (lab_ref, lab_raw)))]
+def fetch(pairs, sems):
+    copies = [pltpu.make_async_copy(src, dst, sems.at[n]) for n, (src, dst) in enumerate(pairs)]
     for copy in copies:
         copy.start()
     for copy in copies:
         copy.wait()
-    hw_full[...] = hw_raw[...].astype(jnp.float32)
+
+
+def widen_planes(zh_raw, lab_raw, zh_full, lab_pad, slots):
     zh_full[...] = zh_raw[...].astype(jnp.float32)
     lab_pad[0:slots, :] = jnp.zeros((slots, lab_raw.shape[1]), jnp.float32)
     lab_pad[slots:, :] = lab_raw[...].astype(jnp.float32)
+
+
+def twice(ids_raw, slots):
     ids = [ids_raw[:, k * 128:(k + 1) * 128] for k in range(slots // 128)]
     return jnp.concatenate(ids + ids, axis=0)
 
@@ -83,14 +86,21 @@
     ref[base:base + 16, :] = both.astype(jnp.float32).astype(jnp.bfloat16)
 
 
-def pack_send_kernel(meta_ref, hw_ref, zh_ref, lab_ref, ids_ref, send_ref,
-                     hw_raw, zh_raw, lab_raw, ids_raw, rid_ref, sems,
-                     hw_full, hw_rows, zh_full, lab_pad, *, depth_z, rows_blk, slots, pair_cols):
-    half = depth_z // 2
+def pack_plane_kernel(meta_ref, zh_ref, lab_ref, send_ref, zh_raw, lab_raw, sems, zh_full, lab_pad,
+                      *, depth_z, rows_blk, slots, pair_cols):
+    fetch(((zh_ref, zh_raw), (lab_ref, lab_raw)), sems)
+    widen_planes(zh_raw, lab_raw, zh_full, lab_pad, slots)
+    fill_planes(1 - meta_ref[0], (send_ref, None), (0, 0), zh_full, lab_pad, meta_ref[1],
+                half=depth_z // 2, rows_blk=rows_blk, depth_z=depth_z, slots=slots)
+
+
+def pack_rows_kernel(meta_ref, hw_ref, ids_ref, send_ref, hw_raw, ids_raw, rid_ref, sems, hw_full, hw_rows,
+                     *, depth_z, rows_blk, slots, pair_cols):
     n_hw = 2 * slots
     count = meta_ref[1]
-    ids = load_inputs(hw_ref, zh_ref, lab_ref, ids_ref, hw_raw, zh_raw, lab_raw, ids_raw, rid_ref, sems,
-                      hw_full, zh_full, lab_pad, slots)
+    fetch(((hw_ref, hw_raw), (ids_ref, rid_ref), (ids_ref, ids_raw)), sems)
+    hw_full[...] = hw_raw[...].astype(jnp.float32)
+    ids = twice(ids_raw, slots)
     gather_rows(rid_ref, hw_full, hw_rows, slots, slots - count)
     send_ref[0:n_hw, :] = hw_rows[...].astype(jnp.bfloat16)
     down = slots - count
@@ -101,12 +111,10 @@
     before = pltpu.roll(turned, jnp.bitwise_and(rows + 1, 7), 0)
     lane = lax.broadcasted_iota(jnp.int32, ids.shape, 1)
     put_ids(send_ref, n_hw, jnp.where(lane < lanes, before, here), pair_cols.bit_length() - 1, pair_cols - 1)
-    fill_planes(1 - meta_ref[0], (send_ref, None), (n_hw + 16, 0), zh_full, lab_pad, count,
-                half=half, rows_blk=rows_blk, depth_z=depth_z, slots=slots)
 
 
 def pack_own_kernel(meta_ref, hw_ref, zh_ref, lab_ref, ids_ref, wz_ref,
-                    own0_ref, own1_ref, send1_ref, wz0_ref, wz1_ref,
+                    hw_out, own0_ref, own1_ref, send1_ref, wz0_ref, wz1_ref,
                     hw_raw, zh_raw, lab_raw, ids_raw, rid_ref, sems,
                     hw_full, hw_rows, zh_full, lab_pad, wz_raw, wz_sem,
                     *, depth_z, rows_blk, slots, pair_cols):
@@ -115,12 +123,13 @@
     z0 = pl.multiple_of(meta_ref[0] * half, half)
     wz_copy = pltpu.make_async_copy(wz_ref.at[:, pl.ds(z0, half), :], wz_raw, wz_sem)
     wz_copy.start()
-    ids = load_inputs(hw_ref, zh_ref, lab_ref, ids_ref, hw_raw, zh_raw, lab_raw, ids_raw, rid_ref, sems,
-                      hw_full, zh_full, lab_pad, slots)
+    fetch(((hw_ref, hw_raw), (ids_ref, rid_ref), (ids_ref, ids_raw), (zh_ref, zh_raw), (lab_ref, lab_raw)), sems)
+    hw_full[...] = hw_raw[...].astype(jnp.float32)
+    widen_planes(zh_raw, lab_raw, zh_full, lab_pad, slots)
     gather_rows(rid_ref, hw_full, hw_rows, slots, 0)
-    own0_ref[0:n_hw, :] = hw_rows[...].astype(jnp.bfloat16)
-    put_ids(own0_ref, n_hw, ids, pair_cols.bit_length() - 1, pair_cols - 1)
-    fill_planes(meta_ref[0], (own0_ref, own1_ref), (n_hw + 16, 0), zh_full, lab_pad, slots,
+    hw_out[0:n_hw, :] = hw_rows[...].astype(jnp.bfloat16)
+    put_ids(hw_out, n_hw, twice(ids_raw, slots), pair_cols.bit_length() - 1, pair_cols - 1)
+    fill_planes(meta_ref[0], (own0_ref, own1_ref), (0, 0), zh_full, lab_pad, slots,
                 half=half, rows_blk=rows_blk, depth_z=depth_z, slots=slots)
     fill_planes(1 - meta_ref[0], (None, send1_ref), (0, 0), zh_full, lab_pad, meta_ref[1],
                 half=half, rows_blk=rows_blk, depth_z=depth_z, slots=slots)
@@ -136,12 +145,6 @@
     lax.fori_loop(0, 2 * pair_cols, widen, 0, unroll=8)
 
 
-def run_slices(dfeat_ref, j, base=0):
-    g, par = j // GROUP, j % GROUP
-    at = [base + g * 128 + p * 64 + par * ZC for p in range(2)]
-    return [dfeat_ref[pl.ds(at[p], ZC), :] for p in range(2)]
-
-
 def add_zh(d, row, zh_accs):
     both = d[0] + d[1]
     now = [acc[row] for acc in zh_accs]
@@ -192,14 +195,12 @@
     n_hw = 2 * slots
     n_zh = rows_blk * ZC
     n_lab = slots // GROUP
-    meta_ref, hw_own, hw_recv = refs[:3]
-    refs = refs[3:]
-    if first:
-        z_own, z_recv, z_base = hw_own, hw_recv, n_hw + 16
-    else:
-        z_own, z_recv, z_base = refs[0], refs[1], 0
-        hw_prev, wgt_prev = refs[2:4]
-        refs = refs[4:]
+    meta_ref, hw_own, hw_recv, z_own, z_recv = refs[:5]
+    refs = refs[5:]
+    z_base = 0
+    if not first:
+        hw_prev, wgt_prev = refs[:2]
+        refs = refs[2:]
     wz_full, w_in_ref, w_in_t_ref, b_in_ref, w_out_t_ref, w_out_half_ref, b_out_ref, sel_ref = refs[:8]
     refs = refs[8:]
     if first:
@@ -209,10 +210,9 @@
         wz_out0, core_out, zh_out0, zh_out1, hw_out, wgt_keep = refs[:6]
         refs = refs[6:]
     (hw_full, zh_full, lab_full, hw_acc, w_in_acc, w_out_acc, b_out_acc, ids_ref, ids_sem) = refs[:9]
-    bufs = (refs[9:14], refs[14:19])
-    outs = (refs[19:22], refs[22:25])
-    dfeat_ref = refs[25]
-    wz_accs, zh_accs, ids_vec, wgt_all = refs[26:28], refs[28:30], refs[30], refs[31]
+    bufs = (refs[9:13], refs[13:17])
+    outs = (refs[17:19], refs[19:21])
+    wz_accs, zh_accs, ids_vec, wgt_all = refs[21:23], refs[23:25], refs[25], refs[26]
     count = meta_ref[1]
     rel_own = meta_ref[7]
 
@@ -248,38 +248,39 @@
 
     groups = RUNS // GROUP
     n_ch = w_in_ref.shape[0]
-    for left_ref, dhid_ref, dpre_ref in outs:
+    for left_ref, dpre_ref in outs:
         left_ref[n_ch:, :] = sel_ref[...]
     class_ids = lax.broadcasted_iota(jnp.int32, (CLS_ROWS, 128), 0).astype(jnp.float32)
     nt = (((1,), (1,)), ((), ()))
 
     def front(b, buf):
-        feat_ref, hid_ref, slope_ref, logit_ref, pre_ref = buf
-        pieces = []
+        feat_ref, hid_ref, slope_ref, logit_ref = buf
         runs = read_runs(ids_ref, RUNS * b, RUNS)
         for g in range(groups):
+            pieces = []
             for p in range(2):
                 for par in range(GROUP):
                     row, col = runs[GROUP * g + par]
                     at = pl.multiple_of(2 * RUNS * b, 2 * RUNS) + 2 * (GROUP * g + par) + p
                     total = hw_full[pl.ds(at, 1), :] + zh_full[row] + wz_full[col + p]
                     pieces.append(total.astype(jnp.bfloat16))
-        feat = jnp.concatenate(pieces, axis=0)
-        feat_ref[...] = feat
-        pre_ref[...] = jnp.dot(feat, w_in_ref[...], preferred_element_type=jnp.float32)
-        for r in range(0, ROWS, STRIP):
-            pre = pre_ref[r:r + STRIP, :] + b_in_ref[...]
-            t = jnp.tanh(pre)
-            a = 1.0 + t
-            u = pre * a
-            hid_ref[r:r + STRIP, :] = u.astype(jnp.bfloat16)
-            slope_ref[r:r + STRIP, :] = a + u * (1.0 - t)
+            feat = jnp.concatenate(pieces, axis=0)
+            feat_ref[g * 128:(g + 1) * 128, :] = feat
+            pre_all = jnp.dot(feat, w_in_ref[...], preferred_element_type=jnp.float32)
+            for r in range(0, 128, STRIP):
+                pre = pre_all[r:r + STRIP] + b_in_ref[...]
+                t = jnp.tanh(pre)
+                a = 1.0 + t
+                u = pre * a
+                at = g * 128 + r
+                hid_ref[at:at + STRIP, :] = u.astype(jnp.bfloat16)
+                slope_ref[at:at + STRIP, :] = a + u * (1.0 - t)
         logits = lax.dot_general(w_out_t_ref[...], hid_ref[...], nt, preferred_element_type=jnp.float32)
         logit_ref[...] = logits[0:CLS_ROWS, :]
 
     def middle(b, buf, out):
-        feat_ref, hid_ref, slope_ref, logit_ref, pre_ref = buf
-        left_ref, dhid_ref, dpre_ref = out
+        feat_ref, hid_ref, slope_ref, logit_ref = buf
+        left_ref, dpre_ref = out
         left_ref[0:n_ch, :] = jnp.transpose(feat_ref[...], (1, 0))
         dl_tiles = []
         b_part = None
@@ -298,22 +299,26 @@
         dl_all = jnp.concatenate([dl_all, jnp.zeros((CLS_PAD - CLS_ROWS, ROWS), jnp.float32)], axis=0)
         dl_t = jnp.transpose(dl_all, (1, 0)).astype(jnp.bfloat16)
         w_out_acc[...] += jnp.dot(dl_all.astype(jnp.bfloat16), hid_ref[...], preferred_element_type=jnp.float32)
-        dhid_ref[...] = jnp.dot(dl_t, w_out_half_ref[...], preferred_element_type=jnp.float32)
-        for r in range(0, ROWS, STRIP):
-            dpre_ref[r:r + STRIP, :] = (dhid_ref[r:r + STRIP, :] * slope_ref[r:r + STRIP, :]).astype(jnp.bfloat16)
+        for g in range(groups):
+            dhid = jnp.dot(dl_t[g * 128:(g + 1) * 128], w_out_half_ref[...], preferred_element_type=jnp.float32)
+            for r in range(0, 128, STRIP):
+                at = g * 128 + r
+                dpre_ref[at:at + STRIP, :] = (dhid[r:r + STRIP] * slope_ref[at:at + STRIP, :]).astype(jnp.bfloat16)
 
     def back(b, out):
-        left_ref, dhid_ref, dpre_ref = out
+        left_ref, dpre_ref = out
         dpre = dpre_ref[...]
         sums = jnp.dot(left_ref[...], dpre, preferred_element_type=jnp.float32)
         w_in_acc[...] += sums[0:n_ch]
         hw_acc[pl.ds(pl.multiple_of(2 * RUNS * b, 2 * RUNS), 2 * RUNS), :] = sums[n_ch:]
-        dfeat_ref[...] = jnp.dot(dpre, w_in_t_ref[...], preferred_element_type=jnp.float32)
         runs = read_runs(ids_ref, RUNS * b, RUNS)
-        for j in range(RUNS):
-            d = run_slices(dfeat_ref, j)
-            add_zh(d, runs[j][0], zh_accs)
-            add_wz(d, runs[j][1], wz_accs)
+        for g in range(groups):
+            dfeat = jnp.dot(dpre_ref[g * 128:(g + 1) * 128, :], w_in_t_ref[...], preferred_element_type=jnp.float32)
+            for par in range(GROUP):
+                d = [dfeat[p * 64 + par * ZC:p * 64 + (par + 1) * ZC] for p in range(2)]
+                row, col = runs[GROUP * g + par]
+                add_zh(d, row, zh_accs)
+                add_wz(d, col, wz_accs)
 
     n_batch = slots // RUNS
     front(0, bufs[0])
@@ -399,7 +404,7 @@
     lax.fori_loop(count // 8 * 8, count, place, 0)
 
 
-def finish_kernel(meta_ref, zh0_ref, zh1_ref, w_mine_ref, w_other_ref,
+def finish_kernel(meta_ref, zh_ref, w_mine_ref, w_other_ref,
                   zh_out, w_in_out, b_in_out, w_out_out, b_out_out, w_all, *, rows_blk):
     mid = w_all.shape[0] // 2
     mine = meta_ref[8] * mid
@@ -412,10 +417,10 @@
     b_out_out[...] = w_all[n_ch + 1:n_ch + 2, 0:b_out_out.shape[1]]
     w_out_out[...] = w_all[n_ch + 8:n_ch + 8 + w_out_out.shape[0], :]
     swapped = meta_ref[6]
-    for n, ref in ((0, zh0_ref), (1, zh1_ref)):
+    for n in range(2):
         base = jnp.bitwise_xor(swapped, n) * 8
         for z in range(8):
-            zh_out[base + z] = ref[pl.ds(z, rows_blk, stride=8), :]
+            zh_out[base + z] = zh_ref[n, pl.ds(z, rows_blk, stride=8), :]
 
 
 def local(n_ha, n_wa, hw_plane, zh_plane, wz_plane, w_in, b_in, w_out, b_out,
@@ -455,14 +460,14 @@
     meta = jnp.stack([y, count] + wz_pos + rest).astype(jnp.int32)
     swap_y = [(i, (i + n_q) % n_ha) for i in range(n_ha)]
 
-    pack_rows = (n_hw + 16 + n_zh + n_lab, n_zh + n_lab)
+    n_rows, n_plane = n_hw + 16, n_zh + n_lab
     planes = (hw_plane.reshape(rows_blk * cols_blk, channels),
               zh_plane.reshape(depth_z * rows_blk, channels), labels[0], run_index)
-    raw = [pltpu.VMEM((rows_blk * cols_blk, channels), bf16), pltpu.VMEM((depth_z * rows_blk, channels), bf16),
-           pltpu.VMEM((slots, 2 * depth_z), jnp.int32), pltpu.VMEM((1, slots), jnp.int32),
-           pltpu.SMEM((1, slots), jnp.int32), pltpu.SemaphoreType.DMA((5,)),
-           pltpu.VMEM((rows_blk * cols_blk, channels), f32), pltpu.VMEM((n_hw, channels), f32),
-           pltpu.VMEM((depth_z * rows_blk, channels), f32), pltpu.VMEM((2 * slots, 2 * depth_z), f32)]
+    hw_raw = pltpu.VMEM((rows_blk * cols_blk, channels), bf16)
+    plane_raw = [pltpu.VMEM((depth_z * rows_blk, channels), bf16), pltpu.VMEM((slots, 2 * depth_z), jnp.int32)]
+    ids_raw = [pltpu.VMEM((1, slots), jnp.int32), pltpu.SMEM((1, slots), jnp.int32)]
+    hw_wide = [pltpu.VMEM((rows_blk * cols_blk, channels), f32), pltpu.VMEM((n_hw, channels), f32)]
+    plane_wide = [pltpu.VMEM((depth_z * rows_blk, channels), f32), pltpu.VMEM((2 * slots, 2 * depth_z), f32)]
 
     def call(kernel, name, operands, specs, outs, scratch, flops, limit=16):
         return pl.pallas_call(
@@ -477,18 +482,24 @@
         )(*operands)
 
     sizes = dict(depth_z=depth_z, rows_blk=rows_blk, slots=slots, pair_cols=pair_cols)
-    send0, = call(functools.partial(pack_send_kernel, **sizes), "pack_send", (meta,) + planes,
-                  [smem] + [hbm] * 4, [((pack_rows[0], channels), bf16)], raw, 3 * 10**9, 60)
+    send0, = call(functools.partial(pack_plane_kernel, **sizes), "pack_plane", (meta, planes[1], planes[2]),
+                  [smem] + [hbm] * 2, [((n_plane, channels), bf16)],
+                  plane_raw + [pltpu.SemaphoreType.DMA((2,))] + plane_wide, 2 * 10**9, 60)
     recv0 = lax.ppermute(send0, "ha", swap_y)
-    later = lax.optimization_barrier((send0, w_in, b_in, w_out, b_out) + planes)
+    send0, hw_late, ids_late = lax.optimization_barrier((send0, planes[0], planes[3]))
+    send_hw, = call(functools.partial(pack_rows_kernel, **sizes), "pack_rows", (meta, hw_late, ids_late),
+                    [smem] + [hbm] * 2, [((n_rows, channels), bf16)],
+                    [hw_raw] + ids_raw + [pltpu.SemaphoreType.DMA((3,))] + hw_wide, 3 * 10**9, 12)
+    recv_hw = lax.ppermute(send_hw, "ha", swap_y)
+    later = lax.optimization_barrier((send_hw, w_in, b_in, w_out, b_out) + planes)
     w_in, b_in, w_out, b_out = later[1:5]
-    own0, own1, send1, wzf0, wzf1 = call(
+    own_hw, own0, own1, send1, wzf0, wzf1 = call(
         functools.partial(pack_own_kernel, **sizes), "pack_own", (meta,) + later[5:] + (wz_plane,),
         [smem] + [hbm] * 5,
-        [((pack_rows[0], channels), bf16), ((pack_rows[1], channels), bf16), ((pack_rows[1], channels), bf16),
-         ((cols_blk, ZC, channels), f32), ((cols_blk, ZC, channels), f32)],
-        raw + [pltpu.VMEM((cols_blk, half, channels), bf16), pltpu.SemaphoreType.DMA], 3 * 10**9)
-    send1, recv0 = lax.optimization_barrier((send1, recv0))
+        [((n_rows, channels), bf16)] + [((n_plane, channels), bf16)] * 3 + [((cols_blk, ZC, channels), f32)] * 2,
+        [hw_raw] + plane_raw + ids_raw + [pltpu.SemaphoreType.DMA((5,))] + hw_wide + plane_wide
+        + [pltpu.VMEM((cols_blk, half, channels), bf16), pltpu.SemaphoreType.DMA], 3 * 10**9, 16)
+    send1, recv0, recv_hw = lax.optimization_barrier((send1, recv0, recv_hw))
     recv1 = lax.ppermute(send1, "ha", swap_y)
 
     w_in_half = (w_in.astype(f32) * 0.5).astype(bf16)
@@ -504,14 +515,13 @@
     wgt_rows = channels + 8 + CLS_ROWS
     mid = wgt_rows // 2
     buf = [pltpu.VMEM((ROWS, channels), bf16), pltpu.VMEM((ROWS, hidden), bf16),
-           pltpu.VMEM((ROWS, hidden), f32), pltpu.VMEM((CLS_ROWS, ROWS), f32), pltpu.VMEM((ROWS, hidden), f32)]
-    out_buf = [pltpu.VMEM((channels + 2 * RUNS, ROWS), bf16), pltpu.VMEM((ROWS, hidden), f32),
-               pltpu.VMEM((ROWS, hidden), bf16)]
+           pltpu.VMEM((ROWS, hidden), f32), pltpu.VMEM((CLS_ROWS, ROWS), f32)]
+    out_buf = [pltpu.VMEM((channels + 2 * RUNS, ROWS), bf16), pltpu.VMEM((ROWS, hidden), bf16)]
     work = [pltpu.VMEM((n_hw, channels), f32), pltpu.VMEM((2 * rows_blk, ZC, channels), f32),
             pltpu.VMEM((n_lab, 128), f32), pltpu.VMEM((n_hw, hidden), f32),
             pltpu.VMEM((channels, hidden), f32), pltpu.VMEM((CLS_PAD, hidden), f32),
             pltpu.VMEM((CLS_ROWS, 128), f32), pltpu.SMEM((8, 128), jnp.int32), pltpu.SemaphoreType.DMA]
-    work += buf + buf + out_buf + out_buf + [pltpu.VMEM((ROWS, channels), f32)]
+    work += buf + buf + out_buf + out_buf
     work += [pltpu.VMEM((cols_blk, 8, channels), f32)] * 2 + [pltpu.VMEM((2 * rows_blk, 8, channels), f32)] * 2
     work += [pltpu.VMEM((8, 128), jnp.int32), pltpu.VMEM((wgt_rows, hidden), f32)]
     sums = [((cols_blk, 8, channels), f32)] * 2 + [((2 * rows_blk, 8, channels), f32)] * 2
@@ -523,10 +533,10 @@
             [smem] + [vmem] * (len(sources) + 8), outs, work, 22 * 10**9, 28)
 
     wz0a, wz0b, zh0a, zh0b, hw0, wgt0 = decode(
-        0, (own0, recv0), sums + [((n_hw, channels), f32), ((wgt_rows, hidden), f32)])
+        0, (own_hw, recv_hw, own0, recv0), sums + [((n_hw, channels), f32), ((wgt_rows, hidden), f32)])
     recv1, wz0a, wz0b, zh0a, zh0b = lax.optimization_barrier((recv1, wz0a, wz0b, zh0a, zh0b))
     wz1a, core_send, zh1a, zh1b, hw1, w_keep = decode(
-        1, (own0, recv0, own1, recv1, hw0, wgt0),
+        1, (own_hw, recv_hw, own1, recv1, hw0, wgt0),
         [sums[0], ((cols_blk + mid // 4, 8, channels), f32), sums[2], sums[3],
          ((n_hw, channels), f32), ((mid // 4, 8, channels), f32)])
 
@@ -554,45 +564,40 @@
         zh0a, zh0b = flat(zh0a), flat(zh0b)
         zh1a, zh1b = flat(zh1a), flat(zh1b)
         wz0r = ppermute_xor(wz0b, "ha", n_ha, 1)
-        zh0 = encode(jnp.concatenate([zh0a, zh0b]).reshape(4, n_part, channels))
-        zh0r = []
-        for k0 in range(2):
-            for k1 in range(2):
-                owners = []
-                for a in range(n_ha):
-                    for b in range(n_wa):
-                        dest_a = ((b // 2) ^ k1) * n_q + a % n_q
-                        dest_b = (a // n_q) * 2 + ((b % 2) ^ k0)
-                        owners.append((a * n_wa + b, dest_a * n_wa + dest_b))
-                zh0r.append(lax.ppermute(zh0[2 * k0 + k1], ("ha", "wa"), owners))
+        zh0r = ppermute_xor(zh0b, "wa", n_wa, 1)
+        stays = y == b1
         wz0r, zh0r, wz1a, core_send, zh1a, zh1b, hw1, w_keep = barrier(
             (wz0r, zh0r, wz1a, core_send, zh1a, zh1b, hw1, w_keep))
+        def corner(value, ha_mask, wa_mask):
+            pairs = [(a * n_wa + b, (a ^ ha_mask) * n_wa + (b ^ wa_mask)) for a in range(n_ha) for b in range(n_wa)]
+            return lax.ppermute(value, ("ha", "wa"), pairs)
+
         zh1r = ppermute_xor(encode(zh1b[None]), "wa", n_wa, 1)
         core_recv = ppermute_xor(core_send, "ha", n_ha, 1)
         hw_recv = lax.ppermute(encode(hw1[None]), "ha", swap_y)
         near0 = wz0a + wz0r
-        zh_first = sum(decode_half(part[None])[0] for part in zh0r)
+        near1 = wz1a + core_recv[:cols_blk]
+        outer = (my_q == 0) | (my_q == 3)
+        far = ppermute_xor(encode(jnp.where(outer, near1, near0).reshape(1, cols_blk * 8, channels)), "ha", n_ha, 2)
+        part0 = zh0a + zh0r
         w = w_keep + core_recv[cols_blk:]
         wr = ppermute_xor(w, "wa", n_wa, 2)
-        zh1r, wr = barrier((zh1r, wr))
-        near1 = wz1a + core_recv[:cols_blk]
-        part1 = zh1a + decode_half(zh1r)[0]
-        zhf = ppermute_xor(encode(part1[None, n_part:]), "wa", n_wa, 2)
-        outer = (my_q == 0) | (my_q == 3)
-        far = ppermute_xor(encode(jnp.where(outer, near1, near0).reshape(1, cols_blk * 8, channels)), "ha", n_ha, 2)
+        zh1r, wr, hw_recv = barrier((zh1r, wr, hw_recv))
+        both = jnp.stack([part0, zh1a + decode_half(zh1r)[0]])
+        zhf = ppermute_xor(encode(both[:, n_part:]), "wa", n_wa, 2)
         w = w + wr
-        w = w + ppermute_xor(w, "ha", n_ha, n_q)
-        wr = ppermute_xor(w, "ha", n_ha, 2)
-        zhf, wr, hw_recv = barrier((zhf, wr, hw_recv))
-        zhm = lax.ppermute(encode(part1[None, :n_part] + decode_half(zhf)), ("ha", "wa"), moves)
-        w = w + wr
-        w = w + ppermute_xor(w, "wa", n_wa, 1)
-        w_other = ppermute_xor(w, "ha", n_ha, 1)
+        wr = [ppermute_xor(w, "ha", n_ha, mask) for mask in (n_q, 2, n_q + 2)]
+        zhf, wr, far, hw_recv = barrier((zhf, wr, far, hw_recv))
+        zh_code = encode(both[:, :n_part] + decode_half(zhf))
+        zhm = jnp.where(stays, zh_code, corner(zh_code, n_q, 2))
+        w = (w + wr[0]) + (wr[1] + wr[2])
+        w_mine = w + ppermute_xor(w, "wa", n_wa, 1)
+        w_other = ppermute_xor(w, "ha", n_ha, 1) + corner(w, 1, 1)
         hw_grad = place(hw1, decode_half(hw_recv)[0])
         wz_grad = jnp.where(outer, near0, near1) + decode_half(far).reshape(near1.shape)
         zh_grad, w_in_grad, b_in_grad, w_out_grad, b_out_grad = call(
-            functools.partial(finish_kernel, rows_blk=rows_blk), "finish", (meta, zh_first, decode_half(zhm)[0], w, w_other),
-            [smem] + [vmem] * 4,
+            functools.partial(finish_kernel, rows_blk=rows_blk), "finish", (meta, decode_half(zhm), w_mine, w_other),
+            [smem] + [vmem] * 3,
             [((2 * 8, rows_blk, channels), f32), ((channels, hidden), f32), ((1, hidden), f32),
              ((classes, hidden), f32), ((1, classes), f32)], [pltpu.VMEM((wgt_rows, hidden), f32)], 10**9, 4)
         return hw_grad, zh_grad, wz_grad, w_in_grad, b_in_grad[0], w_out_grad.T, b_out_grad[0]

time: 101 us -> 98.4 us (0.974)
  the two profiles are of different devices: /device:TPU:7 before, /device:TPU:0 now
where the time goes in v2:
time: 98.4 us; the launch traced here: 98 us
  Pallas kernels  51.1 us (52%)
  starting transfers between devices  22.2 us (23%)
  waiting for transfers between devices  9.91 us (10%)
  local copies, waits for them, and re-layouts  7.85 us (8%)
  other arithmetic  4.95 us (5%)
  between operations  1.95 us (2%)
    pallas_call x7, Pallas kernels, call(): pl.pallas_call(kernel, out_shape=[jax.ShapeDtypeStruct(shape, kind) for s...  51.1 us
    ppermute x12, starting transfers between devices, ppermute_xor(): return lax.ppermute(value, axis, [(i, i ^ mask) for i in range(size)])  14.4 us
    unnamed x40, local copies, waits for them, and re-layouts  6.16 us
    ppermute x12, waiting for transfers between devices, ppermute_xor(): return lax.ppermute(value, axis, [(i, i ^ mask) for i in range(size)])  4.39 us
    ppermute x2, waiting for transfers between devices, corner(): return lax.ppermute(value, ('ha', 'wa'), pairs)  3.63 us
    ppermute x1, starting transfers between devices, local(): recv0 = lax.ppermute(send0, 'ha', swap_y)  3.03 us
    ppermute x2, starting transfers between devices, corner(): return lax.ppermute(value, ('ha', 'wa'), pairs)  2.22 us
    ppermute x1, starting transfers between devices, local(): recv1 = lax.ppermute(send1, 'ha', swap_y)  1.98 us
  transfers between devices with their start and end apart: 18, of which 7 were waited for; matrix products, arithmetic and copies ran while one was open for 5% of the time, Pallas kernels for 48%

profile of v2, /device:TPU:0, one launch (start us, length us, event | category | flops | bytes accessed | tf_op | source)
XLA Modules:
  0.0 98.0 jit_solution(15700340663433983187)
XLA Ops:
  2.0 2.9 %pack_plane.1 = bf16[640,128]{1,0:T(8,128)(2,1)} custom-call(s32[10]{0:T(128)} %stack.48.meta_ref.refs_0_, bf16[2048,128]{1,0:T(8,128)(2,1)} %bitcast.73, s32[512,128]{1,0:T(8,128)} %bitcast.75), custom_call_target="tpu_custom_call" | custom-call | flops 2000000000 | bytes 1048576 | tf_op jit(solution)/shard_map/pack_plane/pallas_call | solution.py:473
  4.9 3.0 %collective-permute-start = (bf16[640,128]{1,0:T(8,128)(2,1)}, bf16[640,128]{1,0:T(8,128)(2,1)S(1)}, u32[]{:S(2)}, u32[]{:S(2)}) collective-permute-start(bf16[640,128]{1,0:T(8,128)(2,1)} %pack_plane.1), channel_id=1, source_target_pairs={{0,16},{4,20},{8,24},{12,28},{16,0},{20,4},{24,8},{28,12},{1,17},{... | collective-permute-start | bytes 491528 | tf_op jit(solution)/shard_map/ppermute | solution.py:488
  8.0 2.7 %pack_rows.1 = bf16[1040,128]{1,0:T(8,128)(2,1)S(1)} custom-call(s32[10]{0:T(128)S(1)} %copy-done, bf16[4096,128]{1,0:T(8,128)(2,1)S(1)} %bitcast.71, s32[1,512]{1,0:T(1,128)S(1)} %copy-done.5), custom_call_target="tpu_custom_call" | custom-call | flops 3000000000 | bytes 1048576 | tf_op jit(solution)/shard_map/pack_rows/pallas_call | solution.py:473
  10.9 3.5 %pack_own.1 = (bf16[1040,128]{1,0:T(8,128)(2,1)S(1)}, bf16[640,128]{1,0:T(8,128)(2,1)S(1)}, bf16[640,128]{1,0:T(8,128)(2,1)S(1)}, bf16[640,128]{1,0:T(8,128)(2,1...) custom-call(s32[10]{0:T(128)S(1)} %copy-done, bf16[4096,128]{1,0:T(8,128)(2,1)S(1)} %bitcast.72, ...), custom_call_target="tpu_custom_call" | custom-call | flops 3000000000 | bytes 1048576 | tf_op jit(solution)/shard_map/pack_own/pallas_call | solution.py:473
  18.6 2.0 %collective-permute-start.2 = (bf16[640,128]{1,0:T(8,128)(2,1)S(1)}, bf16[640,128]{1,0:T(8,128)(2,1)S(1)}, u32[]{:S(2)}, u32[]{:S(2)}) collective-permute-start(bf16[640,128]{1,0:T(8,128)(2,1)S(1)} %get-tuple-element.72), channel_id=1, source_target_pairs={{0,16},{4,20},{8,24},{12,28},{16,0},{20,4},{24,8},{28,12},{1,17},{... | collective-permute-start | bytes 491528 | tf_op jit(solution)/shard_map/ppermute | solution.py:503
  20.6 1.2 %copy-done.7 = f32[128,16,128]{2,1,0:T(8,128)S(1)} copy-done((f32[128,16,128]{2,1,0:T(8,128)S(1)}, f32[128,16,128]{2,1,0:T(8,128)}, u32[]{:S(2)}) %copy-start.7) | copy-done | bytes 1048600
  23.7 18.7 %decode0.1 = (f32[128,8,128]{2,1,0:T(8,128)S(1)}, f32[128,8,128]{2,1,0:T(8,128)S(1)}, f32[64,8,128]{2,1,0:T(8,128)S(1)}, f32[64,8,128]{2,1,0:T(8,128)S(1)}, f32[...) custom-call(s32[10]{0:T(128)S(1)} %copy-done, bf16[1040,128]{1,0:T(8,128)(2,1)S(1)} %copy-done.9, ...), custom_call_target="tpu_custom_call" | custom-call | flops 22000001024 | bytes 1048576 | tf_op jit(solution)/shard_map/decode0/pallas_call | solution.py:473
  42.4 1.6 %collective-permute-start.4 = (f32[512,128]{1,0:T(8,128)S(1)}, f32[512,128]{1,0:T(8,128)S(1)}, u32[]{:S(2)}, u32[]{:S(2)}) collective-permute-start(f32[512,128]{1,0:T(8,128)S(1)} %bitcast.77), channel_id=1, source_target_pairs={{0,1},{1,0},{2,3},{3,2},{4,5},{5,4},{6,7},{7,6},{8,9},{9,8},{10,11... | collective-permute-start | bytes 786440 | tf_op jit(solution)/shard_map/ppermute | solution.py:25
  44.0 18.9 %decode1.1 = (f32[128,8,128]{2,1,0:T(8,128)S(1)}, f32[148,8,128]{2,1,0:T(8,128)S(1)}, f32[64,8,128]{2,1,0:T(8,128)S(1)}, f32[64,8,128]{2,1,0:T(8,128)S(1)}, f32[...) custom-call(s32[10]{0:T(128)S(1)} %copy-done, bf16[1040,128]{1,0:T(8,128)(2,1)S(1)} %copy-done.9, ...), custom_call_target="tpu_custom_call" | custom-call | flops 22000001024 | bytes 1048576 | tf_op jit(solution)/shard_map/decode1/pallas_call | solution.py:473
  64.6 1.1 %collective-permute-done.6 = f32[148,8,128]{2,1,0:T(8,128)S(1)} collective-permute-done((f32[148,8,128]{2,1,0:T(8,128)S(1)}, f32[148,8,128]{2,1,0:T(8,128)S(1)}, u32[]{:S(2)}, u32[]{:S(2)}) %collective-permute-start.6) | collective-permute-done | bytes 606240 | tf_op jit(solution)/shard_map/ppermute | solution.py:25
  65.8 2.7 %collective-permute-start.7 = (f32[20,8,128]{2,1,0:T(8,128)S(1)}, f32[20,8,128]{2,1,0:T(8,128)S(1)}, u32[]{:S(2)}, u32[]{:S(2)}) collective-permute-start(f32[20,8,128]{2,1,0:T(8,128)S(1)} %slice_add_fusion.1), channel_id=1, source_target_pairs={{0,2},{1,3},{2,0},{3,1},{4,6},{5,7},{6,4},{7,5},{8,10},{9,11},{10,... | collective-permute-start | bytes 245768 | tf_op jit(solution)/shard_map/ppermute | solution.py:25
  69.5 1.5 %collective-permute-start.13 = (f16[1,1040,128]{2,1,0:T(8,128)(2,1)}, f16[1,1040,128]{2,1,0:T(8,128)(2,1)}, u32[]{:S(2)}, u32[]{:S(2)}) collective-permute-start(f16[1,1040,128]{2,1,0:T(8,128)(2,1)} %pad_maximum_fusion.1), channel_id=1, source_target_pairs={{0,8},{4,12},{8,0},{12,4},{16,24},{20,28},{24,16},{28,20},{1,9},{5... | collective-permute-start | bytes 798728 | tf_op jit(solution)/shard_map/ppermute | solution.py:25
  71.0 1.8 %collective-permute-done.8 = f16[1,1040,128]{2,1,0:T(8,128)(2,1)S(1)} collective-permute-done((f16[1,1040,128]{2,1,0:T(8,128)(2,1)S(1)}, f16[1,1040,128]{2,1,0:T(8,128)(2,1)S(1)}, u32[]{:S(2)}, u32[]{:S(2)}) %collective-permute-start.8) | collective-permute-done | bytes 266272 | tf_op jit(solution)/shard_map/ppermute | solution.py:577
  73.0 2.7 %collective-permute-start.9 = (f16[2,272,128]{2,1,0:T(8,128)(2,1)S(1)}, f16[2,272,128]{2,1,0:T(8,128)(2,1)S(1)}, u32[]{:S(2)}, u32[]{:S(2)}) collective-permute-start(f16[2,272,128]{2,1,0:T(8,128)(2,1)S(1)} %pad_maximum_fusion.3), channel_id=1, source_target_pairs={{0,2},{1,3},{2,0},{3,1},{4,6},{5,7},{6,4},{7,5},{8,10},{9,11},{10,... | collective-permute-start | bytes 417800 | tf_op jit(solution)/shard_map/ppermute | solution.py:25
  75.7 1.5 %collective-permute-start.12 = (f32[20,8,128]{2,1,0:T(8,128)S(1)}, f32[20,8,128]{2,1,0:T(8,128)}, u32[]{:S(2)}, u32[]{:S(2)}) collective-permute-start(f32[20,8,128]{2,1,0:T(8,128)S(1)} %add.138), channel_id=1, source_target_pairs={{0,24},{4,28},{8,16},{12,20},{16,8},{20,12},{24,0},{28,4},{1,25},{... | collective-permute-start | bytes 245768 | tf_op jit(solution)/shard_map/ppermute | solution.py:25
  77.7 1.5 %collective-permute-start.10 = (f32[20,8,128]{2,1,0:T(8,128)S(1)}, f32[20,8,128]{2,1,0:T(8,128)}, u32[]{:S(2)}, u32[]{:S(2)}) collective-permute-start(f32[20,8,128]{2,1,0:T(8,128)S(1)} %add.138), channel_id=1, source_target_pairs={{0,16},{4,20},{8,24},{12,28},{16,0},{20,4},{24,8},{28,12},{1,17},{... | collective-permute-start | bytes 245768 | tf_op jit(solution)/shard_map/ppermute | solution.py:25
  79.3 2.4 %collective-permute-done.12 = f32[20,8,128]{2,1,0:T(8,128)} collective-permute-done((f32[20,8,128]{2,1,0:T(8,128)S(1)}, f32[20,8,128]{2,1,0:T(8,128)}, u32[]{:S(2)}, u32[]{:S(2)}) %collective-permute-start.12) | collective-permute-done | bytes 81952 | tf_op jit(solution)/shard_map/ppermute | solution.py:25
  82.5 1.0 %add_add_fusion = f32[20,8,128]{2,1,0:T(8,128)S(1)} fusion(f32[20,8,128]{2,1,0:T(8,128)} %collective-permute-done.11, f32[20,8,128]{2,1,0:T(8,128)} %collective-permute-done.12, f32[20,8,128]{2,1,0:T(8,128)S(1)} %add.138, f32[20,8,128]{2,1,0:T(8,128)} %collective-permute-done.10), kind=kLoop, calls=%fused_computation.44 | loop fusion | flops 61440 | bytes 409600 | tf_op jit(solution)/shard_map/add | solution.py:593
  84.0 1.6 %collective-permute-start.16 = (f32[20,8,128]{2,1,0:T(8,128)S(1)}, f32[20,8,128]{2,1,0:T(8,128)S(1)}, u32[]{:S(2)}, u32[]{:S(2)}) collective-permute-start(f32[20,8,128]{2,1,0:T(8,128)S(1)} %add_add_fusion), channel_id=1, source_target_pairs={{0,4},{4,0},{8,12},{12,8},{16,20},{20,16},{24,28},{28,24},{1,5},{5... | collective-permute-start | bytes 245768 | tf_op jit(solution)/shard_map/ppermute | solution.py:25
  86.0 1.7 %collective-permute-start.14 = (f16[2,272,128]{2,1,0:T(8,128)(2,1)S(1)}, f16[2,272,128]{2,1,0:T(8,128)(2,1)S(1)}, u32[]{:S(2)}, u32[]{:S(2)}) collective-permute-start(f16[2,272,128]{2,1,0:T(8,128)(2,1)S(1)} %pad_maximum_fusion.4), channel_id=1, source_target_pairs={{0,18},{1,19},{2,16},{3,17},{4,22},{5,23},{6,20},{7,21},{8,26},{9,... | collective-permute-start | bytes 417800 | tf_op jit(solution)/shard_map/ppermute | solution.py:573
  87.7 1.0 %convert_element_type.73 = f32[1,1040,128]{2,1,0:T(8,128)S(1)} convert(f16[1,1040,128]{2,1,0:T(8,128)(2,1)} %collective-permute-done.13) | non-fusion elementwise | flops 133120 | bytes 798720 | tf_op jit(solution)/shard_map/convert_element_type | solution.py:183
  89.7 3.1 %place.1 = f32[4096,128]{1,0:T(8,128)} custom-call(s32[10]{0:T(128)S(1)} %copy-done, s32[1,512]{1,0:T(1,128)S(1)} %copy-done.5, f32[1024,128]{1,0:T(8,128)S(1)} %get-tuple-element.99.mine_ref, f32[1024,128]{1,0:T(8,128)S(1)} %fusion.2.recv_ref), custom_call_target="tpu_custom_call" | custom-call | flops 3000000000 | bytes 1048576 | tf_op jit(solution)/shard_map/place/pallas_call | solution.py:473
  92.9 3.6 %collective-permute-done.14 = f16[2,272,128]{2,1,0:T(8,128)(2,1)S(1)} collective-permute-done((f16[2,272,128]{2,1,0:T(8,128)(2,1)S(1)}, f16[2,272,128]{2,1,0:T(8,128)(2,1)S(1)}, u32[]{:S(2)}, u32[]{:S(2)}) %collective-permute-start.14) | collective-permute-done | bytes 139296 | tf_op jit(solution)/shard_map/ppermute | solution.py:573
  96.6 1.3 %finish.1 = (f32[16,32,128]{2,1,0:T(8,128)}, f32[128,256]{1,0:T(8,128)}, f32[1,256]{1,0:T(1,128)}, f32[18,256]{1,0:T(8,128)}, f32[1,18]{1,0:T(1,128)}) custom-call(s32[10]{0:T(128)S(1)} %copy-done, f32[2,256,128]{2,1,0:T(8,128)S(1)} %slice_multiply_fusion.2.zh_ref, f32[20,8,128]{2,1,0:T(8,128)S(1)} %add.145.w_mine_ref, f32[20,8,128]{2,1,0:T(8,128)S(1)} %add.146.w_other_ref), custom_call_target="tpu_custom_call" | custom-call | flops 1000000000 | bytes 1048576 | tf_op jit(solution)/shard_map/finish/pallas_call | solution.py:473
  (120 shorter events, 13.1 us)
Async XLA Ops:
  2.0 5.9 %copy-start.2 = (bf16[32,128,128]{2,1,0:T(8,128)(2,1)S(1)}, bf16[32,128,128]{2,1,0:T(8,128)(2,1)}, u32[]{:S(2)}) copy-start(bf16[32,128,128]{2,1,0:T(8,128)(2,1)} %param.10) | copy-start | bytes 3145732
  2.0 5.9 %copy-start.5 = (s32[1,512]{1,0:T(1,128)S(1)}, s32[1,512]{1,0:T(1,128)}, u32[]{:S(2)}) copy-start(s32[1,512]{1,0:T(1,128)} %rid_ref.1) | copy-start | bytes 6148
  4.9 13.6 %collective-permute-start = (bf16[640,128]{1,0:T(8,128)(2,1)}, bf16[640,128]{1,0:T(8,128)(2,1)S(1)}, u32[]{:S(2)}, u32[]{:S(2)}) collective-permute-start(bf16[640,128]{1,0:T(8,128)(2,1)} %pack_plane.1), channel_id=1, source_target_pairs={{0,16},{4,20},{8,24},{12,28},{16,0},{20,4},{24,8},{28,12},{1,17},{... | collective-permute-start | bytes 491528 | tf_op jit(solution)/shard_map/ppermute | solution.py:488
  10.6 7.9 %collective-permute-start.1 = (bf16[1040,128]{1,0:T(8,128)(2,1)S(1)}, bf16[1040,128]{1,0:T(8,128)(2,1)S(1)}, u32[]{:S(2)}, u32[]{:S(2)}) collective-permute-start(bf16[1040,128]{1,0:T(8,128)(2,1)S(1)} %pack_rows.1), channel_id=1, source_target_pairs={{0,16},{4,20},{8,24},{12,28},{16,0},{20,4},{24,8},{28,12},{1,17},{... | collective-permute-start | bytes 798728 | tf_op jit(solution)/shard_map/ppermute | solution.py:493
  10.9 6.6 %copy-start.17 = (bf16[256,18]{0,1:T(8,128)(2,1)S(1)}, bf16[256,18]{0,1:T(8,128)(2,1)}, u32[]{:S(2)}) copy-start(bf16[256,18]{0,1:T(8,128)(2,1)} %param.15) | copy-start | bytes 27652
  10.9 7.6 %copy-start.19 = (f32[18]{0:T(128)S(1)}, f32[18]{0:T(128)}, u32[]{:S(2)}) copy-start(f32[18]{0:T(128)} %param.16) | copy-start | bytes 220
  10.9 7.6 %copy-start.18 = (f32[256]{0:T(256)S(1)}, f32[256]{0:T(256)}, u32[]{:S(2)}) copy-start(f32[256]{0:T(256)} %param.14) | copy-start | bytes 3076
  18.6 23.8 %collective-permute-start.2 = (bf16[640,128]{1,0:T(8,128)(2,1)S(1)}, bf16[640,128]{1,0:T(8,128)(2,1)S(1)}, u32[]{:S(2)}, u32[]{:S(2)}) collective-permute-start(bf16[640,128]{1,0:T(8,128)(2,1)S(1)} %get-tuple-element.72), channel_id=1, source_target_pairs={{0,16},{4,20},{8,24},{12,28},{16,0},{20,4},{24,8},{28,12},{1,17},{... | collective-permute-start | bytes 491528 | tf_op jit(solution)/shard_map/ppermute | solution.py:503
  23.7 20.3 %copy-start.11 = (bf16[640,128]{1,0:T(8,128)(2,1)S(1)}, bf16[640,128]{1,0:T(8,128)(2,1)}, u32[]{:S(2)}) copy-start(bf16[640,128]{1,0:T(8,128)(2,1)} %copy-done.10) | copy-start | bytes 491524
  42.4 20.5 %collective-permute-start.4 = (f32[512,128]{1,0:T(8,128)S(1)}, f32[512,128]{1,0:T(8,128)S(1)}, u32[]{:S(2)}, u32[]{:S(2)}) collective-permute-start(f32[512,128]{1,0:T(8,128)S(1)} %bitcast.77), channel_id=1, source_target_pairs={{0,1},{1,0},{2,3},{3,2},{4,5},{5,4},{6,7},{7,6},{8,9},{9,8},{10,11... | collective-permute-start | bytes 786440 | tf_op jit(solution)/shard_map/ppermute | solution.py:25
  44.0 18.9 %collective-permute-start.3 = (f32[128,8,128]{2,1,0:T(8,128)S(1)}, f32[128,8,128]{2,1,0:T(8,128)S(1)}, u32[]{:S(2)}, u32[]{:S(2)}) collective-permute-start(f32[128,8,128]{2,1,0:T(8,128)S(1)} %get-tuple-element.86), channel_id=1, source_target_pairs={{0,4},{4,0},{8,12},{12,8},{16,20},{20,16},{24,28},{28,24},{1,5},{5... | collective-permute-start | bytes 1572872 | tf_op jit(solution)/shard_map/ppermute | solution.py:25
  63.2 7.7 %collective-permute-start.5 = (f16[1,528,128]{2,1,0:T(8,128)(2,1)S(1)}, f16[1,528,128]{2,1,0:T(8,128)(2,1)S(1)}, u32[]{:S(2)}, u32[]{:S(2)}) collective-permute-start(f16[1,528,128]{2,1,0:T(8,128)(2,1)S(1)} %pad_maximum_fusion.5), channel_id=1, source_target_pairs={{0,1},{1,0},{2,3},{3,2},{4,5},{5,4},{6,7},{7,6},{8,9},{9,8},{10,11... | collective-permute-start | bytes 405512 | tf_op jit(solution)/shard_map/ppermute | solution.py:25
  63.7 2.0 %collective-permute-start.6 = (f32[148,8,128]{2,1,0:T(8,128)S(1)}, f32[148,8,128]{2,1,0:T(8,128)S(1)}, u32[]{:S(2)}, u32[]{:S(2)}) collective-permute-start(f32[148,8,128]{2,1,0:T(8,128)S(1)} %get-tuple-element.105), channel_id=1, source_target_pairs={{0,4},{4,0},{8,12},{12,8},{16,20},{20,16},{24,28},{28,24},{1,5},{5... | collective-permute-start | bytes 1818632 | tf_op jit(solution)/shard_map/ppermute | solution.py:25
  64.1 8.6 %collective-permute-start.8 = (f16[1,1040,128]{2,1,0:T(8,128)(2,1)S(1)}, f16[1,1040,128]{2,1,0:T(8,128)(2,1)S(1)}, u32[]{:S(2)}, u32[]{:S(2)}) collective-permute-start(f16[1,1040,128]{2,1,0:T(8,128)(2,1)S(1)} %pad_maximum_fusion), channel_id=1, source_target_pairs={{0,16},{4,20},{8,24},{12,28},{16,0},{20,4},{24,8},{28,12},{1,17},{... | collective-permute-start | bytes 798728 | tf_op jit(solution)/shard_map/ppermute | solution.py:577
  65.8 7.0 %collective-permute-start.7 = (f32[20,8,128]{2,1,0:T(8,128)S(1)}, f32[20,8,128]{2,1,0:T(8,128)S(1)}, u32[]{:S(2)}, u32[]{:S(2)}) collective-permute-start(f32[20,8,128]{2,1,0:T(8,128)S(1)} %slice_add_fusion.1), channel_id=1, source_target_pairs={{0,2},{1,3},{2,0},{3,1},{4,6},{5,7},{6,4},{7,5},{8,10},{9,11},{10,... | collective-permute-start | bytes 245768 | tf_op jit(solution)/shard_map/ppermute | solution.py:25
  69.5 13.0 %collective-permute-start.13 = (f16[1,1040,128]{2,1,0:T(8,128)(2,1)}, f16[1,1040,128]{2,1,0:T(8,128)(2,1)}, u32[]{:S(2)}, u32[]{:S(2)}) collective-permute-start(f16[1,1040,128]{2,1,0:T(8,128)(2,1)} %pad_maximum_fusion.1), channel_id=1, source_target_pairs={{0,8},{4,12},{8,0},{12,4},{16,24},{20,28},{24,16},{28,20},{1,9},{5... | collective-permute-start | bytes 798728 | tf_op jit(solution)/shard_map/ppermute | solution.py:25
  73.0 9.5 %collective-permute-start.9 = (f16[2,272,128]{2,1,0:T(8,128)(2,1)S(1)}, f16[2,272,128]{2,1,0:T(8,128)(2,1)S(1)}, u32[]{:S(2)}, u32[]{:S(2)}) collective-permute-start(f16[2,272,128]{2,1,0:T(8,128)(2,1)S(1)} %pad_maximum_fusion.3), channel_id=1, source_target_pairs={{0,2},{1,3},{2,0},{3,1},{4,6},{5,7},{6,4},{7,5},{8,10},{9,11},{10,... | collective-permute-start | bytes 417800 | tf_op jit(solution)/shard_map/ppermute | solution.py:25
  75.7 5.9 %collective-permute-start.12 = (f32[20,8,128]{2,1,0:T(8,128)S(1)}, f32[20,8,128]{2,1,0:T(8,128)}, u32[]{:S(2)}, u32[]{:S(2)}) collective-permute-start(f32[20,8,128]{2,1,0:T(8,128)S(1)} %add.138), channel_id=1, source_target_pairs={{0,24},{4,28},{8,16},{12,20},{16,8},{20,12},{24,0},{28,4},{1,25},{... | collective-permute-start | bytes 245768 | tf_op jit(solution)/shard_map/ppermute | solution.py:25
  77.2 4.5 %collective-permute-start.11 = (f32[20,8,128]{2,1,0:T(8,128)S(1)}, f32[20,8,128]{2,1,0:T(8,128)}, u32[]{:S(2)}, u32[]{:S(2)}) collective-permute-start(f32[20,8,128]{2,1,0:T(8,128)S(1)} %add.138), channel_id=1, source_target_pairs={{0,8},{4,12},{8,0},{12,4},{16,24},{20,28},{24,16},{28,20},{1,9},{5... | collective-permute-start | bytes 245768 | tf_op jit(solution)/shard_map/ppermute | solution.py:25
  77.7 4.8 %collective-permute-start.10 = (f32[20,8,128]{2,1,0:T(8,128)S(1)}, f32[20,8,128]{2,1,0:T(8,128)}, u32[]{:S(2)}, u32[]{:S(2)}) collective-permute-start(f32[20,8,128]{2,1,0:T(8,128)S(1)} %add.138), channel_id=1, source_target_pairs={{0,16},{4,20},{8,24},{12,28},{16,0},{20,4},{24,8},{28,12},{1,17},{... | collective-permute-start | bytes 245768 | tf_op jit(solution)/shard_map/ppermute | solution.py:25
  83.5 9.4 %collective-permute-start.17 = (f32[20,8,128]{2,1,0:T(8,128)S(1)}, f32[20,8,128]{2,1,0:T(8,128)S(1)}, u32[]{:S(2)}, u32[]{:S(2)}) collective-permute-start(f32[20,8,128]{2,1,0:T(8,128)S(1)} %add_add_fusion), channel_id=1, source_target_pairs={{0,5},{1,4},{2,7},{3,6},{4,1},{5,0},{6,3},{7,2},{8,13},{9,12},{10,... | collective-permute-start | bytes 245768 | tf_op jit(solution)/shard_map/ppermute | solution.py:573
  84.0 8.9 %collective-permute-start.16 = (f32[20,8,128]{2,1,0:T(8,128)S(1)}, f32[20,8,128]{2,1,0:T(8,128)S(1)}, u32[]{:S(2)}, u32[]{:S(2)}) collective-permute-start(f32[20,8,128]{2,1,0:T(8,128)S(1)} %add_add_fusion), channel_id=1, source_target_pairs={{0,4},{4,0},{8,12},{12,8},{16,20},{20,16},{24,28},{28,24},{1,5},{5... | collective-permute-start | bytes 245768 | tf_op jit(solution)/shard_map/ppermute | solution.py:25
  85.6 7.3 %collective-permute-start.15 = (f32[20,8,128]{2,1,0:T(8,128)S(1)}, f32[20,8,128]{2,1,0:T(8,128)S(1)}, u32[]{:S(2)}, u32[]{:S(2)}) collective-permute-start(f32[20,8,128]{2,1,0:T(8,128)S(1)} %add_add_fusion), channel_id=1, source_target_pairs={{0,1},{1,0},{2,3},{3,2},{4,5},{5,4},{6,7},{7,6},{8,9},{9,8},{10,11... | collective-permute-start | bytes 245768 | tf_op jit(solution)/shard_map/ppermute | solution.py:25
  86.0 10.5 %collective-permute-start.14 = (f16[2,272,128]{2,1,0:T(8,128)(2,1)S(1)}, f16[2,272,128]{2,1,0:T(8,128)(2,1)S(1)}, u32[]{:S(2)}, u32[]{:S(2)}) collective-permute-start(f16[2,272,128]{2,1,0:T(8,128)(2,1)S(1)} %pad_maximum_fusion.4), channel_id=1, source_target_pairs={{0,18},{1,19},{2,16},{3,17},{4,22},{5,23},{6,20},{7,21},{8,26},{9,... | collective-permute-start | bytes 417800 | tf_op jit(solution)/shard_map/ppermute | solution.py:573
  (14 other events, 32.2 us)

commit v3 on v2

--- a/solution.py
+++ b/solution.py
@@ -113,16 +113,36 @@
     put_ids(send_ref, n_hw, jnp.where(lane < lanes, before, here), pair_cols.bit_length() - 1, pair_cols - 1)
 
 
-def pack_own_kernel(meta_ref, hw_ref, zh_ref, lab_ref, ids_ref, wz_ref,
+def prepare_weights(w_in_ref, b_in_ref, w_out_ref, b_out_ref,
+                    w_in_half, w_in_t, b_in_half, w_out_t, w_out_half, b_out_rows, w_wide, b_wide):
+    w_in = w_in_ref[...].astype(jnp.float32)
+    w_in_half[...] = (w_in * 0.5).astype(jnp.bfloat16)
+    w_in_t[...] = jnp.transpose(w_in, (1, 0)).astype(jnp.bfloat16)
+    b_in_half[...] = b_in_ref[...] * 0.5
+    classes = w_out_ref.shape[0]
+    w_wide[...] = jnp.zeros_like(w_wide)
+    w_wide[0:classes, :] = w_out_ref[...].astype(jnp.float32)
+    turned = w_wide[...]
+    w_out_t[...] = turned.astype(jnp.bfloat16)
+    w_out_half[...] = (turned * 0.5).astype(jnp.bfloat16)
+    b_wide[...] = jnp.full_like(b_wide, -1e30)
+    b_wide[0:1, 0:classes] = b_out_ref[...]
+    b_out_rows[...] = jnp.broadcast_to(jnp.transpose(b_wide[...], (1, 0))[0:CLS_ROWS, 0:1], (CLS_ROWS, 128))
+
+
+def pack_own_kernel(meta_ref, hw_ref, zh_ref, lab_ref, ids_ref, wz_ref, w_in_ref, b_in_ref, w_out_ref, b_out_ref,
                     hw_out, own0_ref, own1_ref, send1_ref, wz0_ref, wz1_ref,
+                    w_in_half, w_in_t, b_in_half, w_out_t, w_out_half, b_out_rows,
                     hw_raw, zh_raw, lab_raw, ids_raw, rid_ref, sems,
-                    hw_full, hw_rows, zh_full, lab_pad, wz_raw, wz_sem,
+                    hw_full, hw_rows, zh_full, lab_pad, wz_raw, wz_sem, w_wide, b_wide,
                     *, depth_z, rows_blk, slots, pair_cols):
     half = depth_z // 2
     n_hw = 2 * slots
     z0 = pl.multiple_of(meta_ref[0] * half, half)
     wz_copy = pltpu.make_async_copy(wz_ref.at[:, pl.ds(z0, half), :], wz_raw, wz_sem)
     wz_copy.start()
+    prepare_weights(w_in_ref, b_in_ref, w_out_ref, b_out_ref,
+                    w_in_half, w_in_t, b_in_half, w_out_t, w_out_half, b_out_rows, w_wide, b_wide)
     fetch(((hw_ref, hw_raw), (ids_ref, rid_ref), (ids_ref, ids_raw), (zh_ref, zh_raw), (lab_ref, lab_raw)), sems)
     hw_full[...] = hw_raw[...].astype(jnp.float32)
     widen_planes(zh_raw, lab_raw, zh_full, lab_pad, slots)
@@ -201,8 +221,8 @@
     if not first:
         hw_prev, wgt_prev = refs[:2]
         refs = refs[2:]
-    wz_full, w_in_ref, w_in_t_ref, b_in_ref, w_out_t_ref, w_out_half_ref, b_out_ref, sel_ref = refs[:8]
-    refs = refs[8:]
+    wz_full, w_in_ref, w_in_t_ref, b_in_ref, w_out_t_ref, w_out_half_ref, b_out_ref = refs[:7]
+    refs = refs[7:]
     if first:
         wz_out0, wz_out1, zh_out0, zh_out1, hw_out, wgt_out = refs[:6]
         refs = refs[6:]
@@ -248,8 +268,13 @@
 
     groups = RUNS // GROUP
     n_ch = w_in_ref.shape[0]
+    sel_row = lax.broadcasted_iota(jnp.int32, (2 * RUNS, ROWS), 0)
+    sample = lax.broadcasted_iota(jnp.int32, (2 * RUNS, ROWS), 1)
+    sample_run = lax.shift_right_logical(sample, 7) * GROUP + lax.shift_right_logical(jnp.bitwise_and(sample, 63), 4)
+    sample_row = 2 * sample_run + jnp.bitwise_and(lax.shift_right_logical(sample, 6), 1)
+    select = jnp.where(sel_row == sample_row, 1.0, 0.0).astype(jnp.bfloat16)
     for left_ref, dpre_ref in outs:
-        left_ref[n_ch:, :] = sel_ref[...]
+        left_ref[n_ch:, :] = select
     class_ids = lax.broadcasted_iota(jnp.int32, (CLS_ROWS, 128), 0).astype(jnp.float32)
     nt = (((1,), (1,)), ((), ()))
 
@@ -491,27 +516,21 @@
                     [smem] + [hbm] * 2, [((n_rows, channels), bf16)],
                     [hw_raw] + ids_raw + [pltpu.SemaphoreType.DMA((3,))] + hw_wide, 3 * 10**9, 12)
     recv_hw = lax.ppermute(send_hw, "ha", swap_y)
-    later = lax.optimization_barrier((send_hw, w_in, b_in, w_out, b_out) + planes)
-    w_in, b_in, w_out, b_out = later[1:5]
-    own_hw, own0, own1, send1, wzf0, wzf1 = call(
-        functools.partial(pack_own_kernel, **sizes), "pack_own", (meta,) + later[5:] + (wz_plane,),
-        [smem] + [hbm] * 5,
-        [((n_rows, channels), bf16)] + [((n_plane, channels), bf16)] * 3 + [((cols_blk, ZC, channels), f32)] * 2,
+    later = lax.optimization_barrier((send_hw,) + planes)
+    own_hw, own0, own1, send1, wzf0, wzf1, *shared = call(
+        functools.partial(pack_own_kernel, **sizes), "pack_own",
+        (meta,) + later[1:] + (wz_plane, w_in, b_in.reshape(1, hidden), w_out.T, b_out.reshape(1, classes)),
+        [smem] + [hbm] * 5 + [vmem] * 4,
+        [((n_rows, channels), bf16)] + [((n_plane, channels), bf16)] * 3 + [((cols_blk, ZC, channels), f32)] * 2
+        + [((channels, hidden), bf16), ((hidden, channels), bf16), ((1, hidden), f32), ((CLS_PAD, hidden), bf16),
+           ((CLS_PAD, hidden), bf16), ((CLS_ROWS, 128), f32)],
         [hw_raw] + plane_raw + ids_raw + [pltpu.SemaphoreType.DMA((5,))] + hw_wide + plane_wide
-        + [pltpu.VMEM((cols_blk, half, channels), bf16), pltpu.SemaphoreType.DMA], 3 * 10**9, 16)
+        + [pltpu.VMEM((cols_blk, half, channels), bf16), pltpu.SemaphoreType.DMA,
+           pltpu.VMEM((CLS_PAD, hidden), f32), pltpu.VMEM((8, 128), f32)], 3 * 10**9, 16)
     send1, recv0, recv_hw = lax.optimization_barrier((send1, recv0, recv_hw))
     recv1 = lax.ppermute(send1, "ha", swap_y)
 
-    w_in_half = (w_in.astype(f32) * 0.5).astype(bf16)
-    w_out_half = jnp.pad((w_out.astype(f32) * 0.5).astype(bf16).T, ((0, CLS_PAD - classes), (0, 0)))
-    w_out_t = jnp.pad(w_out.T, ((0, CLS_PAD - classes), (0, 0)))
-    b_out_rows = jnp.broadcast_to(
-        jnp.pad(b_out, (0, CLS_ROWS - classes), constant_values=-1e30)[:, None], (CLS_ROWS, 128))
-    spot = jnp.arange(ROWS)
-    run_of = (spot // 128) * GROUP + (spot % 64) // ZC
-    select = (jnp.arange(2 * RUNS)[:, None] == (2 * run_of + (spot // 64) % 2)[None, :]).astype(bf16)
-    w_in_t = w_in.T
-    shared = (w_in_half, w_in_t, (b_in * 0.5).reshape(1, hidden), w_out_t, w_out_half, b_out_rows, select)
+    shared = tuple(shared)
     wgt_rows = channels + 8 + CLS_ROWS
     mid = wgt_rows // 2
     buf = [pltpu.VMEM((ROWS, channels), bf16), pltpu.VMEM((ROWS, hidden), bf16),
@@ -530,7 +549,7 @@
             functools.partial(decode_kernel, chunk=CHUNKS[n], first=n == 0, rows_blk=rows_blk,
                               slots=slots, pair_cols=pair_cols), "decode%d" % n,
             (meta,) + sources + (wzf0, wzf1)[n:n + 1] + shared,
-            [smem] + [vmem] * (len(sources) + 8), outs, work, 22 * 10**9, 28)
+            [smem] + [vmem] * (len(sources) + 8 - 1), outs, work, 22 * 10**9, 20)
 
     wz0a, wz0b, zh0a, zh0b, hw0, wgt0 = decode(
         0, (own_hw, recv_hw, own0, recv0), sums + [((n_hw, channels), f32), ((wgt_rows, hidden), f32)])

time: 98.4 us -> 94.9 us (0.964)
  local copies, waits for them, and re-layouts: 7.85 us -> 2.37 us
  waiting for transfers between devices: 9.91 us -> 11.9 us
    unnamed x40 -> x24, local copies, waits for them, and re-layouts: 6.16 us -> 1.65 us
    ppermute x1, waiting for transfers between devices: 0.08 us -> 2.51 us  [local(): recv_hw = lax.ppermute(send_hw, 'ha', swap_y)]
  transfers between devices with their start and end apart: 18 -> 18, of which waited for: 7 -> 7; matrix products, arithmetic and copies ran while one was open for 5% -> 4% of each run, Pallas kernels for 48% -> 50%
where the time goes in v3:
time: 94.9 us; the launch traced here: 94.6 us
  Pallas kernels  51.7 us (54%)
  starting transfers between devices  22 us (23%)
  waiting for transfers between devices  11.9 us (13%)
  other arithmetic  4.75 us (5%)
  local copies, waits for them, and re-layouts  2.37 us (2%)
  between operations  1.86 us (2%)
    pallas_call x7, Pallas kernels, call(): pl.pallas_call(kernel, out_shape=[jax.ShapeDtypeStruct(shape, kind) for s...  51.7 us
    ppermute x12, starting transfers between devices, ppermute_xor(): return lax.ppermute(value, axis, [(i, i ^ mask) for i in range(size)])  14.6 us
    ppermute x12, waiting for transfers between devices, ppermute_xor(): return lax.ppermute(value, axis, [(i, i ^ mask) for i in range(size)])  4.09 us
    ppermute x2, waiting for transfers between devices, corner(): return lax.ppermute(value, ('ha', 'wa'), pairs)  3.44 us
    ppermute x1, starting transfers between devices, local(): recv0 = lax.ppermute(send0, 'ha', swap_y)  3.03 us
    ppermute x1, waiting for transfers between devices, local(): recv_hw = lax.ppermute(send_hw, 'ha', swap_y)  2.51 us
    ppermute x2, starting transfers between devices, corner(): return lax.ppermute(value, ('ha', 'wa'), pairs)  2.23 us
  transfers between devices with their start and end apart: 18, of which 7 were waited for; matrix products, arithmetic and copies ran while one was open for 4% of the time, Pallas kernels for 50%

profile of v3, /device:TPU:0, one launch (start us, length us, event | category | flops | bytes accessed | tf_op | source)
XLA Modules:
  0.0 94.6 jit_solution(12861984022780280972)
XLA Ops:
  2.1 2.9 %pack_plane.1 = bf16[640,128]{1,0:T(8,128)(2,1)} custom-call(s32[10]{0:T(128)} %stack.48.meta_ref.refs_0_, bf16[2048,128]{1,0:T(8,128)(2,1)} %bitcast.67, s32[512,128]{1,0:T(8,128)} %bitcast.69), custom_call_target="tpu_custom_call" | custom-call | flops 2000000000 | bytes 1048576 | tf_op jit(solution)/shard_map/pack_plane/pallas_call | solution.py:498
  5.0 3.0 %collective-permute-start = (bf16[640,128]{1,0:T(8,128)(2,1)}, bf16[640,128]{1,0:T(8,128)(2,1)S(1)}, u32[]{:S(2)}, u32[]{:S(2)}) collective-permute-start(bf16[640,128]{1,0:T(8,128)(2,1)} %pack_plane.1), channel_id=1, source_target_pairs={{0,16},{4,20},{8,24},{12,28},{16,0},{20,4},{24,8},{28,12},{1,17},{... | collective-permute-start | bytes 491528 | tf_op jit(solution)/shard_map/ppermute | solution.py:513
  8.1 2.7 %pack_rows.1 = bf16[1040,128]{1,0:T(8,128)(2,1)S(1)} custom-call(s32[10]{0:T(128)S(1)} %copy-done, bf16[4096,128]{1,0:T(8,128)(2,1)S(1)} %bitcast.65, s32[1,512]{1,0:T(1,128)S(1)} %copy-done.7), custom_call_target="tpu_custom_call" | custom-call | flops 3000000000 | bytes 1048576 | tf_op jit(solution)/shard_map/pack_rows/pallas_call | solution.py:498
  10.9 1.6 %copy-done.1 = bf16[128,64,128]{2,1,0:T(8,128)(2,1)S(1)} copy-done((bf16[128,64,128]{2,1,0:T(8,128)(2,1)S(1)}, bf16[128,64,128]{2,1,0:T(8,128)(2,1)}, u32[]{:S(2)}) %copy-start.1) | copy-done | bytes 2097176
  12.5 3.6 %pack_own.1 = (bf16[1040,128]{1,0:T(8,128)(2,1)S(1)}, bf16[640,128]{1,0:T(8,128)(2,1)S(1)}, bf16[640,128]{1,0:T(8,128)(2,1)S(1)}, bf16[640,128]{1,0:T(8,128)(2,1...) custom-call(s32[10]{0:T(128)S(1)} %copy-done, ...), custom_call_target="tpu_custom_call" | custom-call | flops 3000000000 | bytes 1048576 | tf_op jit(solution)/shard_map/pack_own/pallas_call | solution.py:498
  16.2 2.5 %collective-permute-done.1.refs_2_ = bf16[1040,128]{1,0:T(8,128)(2,1)S(1)} collective-permute-done((bf16[1040,128]{1,0:T(8,128)(2,1)S(1)}, bf16[1040,128]{1,0:T(8,128)(2,1)S(1)}, u32[]{:S(2)}, u32[]{:S(2)}) %collective-permute-start.1) | collective-permute-done | bytes 266272 | tf_op jit(solution)/shard_map/ppermute | solution.py:518
  18.7 1.2 %collective-permute-start.2 = (bf16[640,128]{1,0:T(8,128)(2,1)S(1)}, bf16[640,128]{1,0:T(8,128)(2,1)S(1)}, u32[]{:S(2)}, u32[]{:S(2)}) collective-permute-start(bf16[640,128]{1,0:T(8,128)(2,1)S(1)} %get-tuple-element.74), channel_id=1, source_target_pairs={{0,16},{4,20},{8,24},{12,28},{16,0},{20,4},{24,8},{28,12},{1,17},{... | collective-permute-start | bytes 491528 | tf_op jit(solution)/shard_map/ppermute | solution.py:531
  19.9 18.9 %decode0.1 = (f32[128,8,128]{2,1,0:T(8,128)S(1)}, f32[128,8,128]{2,1,0:T(8,128)S(1)}, f32[64,8,128]{2,1,0:T(8,128)S(1)}, f32[64,8,128]{2,1,0:T(8,128)S(1)}, f32[...) custom-call(s32[10]{0:T(128)S(1)} %copy-done, bf16[1040,128]{1,0:T(8,128)(2,1)S(1)} %get-tuple-element.75.refs_1_, ...), custom_call_target="tpu_custom_call" | custom-call | flops 22000001024 | bytes 1048576 | tf_op jit(solution)/shard_map/decode0/pallas_call | solution.py:498
  38.8 1.6 %collective-permute-start.4 = (f32[512,128]{1,0:T(8,128)S(1)}, f32[512,128]{1,0:T(8,128)S(1)}, u32[]{:S(2)}, u32[]{:S(2)}) collective-permute-start(f32[512,128]{1,0:T(8,128)S(1)} %bitcast.71), channel_id=1, source_target_pairs={{0,1},{1,0},{2,3},{3,2},{4,5},{5,4},{6,7},{7,6},{8,9},{9,8},{10,11... | collective-permute-start | bytes 786440 | tf_op jit(solution)/shard_map/ppermute | solution.py:25
  40.4 19.1 %decode1.1 = (f32[128,8,128]{2,1,0:T(8,128)S(1)}, f32[148,8,128]{2,1,0:T(8,128)S(1)}, f32[64,8,128]{2,1,0:T(8,128)S(1)}, f32[64,8,128]{2,1,0:T(8,128)S(1)}, f32[...) custom-call(s32[10]{0:T(128)S(1)} %copy-done, bf16[1040,128]{1,0:T(8,128)(2,1)S(1)} %get-tuple-element.75.refs_1_, ...), custom_call_target="tpu_custom_call" | custom-call | flops 22000001024 | bytes 1048576 | tf_op jit(solution)/shard_map/decode1/pallas_call | solution.py:498
  62.4 2.6 %collective-permute-start.7 = (f32[20,8,128]{2,1,0:T(8,128)S(1)}, f32[20,8,128]{2,1,0:T(8,128)S(1)}, u32[]{:S(2)}, u32[]{:S(2)}) collective-permute-start(f32[20,8,128]{2,1,0:T(8,128)S(1)} %slice_add_fusion.1), channel_id=1, source_target_pairs={{0,2},{1,3},{2,0},{3,1},{4,6},{5,7},{6,4},{7,5},{8,10},{9,11},{10,... | collective-permute-start | bytes 245768 | tf_op jit(solution)/shard_map/ppermute | solution.py:25
  66.0 1.5 %collective-permute-start.13 = (f16[1,1040,128]{2,1,0:T(8,128)(2,1)}, f16[1,1040,128]{2,1,0:T(8,128)(2,1)}, u32[]{:S(2)}, u32[]{:S(2)}) collective-permute-start(f16[1,1040,128]{2,1,0:T(8,128)(2,1)} %pad_maximum_fusion.1), channel_id=1, source_target_pairs={{0,8},{4,12},{8,0},{12,4},{16,24},{20,28},{24,16},{28,20},{1,9},{5... | collective-permute-start | bytes 798728 | tf_op jit(solution)/shard_map/ppermute | solution.py:25
  67.5 1.9 %collective-permute-done.8 = f16[1,1040,128]{2,1,0:T(8,128)(2,1)S(1)} collective-permute-done((f16[1,1040,128]{2,1,0:T(8,128)(2,1)S(1)}, f16[1,1040,128]{2,1,0:T(8,128)(2,1)S(1)}, u32[]{:S(2)}, u32[]{:S(2)}) %collective-permute-start.8) | collective-permute-done | bytes 266272 | tf_op jit(solution)/shard_map/ppermute | solution.py:596
  69.6 2.6 %collective-permute-start.9 = (f16[2,272,128]{2,1,0:T(8,128)(2,1)S(1)}, f16[2,272,128]{2,1,0:T(8,128)(2,1)S(1)}, u32[]{:S(2)}, u32[]{:S(2)}) collective-permute-start(f16[2,272,128]{2,1,0:T(8,128)(2,1)S(1)} %pad_maximum_fusion.3), channel_id=1, source_target_pairs={{0,2},{1,3},{2,0},{3,1},{4,6},{5,7},{6,4},{7,5},{8,10},{9,11},{10,... | collective-permute-start | bytes 417800 | tf_op jit(solution)/shard_map/ppermute | solution.py:25
  72.3 1.8 %collective-permute-start.12 = (f32[20,8,128]{2,1,0:T(8,128)S(1)}, f32[20,8,128]{2,1,0:T(8,128)S(1)}, u32[]{:S(2)}, u32[]{:S(2)}) collective-permute-start(f32[20,8,128]{2,1,0:T(8,128)S(1)} %add.73), channel_id=1, source_target_pairs={{0,24},{4,28},{8,16},{12,20},{16,8},{20,12},{24,0},{28,4},{1,25},{... | collective-permute-start | bytes 245768 | tf_op jit(solution)/shard_map/ppermute | solution.py:25
  74.6 1.2 %collective-permute-start.10 = (f32[20,8,128]{2,1,0:T(8,128)S(1)}, f32[20,8,128]{2,1,0:T(8,128)}, u32[]{:S(2)}, u32[]{:S(2)}) collective-permute-start(f32[20,8,128]{2,1,0:T(8,128)S(1)} %add.73), channel_id=1, source_target_pairs={{0,16},{4,20},{8,24},{12,28},{16,0},{20,4},{24,8},{28,12},{1,17},{... | collective-permute-start | bytes 245768 | tf_op jit(solution)/shard_map/ppermute | solution.py:25
  75.8 2.3 %collective-permute-done.12 = f32[20,8,128]{2,1,0:T(8,128)S(1)} collective-permute-done((f32[20,8,128]{2,1,0:T(8,128)S(1)}, f32[20,8,128]{2,1,0:T(8,128)S(1)}, u32[]{:S(2)}, u32[]{:S(2)}) %collective-permute-start.12) | collective-permute-done | bytes 81952 | tf_op jit(solution)/shard_map/ppermute | solution.py:25
  80.4 1.8 %collective-permute-start.16 = (f32[20,8,128]{2,1,0:T(8,128)S(1)}, f32[20,8,128]{2,1,0:T(8,128)S(1)}, u32[]{:S(2)}, u32[]{:S(2)}) collective-permute-start(f32[20,8,128]{2,1,0:T(8,128)S(1)} %add_add_fusion), channel_id=1, source_target_pairs={{0,4},{4,0},{8,12},{12,8},{16,20},{20,16},{24,28},{28,24},{1,5},{5... | collective-permute-start | bytes 245768 | tf_op jit(solution)/shard_map/ppermute | solution.py:25
  82.7 1.9 %collective-permute-start.14 = (f16[2,272,128]{2,1,0:T(8,128)(2,1)S(1)}, f16[2,272,128]{2,1,0:T(8,128)(2,1)S(1)}, u32[]{:S(2)}, u32[]{:S(2)}) collective-permute-start(f16[2,272,128]{2,1,0:T(8,128)(2,1)S(1)} %pad_maximum_fusion.4), channel_id=1, source_target_pairs={{0,18},{1,19},{2,16},{3,17},{4,22},{5,23},{6,20},{7,21},{8,26},{9,... | collective-permute-start | bytes 417800 | tf_op jit(solution)/shard_map/ppermute | solution.py:592
  84.6 1.0 %convert_element_type.48 = f32[1,1040,128]{2,1,0:T(8,128)S(1)} convert(f16[1,1040,128]{2,1,0:T(8,128)(2,1)} %collective-permute-done.13) | non-fusion elementwise | flops 133120 | bytes 798720 | tf_op jit(solution)/shard_map/convert_element_type | solution.py:203
  85.6 1.0 %fusion.1 = f32[128,8,128]{2,1,0:T(8,128)} fusion(f32[1,1040,128]{2,1,0:T(8,128)S(1)} %convert_element_type.48, f32[128]{0:T(128)S(1)} %fusion.15, pred[]{:T(512)S(6)} %or.3, f32[128,8,128]{2,1,0:T(8,128)S(1)} %get-tuple-element.113, f32[128,8,128]{2,1,0:T(8,128)S(1)} %copy-done.11, f32[128,8,128]{2,1,0:T(8,128)S(1)} %get-tuple-element.112, ...), kind=kLoop, calls=%fused_computation.2 | loop fusion | flops 655360 | bytes 3146241 | tf_op jit(solution)/shard_map/add | solution.py:616
  86.6 3.1 %place.1 = f32[4096,128]{1,0:T(8,128)} custom-call(s32[10]{0:T(128)S(1)} %copy-done, s32[1,512]{1,0:T(1,128)S(1)} %copy-done.7, f32[1024,128]{1,0:T(8,128)S(1)} %get-tuple-element.103.mine_ref, f32[1024,128]{1,0:T(8,128)S(1)} %fusion.2.recv_ref), custom_call_target="tpu_custom_call" | custom-call | flops 3000000000 | bytes 1048576 | tf_op jit(solution)/shard_map/place/pallas_call | solution.py:498
  89.8 3.4 %collective-permute-done.14 = f16[2,272,128]{2,1,0:T(8,128)(2,1)S(1)} collective-permute-done((f16[2,272,128]{2,1,0:T(8,128)(2,1)S(1)}, f16[2,272,128]{2,1,0:T(8,128)(2,1)S(1)}, u32[]{:S(2)}, u32[]{:S(2)}) %collective-permute-start.14) | collective-permute-done | bytes 139296 | tf_op jit(solution)/shard_map/ppermute | solution.py:592
  93.3 1.3 %finish.1 = (f32[16,32,128]{2,1,0:T(8,128)}, f32[128,256]{1,0:T(8,128)}, f32[1,256]{1,0:T(1,128)}, f32[18,256]{1,0:T(8,128)}, f32[1,18]{1,0:T(1,128)}) custom-call(s32[10]{0:T(128)S(1)} %copy-done, f32[2,256,128]{2,1,0:T(8,128)S(1)} %slice_multiply_fusion.2.zh_ref, f32[20,8,128]{2,1,0:T(8,128)S(1)} %add.80.w_mine_ref, f32[20,8,128]{2,1,0:T(8,128)S(1)} %add.81.w_other_ref), custom_call_target="tpu_custom_call" | custom-call | flops 1000000000 | bytes 1048576 | tf_op jit(solution)/shard_map/finish/pallas_call | solution.py:498
  (94 shorter events, 8.1 us)
Async XLA Ops:
  2.1 5.9 %copy-start = (s32[10]{0:T(128)S(1)}, s32[10]{0:T(128)}, u32[]{:S(2)}) copy-start(s32[10]{0:T(128)} %stack.48.meta_ref.refs_0_) | copy-start | bytes 124
  2.1 5.9 %copy-start.2 = (bf16[32,128,128]{2,1,0:T(8,128)(2,1)S(1)}, bf16[32,128,128]{2,1,0:T(8,128)(2,1)}, u32[]{:S(2)}) copy-start(bf16[32,128,128]{2,1,0:T(8,128)(2,1)} %param.10) | copy-start | bytes 3145732
  2.1 5.9 %copy-start.7 = (s32[1,512]{1,0:T(1,128)S(1)}, s32[1,512]{1,0:T(1,128)}, u32[]{:S(2)}) copy-start(s32[1,512]{1,0:T(1,128)} %rid_ref.1) | copy-start | bytes 6148
  5.0 11.2 %collective-permute-start = (bf16[640,128]{1,0:T(8,128)(2,1)}, bf16[640,128]{1,0:T(8,128)(2,1)S(1)}, u32[]{:S(2)}, u32[]{:S(2)}) collective-permute-start(bf16[640,128]{1,0:T(8,128)(2,1)} %pack_plane.1), channel_id=1, source_target_pairs={{0,16},{4,20},{8,24},{12,28},{16,0},{20,4},{24,8},{28,12},{1,17},{... | collective-permute-start | bytes 491528 | tf_op jit(solution)/shard_map/ppermute | solution.py:513
  8.0 2.8 %copy-start.3 = (bf16[64,32,128]{2,1,0:T(8,128)(2,1)S(1)}, bf16[64,32,128]{2,1,0:T(8,128)(2,1)}, u32[]{:S(2)}) copy-start(bf16[64,32,128]{2,1,0:T(8,128)(2,1)} %param.11) | copy-start | bytes 1572868
  10.7 7.9 %collective-permute-start.1 = (bf16[1040,128]{1,0:T(8,128)(2,1)S(1)}, bf16[1040,128]{1,0:T(8,128)(2,1)S(1)}, u32[]{:S(2)}, u32[]{:S(2)}) collective-permute-start(bf16[1040,128]{1,0:T(8,128)(2,1)S(1)} %pack_rows.1), channel_id=1, source_target_pairs={{0,16},{4,20},{8,24},{12,28},{16,0},{20,4},{24,8},{28,12},{1,17},{... | collective-permute-start | bytes 798728 | tf_op jit(solution)/shard_map/ppermute | solution.py:518
  18.7 20.1 %collective-permute-start.2 = (bf16[640,128]{1,0:T(8,128)(2,1)S(1)}, bf16[640,128]{1,0:T(8,128)(2,1)S(1)}, u32[]{:S(2)}, u32[]{:S(2)}) collective-permute-start(bf16[640,128]{1,0:T(8,128)(2,1)S(1)} %get-tuple-element.74), channel_id=1, source_target_pairs={{0,16},{4,20},{8,24},{12,28},{16,0},{20,4},{24,8},{28,12},{1,17},{... | collective-permute-start | bytes 491528 | tf_op jit(solution)/shard_map/ppermute | solution.py:531
  38.8 20.8 %collective-permute-start.4 = (f32[512,128]{1,0:T(8,128)S(1)}, f32[512,128]{1,0:T(8,128)S(1)}, u32[]{:S(2)}, u32[]{:S(2)}) collective-permute-start(f32[512,128]{1,0:T(8,128)S(1)} %bitcast.71), channel_id=1, source_target_pairs={{0,1},{1,0},{2,3},{3,2},{4,5},{5,4},{6,7},{7,6},{8,9},{9,8},{10,11... | collective-permute-start | bytes 786440 | tf_op jit(solution)/shard_map/ppermute | solution.py:25
  40.4 19.1 %collective-permute-start.3 = (f32[128,8,128]{2,1,0:T(8,128)S(1)}, f32[128,8,128]{2,1,0:T(8,128)S(1)}, u32[]{:S(2)}, u32[]{:S(2)}) collective-permute-start(f32[128,8,128]{2,1,0:T(8,128)S(1)} %get-tuple-element.90), channel_id=1, source_target_pairs={{0,4},{4,0},{8,12},{12,8},{16,20},{20,16},{24,28},{28,24},{1,5},{5... | collective-permute-start | bytes 1572872 | tf_op jit(solution)/shard_map/ppermute | solution.py:25
  59.6 5.6 %copy-start.10 = (f32[128,8,128]{2,1,0:T(8,128)}, f32[128,8,128]{2,1,0:T(8,128)S(1)}, u32[]{:S(2)}) copy-start(f32[128,8,128]{2,1,0:T(8,128)S(1)} %collective-permute-done.3) | copy-start | bytes 1572868
  59.8 7.7 %collective-permute-start.5 = (f16[1,528,128]{2,1,0:T(8,128)(2,1)S(1)}, f16[1,528,128]{2,1,0:T(8,128)(2,1)S(1)}, u32[]{:S(2)}, u32[]{:S(2)}) collective-permute-start(f16[1,528,128]{2,1,0:T(8,128)(2,1)S(1)} %pad_maximum_fusion.5), channel_id=1, source_target_pairs={{0,1},{1,0},{2,3},{3,2},{4,5},{5,4},{6,7},{7,6},{8,9},{9,8},{10,11... | collective-permute-start | bytes 405512 | tf_op jit(solution)/shard_map/ppermute | solution.py:25
  60.4 2.0 %collective-permute-start.6 = (f32[148,8,128]{2,1,0:T(8,128)S(1)}, f32[148,8,128]{2,1,0:T(8,128)S(1)}, u32[]{:S(2)}, u32[]{:S(2)}) collective-permute-start(f32[148,8,128]{2,1,0:T(8,128)S(1)} %get-tuple-element.109), channel_id=1, source_target_pairs={{0,4},{4,0},{8,12},{12,8},{16,20},{20,16},{24,28},{28,24},{1,5},{5... | collective-permute-start | bytes 1818632 | tf_op jit(solution)/shard_map/ppermute | solution.py:25
  60.7 8.7 %collective-permute-start.8 = (f16[1,1040,128]{2,1,0:T(8,128)(2,1)S(1)}, f16[1,1040,128]{2,1,0:T(8,128)(2,1)S(1)}, u32[]{:S(2)}, u32[]{:S(2)}) collective-permute-start(f16[1,1040,128]{2,1,0:T(8,128)(2,1)S(1)} %pad_maximum_fusion), channel_id=1, source_target_pairs={{0,16},{4,20},{8,24},{12,28},{16,0},{20,4},{24,8},{28,12},{1,17},{... | collective-permute-start | bytes 798728 | tf_op jit(solution)/shard_map/ppermute | solution.py:596
  62.4 7.0 %collective-permute-start.7 = (f32[20,8,128]{2,1,0:T(8,128)S(1)}, f32[20,8,128]{2,1,0:T(8,128)S(1)}, u32[]{:S(2)}, u32[]{:S(2)}) collective-permute-start(f32[20,8,128]{2,1,0:T(8,128)S(1)} %slice_add_fusion.1), channel_id=1, source_target_pairs={{0,2},{1,3},{2,0},{3,1},{4,6},{5,7},{6,4},{7,5},{8,10},{9,11},{10,... | collective-permute-start | bytes 245768 | tf_op jit(solution)/shard_map/ppermute | solution.py:25
  66.0 13.2 %collective-permute-start.13 = (f16[1,1040,128]{2,1,0:T(8,128)(2,1)}, f16[1,1040,128]{2,1,0:T(8,128)(2,1)}, u32[]{:S(2)}, u32[]{:S(2)}) collective-permute-start(f16[1,1040,128]{2,1,0:T(8,128)(2,1)} %pad_maximum_fusion.1), channel_id=1, source_target_pairs={{0,8},{4,12},{8,0},{12,4},{16,24},{20,28},{24,16},{28,20},{1,9},{5... | collective-permute-start | bytes 798728 | tf_op jit(solution)/shard_map/ppermute | solution.py:25
  69.6 9.5 %collective-permute-start.9 = (f16[2,272,128]{2,1,0:T(8,128)(2,1)S(1)}, f16[2,272,128]{2,1,0:T(8,128)(2,1)S(1)}, u32[]{:S(2)}, u32[]{:S(2)}) collective-permute-start(f16[2,272,128]{2,1,0:T(8,128)(2,1)S(1)} %pad_maximum_fusion.3), channel_id=1, source_target_pairs={{0,2},{1,3},{2,0},{3,1},{4,6},{5,7},{6,4},{7,5},{8,10},{9,11},{10,... | collective-permute-start | bytes 417800 | tf_op jit(solution)/shard_map/ppermute | solution.py:25
  72.3 5.9 %collective-permute-start.12 = (f32[20,8,128]{2,1,0:T(8,128)S(1)}, f32[20,8,128]{2,1,0:T(8,128)S(1)}, u32[]{:S(2)}, u32[]{:S(2)}) collective-permute-start(f32[20,8,128]{2,1,0:T(8,128)S(1)} %add.73), channel_id=1, source_target_pairs={{0,24},{4,28},{8,16},{12,20},{16,8},{20,12},{24,0},{28,4},{1,25},{... | collective-permute-start | bytes 245768 | tf_op jit(solution)/shard_map/ppermute | solution.py:25
  74.1 4.4 %collective-permute-start.11 = (f32[20,8,128]{2,1,0:T(8,128)S(1)}, f32[20,8,128]{2,1,0:T(8,128)S(1)}, u32[]{:S(2)}, u32[]{:S(2)}) collective-permute-start(f32[20,8,128]{2,1,0:T(8,128)S(1)} %add.73), channel_id=1, source_target_pairs={{0,8},{4,12},{8,0},{12,4},{16,24},{20,28},{24,16},{28,20},{1,9},{5... | collective-permute-start | bytes 245768 | tf_op jit(solution)/shard_map/ppermute | solution.py:25
  74.6 4.5 %collective-permute-start.10 = (f32[20,8,128]{2,1,0:T(8,128)S(1)}, f32[20,8,128]{2,1,0:T(8,128)}, u32[]{:S(2)}, u32[]{:S(2)}) collective-permute-start(f32[20,8,128]{2,1,0:T(8,128)S(1)} %add.73), channel_id=1, source_target_pairs={{0,16},{4,20},{8,24},{12,28},{16,0},{20,4},{24,8},{28,12},{1,17},{... | collective-permute-start | bytes 245768 | tf_op jit(solution)/shard_map/ppermute | solution.py:25
  80.1 9.6 %collective-permute-start.17 = (f32[20,8,128]{2,1,0:T(8,128)S(1)}, f32[20,8,128]{2,1,0:T(8,128)S(1)}, u32[]{:S(2)}, u32[]{:S(2)}) collective-permute-start(f32[20,8,128]{2,1,0:T(8,128)S(1)} %add_add_fusion), channel_id=1, source_target_pairs={{0,5},{1,4},{2,7},{3,6},{4,1},{5,0},{6,3},{7,2},{8,13},{9,12},{10,... | collective-permute-start | bytes 245768 | tf_op jit(solution)/shard_map/ppermute | solution.py:592
  80.4 9.3 %collective-permute-start.16 = (f32[20,8,128]{2,1,0:T(8,128)S(1)}, f32[20,8,128]{2,1,0:T(8,128)S(1)}, u32[]{:S(2)}, u32[]{:S(2)}) collective-permute-start(f32[20,8,128]{2,1,0:T(8,128)S(1)} %add_add_fusion), channel_id=1, source_target_pairs={{0,4},{4,0},{8,12},{12,8},{16,20},{20,16},{24,28},{28,24},{1,5},{5... | collective-permute-start | bytes 245768 | tf_op jit(solution)/shard_map/ppermute | solution.py:25
  82.2 7.5 %collective-permute-start.15 = (f32[20,8,128]{2,1,0:T(8,128)S(1)}, f32[20,8,128]{2,1,0:T(8,128)S(1)}, u32[]{:S(2)}, u32[]{:S(2)}) collective-permute-start(f32[20,8,128]{2,1,0:T(8,128)S(1)} %add_add_fusion), channel_id=1, source_target_pairs={{0,1},{1,0},{2,3},{3,2},{4,5},{5,4},{6,7},{7,6},{8,9},{9,8},{10,11... | collective-permute-start | bytes 245768 | tf_op jit(solution)/shard_map/ppermute | solution.py:25
  82.4 3.2 %copy-start.11 = (f32[128,8,128]{2,1,0:T(8,128)S(1)}, f32[128,8,128]{2,1,0:T(8,128)}, u32[]{:S(2)}) copy-start(f32[128,8,128]{2,1,0:T(8,128)} %copy-done.10) | copy-start | bytes 1572868
  82.7 10.5 %collective-permute-start.14 = (f16[2,272,128]{2,1,0:T(8,128)(2,1)S(1)}, f16[2,272,128]{2,1,0:T(8,128)(2,1)S(1)}, u32[]{:S(2)}, u32[]{:S(2)}) collective-permute-start(f16[2,272,128]{2,1,0:T(8,128)(2,1)S(1)} %pad_maximum_fusion.4), channel_id=1, source_target_pairs={{0,18},{1,19},{2,16},{3,17},{4,22},{5,23},{6,20},{7,21},{8,26},{9,... | collective-permute-start | bytes 417800 | tf_op jit(solution)/shard_map/ppermute | solution.py:592
  (6 other events, 15.7 us)

commit v4 on v3

--- a/solution.py
+++ b/solution.py
@@ -12,7 +12,7 @@
 CLS_PAD = 32
 CHUNKS = ((0, 3), (1, 2))
 ZC = 16
-RUNS = 32
+RUNS = 16
 GROUP = 4
 ROWS = RUNS * 2 * ZC
 STRIP = 32
@@ -601,7 +601,7 @@
         part0 = zh0a + zh0r
         w = w_keep + core_recv[cols_blk:]
         wr = ppermute_xor(w, "wa", n_wa, 2)
-        zh1r, wr, hw_recv = barrier((zh1r, wr, hw_recv))
+        zh1r, wr = barrier((zh1r, wr))
         both = jnp.stack([part0, zh1a + decode_half(zh1r)[0]])
         zhf = ppermute_xor(encode(both[:, n_part:]), "wa", n_wa, 2)
         w = w + wr

time: 94.9 us -> 100 us (1.054)
  Pallas kernels: 51.7 us -> 57 us
    pallas_call x7, Pallas kernels: 51.7 us -> 57 us  [call(): pl.pallas_call(kernel, out_shape=[jax.ShapeDtypeStruct(shape, kind) for s...]
    ppermute x1, waiting for transfers between devices: 1.85 us -> 0.01 us  [local(): hw_recv = lax.ppermute(encode(hw1[None]), 'ha', swap_y)]
    ppermute x2, waiting for transfers between devices: 3.44 us -> 4.85 us  [corner(): return lax.ppermute(value, ('ha', 'wa'), pairs)]
    ppermute x12, waiting for transfers between devices: 4.09 us -> 5.2 us  [ppermute_xor(): return lax.ppermute(value, axis, [(i, i ^ mask) for i in range(size)])]
  transfers between devices with their start and end apart: 18 -> 18, of which waited for: 7 -> 7; matrix products, arithmetic and copies ran while one was open for 4% -> 4% of each run, Pallas kernels for 50% -> 53%
where the time goes in v4:
time: 100 us; the launch traced here: 99.9 us
  Pallas kernels  57 us (57%)
  starting transfers between devices  21.4 us (21%)
  waiting for transfers between devices  12.6 us (13%)
  other arithmetic  4.76 us (5%)
  local copies, waits for them, and re-layouts  2.37 us (2%)
  between operations  1.85 us (2%)
    pallas_call x7, Pallas kernels, call(): pl.pallas_call(kernel, out_shape=[jax.ShapeDtypeStruct(shape, kind) for s...  57 us
    ppermute x12, starting transfers between devices, ppermute_xor(): return lax.ppermute(value, axis, [(i, i ^ mask) for i in range(size)])  14.3 us
    ppermute x12, waiting for transfers between devices, ppermute_xor(): return lax.ppermute(value, axis, [(i, i ^ mask) for i in range(size)])  5.2 us
    ppermute x2, waiting for transfers between devices, corner(): return lax.ppermute(value, ('ha', 'wa'), pairs)  4.85 us
    ppermute x1, starting transfers between devices, local(): recv0 = lax.ppermute(send0, 'ha', swap_y)  3.03 us
    ppermute x1, waiting for transfers between devices, local(): recv_hw = lax.ppermute(send_hw, 'ha', swap_y)  2.51 us
  transfers between devices with their start and end apart: 18, of which 7 were waited for; matrix products, arithmetic and copies ran while one was open for 4% of the time, Pallas kernels for 53%

profile of v4, /device:TPU:0, one launch (start us, length us, event | category | flops | bytes accessed | tf_op | source)
XLA Modules:
  0.0 99.9 jit_solution(13587803649519543210)
XLA Ops:
  2.1 2.9 %pack_plane.1 = bf16[640,128]{1,0:T(8,128)(2,1)} custom-call(s32[10]{0:T(128)} %stack.48.meta_ref.refs_0_, bf16[2048,128]{1,0:T(8,128)(2,1)} %bitcast.67, s32[512,128]{1,0:T(8,128)} %bitcast.69), custom_call_target="tpu_custom_call" | custom-call | flops 2000000000 | bytes 1048576 | tf_op jit(solution)/shard_map/pack_plane/pallas_call | solution.py:498
  5.0 3.0 %collective-permute-start = (bf16[640,128]{1,0:T(8,128)(2,1)}, bf16[640,128]{1,0:T(8,128)(2,1)S(1)}, u32[]{:S(2)}, u32[]{:S(2)}) collective-permute-start(bf16[640,128]{1,0:T(8,128)(2,1)} %pack_plane.1), channel_id=1, source_target_pairs={{0,16},{4,20},{8,24},{12,28},{16,0},{20,4},{24,8},{28,12},{1,17},{... | collective-permute-start | bytes 491528 | tf_op jit(solution)/shard_map/ppermute | solution.py:513
  8.1 2.7 %pack_rows.1 = bf16[1040,128]{1,0:T(8,128)(2,1)S(1)} custom-call(s32[10]{0:T(128)S(1)} %copy-done, bf16[4096,128]{1,0:T(8,128)(2,1)S(1)} %bitcast.65, s32[1,512]{1,0:T(1,128)S(1)} %copy-done.7), custom_call_target="tpu_custom_call" | custom-call | flops 3000000000 | bytes 1048576 | tf_op jit(solution)/shard_map/pack_rows/pallas_call | solution.py:498
  10.9 1.6 %copy-done.1 = bf16[128,64,128]{2,1,0:T(8,128)(2,1)S(1)} copy-done((bf16[128,64,128]{2,1,0:T(8,128)(2,1)S(1)}, bf16[128,64,128]{2,1,0:T(8,128)(2,1)}, u32[]{:S(2)}) %copy-start.1) | copy-done | bytes 2097176
  12.5 3.6 %pack_own.1 = (bf16[1040,128]{1,0:T(8,128)(2,1)S(1)}, bf16[640,128]{1,0:T(8,128)(2,1)S(1)}, bf16[640,128]{1,0:T(8,128)(2,1)S(1)}, bf16[640,128]{1,0:T(8,128)(2,1...) custom-call(s32[10]{0:T(128)S(1)} %copy-done, ...), custom_call_target="tpu_custom_call" | custom-call | flops 3000000000 | bytes 1048576 | tf_op jit(solution)/shard_map/pack_own/pallas_call | solution.py:498
  16.2 2.5 %collective-permute-done.1.refs_2_ = bf16[1040,128]{1,0:T(8,128)(2,1)S(1)} collective-permute-done((bf16[1040,128]{1,0:T(8,128)(2,1)S(1)}, bf16[1040,128]{1,0:T(8,128)(2,1)S(1)}, u32[]{:S(2)}, u32[]{:S(2)}) %collective-permute-start.1) | collective-permute-done | bytes 266272 | tf_op jit(solution)/shard_map/ppermute | solution.py:518
  18.7 1.2 %collective-permute-start.2 = (bf16[640,128]{1,0:T(8,128)(2,1)S(1)}, bf16[640,128]{1,0:T(8,128)(2,1)S(1)}, u32[]{:S(2)}, u32[]{:S(2)}) collective-permute-start(bf16[640,128]{1,0:T(8,128)(2,1)S(1)} %get-tuple-element.73), channel_id=1, source_target_pairs={{0,16},{4,20},{8,24},{12,28},{16,0},{20,4},{24,8},{28,12},{1,17},{... | collective-permute-start | bytes 491528 | tf_op jit(solution)/shard_map/ppermute | solution.py:531
  19.9 21.7 %decode0.1 = (f32[128,8,128]{2,1,0:T(8,128)S(1)}, f32[128,8,128]{2,1,0:T(8,128)S(1)}, f32[64,8,128]{2,1,0:T(8,128)S(1)}, f32[64,8,128]{2,1,0:T(8,128)S(1)}, f32[...) custom-call(s32[10]{0:T(128)S(1)} %copy-done, bf16[1040,128]{1,0:T(8,128)(2,1)S(1)} %get-tuple-element.74.refs_1_, ...), custom_call_target="tpu_custom_call" | custom-call | flops 22000001024 | bytes 1048576 | tf_op jit(solution)/shard_map/decode0/pallas_call | solution.py:498
  41.5 1.6 %collective-permute-start.4 = (f32[512,128]{1,0:T(8,128)S(1)}, f32[512,128]{1,0:T(8,128)S(1)}, u32[]{:S(2)}, u32[]{:S(2)}) collective-permute-start(f32[512,128]{1,0:T(8,128)S(1)} %bitcast.71), channel_id=1, source_target_pairs={{0,1},{1,0},{2,3},{3,2},{4,5},{5,4},{6,7},{7,6},{8,9},{9,8},{10,11... | collective-permute-start | bytes 786440 | tf_op jit(solution)/shard_map/ppermute | solution.py:25
  43.2 21.7 %decode1.1 = (f32[128,8,128]{2,1,0:T(8,128)S(1)}, f32[148,8,128]{2,1,0:T(8,128)S(1)}, f32[64,8,128]{2,1,0:T(8,128)S(1)}, f32[64,8,128]{2,1,0:T(8,128)S(1)}, f32[...) custom-call(s32[10]{0:T(128)S(1)} %copy-done, bf16[1040,128]{1,0:T(8,128)(2,1)S(1)} %get-tuple-element.74.refs_1_, ...), custom_call_target="tpu_custom_call" | custom-call | flops 22000001024 | bytes 1048576 | tf_op jit(solution)/shard_map/decode1/pallas_call | solution.py:498
  66.1 0.9 collective-permute-start.13
  67.8 2.6 %collective-permute-start.7 = (f32[20,8,128]{2,1,0:T(8,128)S(1)}, f32[20,8,128]{2,1,0:T(8,128)S(1)}, u32[]{:S(2)}, u32[]{:S(2)}) collective-permute-start(f32[20,8,128]{2,1,0:T(8,128)S(1)} %slice_add_fusion.1), channel_id=1, source_target_pairs={{0,2},{1,3},{2,0},{3,1},{4,6},{5,7},{6,4},{7,5},{8,10},{9,11},{10,... | collective-permute-start | bytes 245768 | tf_op jit(solution)/shard_map/ppermute | solution.py:25
  71.4 1.5 %collective-permute-start.12 = (f16[1,1040,128]{2,1,0:T(8,128)(2,1)}, f16[1,1040,128]{2,1,0:T(8,128)(2,1)}, u32[]{:S(2)}, u32[]{:S(2)}) collective-permute-start(f16[1,1040,128]{2,1,0:T(8,128)(2,1)} %pad_maximum_fusion), channel_id=1, source_target_pairs={{0,8},{4,12},{8,0},{12,4},{16,24},{20,28},{24,16},{28,20},{1,9},{5... | collective-permute-start | bytes 798728 | tf_op jit(solution)/shard_map/ppermute | solution.py:25
  73.9 2.3 %collective-permute-start.8 = (f16[2,272,128]{2,1,0:T(8,128)(2,1)S(1)}, f16[2,272,128]{2,1,0:T(8,128)(2,1)S(1)}, u32[]{:S(2)}, u32[]{:S(2)}) collective-permute-start(f16[2,272,128]{2,1,0:T(8,128)(2,1)S(1)} %pad_maximum_fusion.3), channel_id=1, source_target_pairs={{0,2},{1,3},{2,0},{3,1},{4,6},{5,7},{6,4},{7,5},{8,10},{9,11},{10,... | collective-permute-start | bytes 417800 | tf_op jit(solution)/shard_map/ppermute | solution.py:25
  76.3 1.9 %collective-permute-start.11 = (f32[20,8,128]{2,1,0:T(8,128)S(1)}, f32[20,8,128]{2,1,0:T(8,128)S(1)}, u32[]{:S(2)}, u32[]{:S(2)}) collective-permute-start(f32[20,8,128]{2,1,0:T(8,128)S(1)} %add.73), channel_id=1, source_target_pairs={{0,24},{4,28},{8,16},{12,20},{16,8},{20,12},{24,0},{28,4},{1,25},{... | collective-permute-start | bytes 245768 | tf_op jit(solution)/shard_map/ppermute | solution.py:25
  78.6 1.2 %collective-permute-start.9 = (f32[20,8,128]{2,1,0:T(8,128)S(1)}, f32[20,8,128]{2,1,0:T(8,128)}, u32[]{:S(2)}, u32[]{:S(2)}) collective-permute-start(f32[20,8,128]{2,1,0:T(8,128)S(1)} %add.73), channel_id=1, source_target_pairs={{0,16},{4,20},{8,24},{12,28},{16,0},{20,4},{24,8},{28,12},{1,17},{... | collective-permute-start | bytes 245768 | tf_op jit(solution)/shard_map/ppermute | solution.py:25
  79.8 3.0 %collective-permute-done.11 = f32[20,8,128]{2,1,0:T(8,128)S(1)} collective-permute-done((f32[20,8,128]{2,1,0:T(8,128)S(1)}, f32[20,8,128]{2,1,0:T(8,128)S(1)}, u32[]{:S(2)}, u32[]{:S(2)}) %collective-permute-start.11) | collective-permute-done | bytes 81952 | tf_op jit(solution)/shard_map/ppermute | solution.py:25
  84.5 1.3 %collective-permute-start.17 = (f32[20,8,128]{2,1,0:T(8,128)S(1)}, f32[20,8,128]{2,1,0:T(8,128)S(1)}, u32[]{:S(2)}, u32[]{:S(2)}) collective-permute-start(f32[20,8,128]{2,1,0:T(8,128)S(1)} %add_add_fusion), channel_id=1, source_target_pairs={{0,5},{1,4},{2,7},{3,6},{4,1},{5,0},{6,3},{7,2},{8,13},{9,12},{10,... | collective-permute-start | bytes 245768 | tf_op jit(solution)/shard_map/ppermute | solution.py:592
  85.8 1.8 %collective-permute-start.16 = (f32[20,8,128]{2,1,0:T(8,128)S(1)}, f32[20,8,128]{2,1,0:T(8,128)S(1)}, u32[]{:S(2)}, u32[]{:S(2)}) collective-permute-start(f32[20,8,128]{2,1,0:T(8,128)S(1)} %add_add_fusion), channel_id=1, source_target_pairs={{0,4},{4,0},{8,12},{12,8},{16,20},{20,16},{24,28},{28,24},{1,5},{5... | collective-permute-start | bytes 245768 | tf_op jit(solution)/shard_map/ppermute | solution.py:25
  88.5 1.0 convert_element_type.48
  89.5 1.0 fusion.1
  90.5 3.1 %place.1 = f32[4096,128]{1,0:T(8,128)} custom-call(s32[10]{0:T(128)S(1)} %copy-done, s32[1,512]{1,0:T(1,128)S(1)} %copy-done.7, f32[1024,128]{1,0:T(8,128)S(1)} %get-tuple-element.102.mine_ref, f32[1024,128]{1,0:T(8,128)S(1)} %fusion.2.recv_ref), custom_call_target="tpu_custom_call" | custom-call | flops 3000000000 | bytes 1048576 | tf_op jit(solution)/shard_map/place/pallas_call | solution.py:498
  93.7 4.8 %collective-permute-done.14 = f16[2,272,128]{2,1,0:T(8,128)(2,1)S(1)} collective-permute-done((f16[2,272,128]{2,1,0:T(8,128)(2,1)S(1)}, f16[2,272,128]{2,1,0:T(8,128)(2,1)S(1)}, u32[]{:S(2)}, u32[]{:S(2)}) %collective-permute-start.14) | collective-permute-done | bytes 139296 | tf_op jit(solution)/shard_map/ppermute | solution.py:592
  98.6 1.3 %finish.1 = (f32[16,32,128]{2,1,0:T(8,128)}, f32[128,256]{1,0:T(8,128)}, f32[1,256]{1,0:T(1,128)}, f32[18,256]{1,0:T(8,128)}, f32[1,18]{1,0:T(1,128)}) custom-call(s32[10]{0:T(128)S(1)} %copy-done, f32[2,256,128]{2,1,0:T(8,128)S(1)} %slice_multiply_fusion.2.zh_ref, f32[20,8,128]{2,1,0:T(8,128)S(1)} %add.80.w_mine_ref, f32[20,8,128]{2,1,0:T(8,128)S(1)} %add.81.w_other_ref), custom_call_target="tpu_custom_call" | custom-call | flops 1000000000 | bytes 1048576 | tf_op jit(solution)/shard_map/finish/pallas_call | solution.py:498
  (94 shorter events, 7.8 us)
Async XLA Ops:
  2.1 5.9 %copy-start = (s32[10]{0:T(128)S(1)}, s32[10]{0:T(128)}, u32[]{:S(2)}) copy-start(s32[10]{0:T(128)} %stack.48.meta_ref.refs_0_) | copy-start | bytes 124
  2.1 5.9 %copy-start.2 = (bf16[32,128,128]{2,1,0:T(8,128)(2,1)S(1)}, bf16[32,128,128]{2,1,0:T(8,128)(2,1)}, u32[]{:S(2)}) copy-start(bf16[32,128,128]{2,1,0:T(8,128)(2,1)} %param.10) | copy-start | bytes 3145732
  2.1 5.9 %copy-start.7 = (s32[1,512]{1,0:T(1,128)S(1)}, s32[1,512]{1,0:T(1,128)}, u32[]{:S(2)}) copy-start(s32[1,512]{1,0:T(1,128)} %rid_ref.1) | copy-start | bytes 6148
  5.0 11.2 %collective-permute-start = (bf16[640,128]{1,0:T(8,128)(2,1)}, bf16[640,128]{1,0:T(8,128)(2,1)S(1)}, u32[]{:S(2)}, u32[]{:S(2)}) collective-permute-start(bf16[640,128]{1,0:T(8,128)(2,1)} %pack_plane.1), channel_id=1, source_target_pairs={{0,16},{4,20},{8,24},{12,28},{16,0},{20,4},{24,8},{28,12},{1,17},{... | collective-permute-start | bytes 491528 | tf_op jit(solution)/shard_map/ppermute | solution.py:513
  8.0 2.8 %copy-start.3 = (bf16[64,32,128]{2,1,0:T(8,128)(2,1)S(1)}, bf16[64,32,128]{2,1,0:T(8,128)(2,1)}, u32[]{:S(2)}) copy-start(bf16[64,32,128]{2,1,0:T(8,128)(2,1)} %param.11) | copy-start | bytes 1572868
  8.0 2.8 %copy-start.4 = (s32[1,512,128]{2,1,0:T(8,128)S(1)}, s32[1,512,128]{2,1,0:T(8,128)}, u32[]{:S(2)}) copy-start(s32[1,512,128]{2,1,0:T(8,128)} %param.19) | copy-start | bytes 786436
  10.7 7.9 %collective-permute-start.1 = (bf16[1040,128]{1,0:T(8,128)(2,1)S(1)}, bf16[1040,128]{1,0:T(8,128)(2,1)S(1)}, u32[]{:S(2)}, u32[]{:S(2)}) collective-permute-start(bf16[1040,128]{1,0:T(8,128)(2,1)S(1)} %pack_rows.1), channel_id=1, source_target_pairs={{0,16},{4,20},{8,24},{12,28},{16,0},{20,4},{24,8},{28,12},{1,17},{... | collective-permute-start | bytes 798728 | tf_op jit(solution)/shard_map/ppermute | solution.py:518
  18.7 22.9 %collective-permute-start.2 = (bf16[640,128]{1,0:T(8,128)(2,1)S(1)}, bf16[640,128]{1,0:T(8,128)(2,1)S(1)}, u32[]{:S(2)}, u32[]{:S(2)}) collective-permute-start(bf16[640,128]{1,0:T(8,128)(2,1)S(1)} %get-tuple-element.73), channel_id=1, source_target_pairs={{0,16},{4,20},{8,24},{12,28},{16,0},{20,4},{24,8},{28,12},{1,17},{... | collective-permute-start | bytes 491528 | tf_op jit(solution)/shard_map/ppermute | solution.py:531
  41.5 23.3 %collective-permute-start.4 = (f32[512,128]{1,0:T(8,128)S(1)}, f32[512,128]{1,0:T(8,128)S(1)}, u32[]{:S(2)}, u32[]{:S(2)}) collective-permute-start(f32[512,128]{1,0:T(8,128)S(1)} %bitcast.71), channel_id=1, source_target_pairs={{0,1},{1,0},{2,3},{3,2},{4,5},{5,4},{6,7},{7,6},{8,9},{9,8},{10,11... | collective-permute-start | bytes 786440 | tf_op jit(solution)/shard_map/ppermute | solution.py:25
  43.2 21.7 %collective-permute-start.3 = (f32[128,8,128]{2,1,0:T(8,128)S(1)}, f32[128,8,128]{2,1,0:T(8,128)S(1)}, u32[]{:S(2)}, u32[]{:S(2)}) collective-permute-start(f32[128,8,128]{2,1,0:T(8,128)S(1)} %get-tuple-element.89), channel_id=1, source_target_pairs={{0,4},{4,0},{8,12},{12,8},{16,20},{20,16},{24,28},{28,24},{1,5},{5... | collective-permute-start | bytes 1572872 | tf_op jit(solution)/shard_map/ppermute | solution.py:25
  64.9 5.6 %copy-start.10 = (f32[128,8,128]{2,1,0:T(8,128)}, f32[128,8,128]{2,1,0:T(8,128)S(1)}, u32[]{:S(2)}) copy-start(f32[128,8,128]{2,1,0:T(8,128)S(1)} %collective-permute-done.3) | copy-start | bytes 1572868
  65.1 7.8 %collective-permute-start.5 = (f16[1,528,128]{2,1,0:T(8,128)(2,1)S(1)}, f16[1,528,128]{2,1,0:T(8,128)(2,1)S(1)}, u32[]{:S(2)}, u32[]{:S(2)}) collective-permute-start(f16[1,528,128]{2,1,0:T(8,128)(2,1)S(1)} %pad_maximum_fusion.5), channel_id=1, source_target_pairs={{0,1},{1,0},{2,3},{3,2},{4,5},{5,4},{6,7},{7,6},{8,9},{9,8},{10,11... | collective-permute-start | bytes 405512 | tf_op jit(solution)/shard_map/ppermute | solution.py:25
  65.7 2.0 %collective-permute-start.6 = (f32[148,8,128]{2,1,0:T(8,128)S(1)}, f32[148,8,128]{2,1,0:T(8,128)S(1)}, u32[]{:S(2)}, u32[]{:S(2)}) collective-permute-start(f32[148,8,128]{2,1,0:T(8,128)S(1)} %get-tuple-element.108), channel_id=1, source_target_pairs={{0,4},{4,0},{8,12},{12,8},{16,20},{20,16},{24,28},{28,24},{1,5},{5... | collective-permute-start | bytes 1818632 | tf_op jit(solution)/shard_map/ppermute | solution.py:25
  66.1 12.6 %collective-permute-start.13 = (f16[1,1040,128]{2,1,0:T(8,128)(2,1)S(1)}, f16[1,1040,128]{2,1,0:T(8,128)(2,1)S(1)}, u32[]{:S(2)}, u32[]{:S(2)}) collective-permute-start(f16[1,1040,128]{2,1,0:T(8,128)(2,1)S(1)} %pad_maximum_fusion.1), channel_id=1, source_target_pairs={{0,16},{4,20},{8,24},{12,28},{16,0},{20,4},{24,8},{28,12},{1,17},{... | collective-permute-start | bytes 798728 | tf_op jit(solution)/shard_map/ppermute | solution.py:596
  67.8 5.9 %collective-permute-start.7 = (f32[20,8,128]{2,1,0:T(8,128)S(1)}, f32[20,8,128]{2,1,0:T(8,128)S(1)}, u32[]{:S(2)}, u32[]{:S(2)}) collective-permute-start(f32[20,8,128]{2,1,0:T(8,128)S(1)} %slice_add_fusion.1), channel_id=1, source_target_pairs={{0,2},{1,3},{2,0},{3,1},{4,6},{5,7},{6,4},{7,5},{8,10},{9,11},{10,... | collective-permute-start | bytes 245768 | tf_op jit(solution)/shard_map/ppermute | solution.py:25
  71.4 12.2 %collective-permute-start.12 = (f16[1,1040,128]{2,1,0:T(8,128)(2,1)}, f16[1,1040,128]{2,1,0:T(8,128)(2,1)}, u32[]{:S(2)}, u32[]{:S(2)}) collective-permute-start(f16[1,1040,128]{2,1,0:T(8,128)(2,1)} %pad_maximum_fusion), channel_id=1, source_target_pairs={{0,8},{4,12},{8,0},{12,4},{16,24},{20,28},{24,16},{28,20},{1,9},{5... | collective-permute-start | bytes 798728 | tf_op jit(solution)/shard_map/ppermute | solution.py:25
  73.9 9.6 %collective-permute-start.8 = (f16[2,272,128]{2,1,0:T(8,128)(2,1)S(1)}, f16[2,272,128]{2,1,0:T(8,128)(2,1)S(1)}, u32[]{:S(2)}, u32[]{:S(2)}) collective-permute-start(f16[2,272,128]{2,1,0:T(8,128)(2,1)S(1)} %pad_maximum_fusion.3), channel_id=1, source_target_pairs={{0,2},{1,3},{2,0},{3,1},{4,6},{5,7},{6,4},{7,5},{8,10},{9,11},{10,... | collective-permute-start | bytes 417800 | tf_op jit(solution)/shard_map/ppermute | solution.py:25
  76.3 6.6 %collective-permute-start.11 = (f32[20,8,128]{2,1,0:T(8,128)S(1)}, f32[20,8,128]{2,1,0:T(8,128)S(1)}, u32[]{:S(2)}, u32[]{:S(2)}) collective-permute-start(f32[20,8,128]{2,1,0:T(8,128)S(1)} %add.73), channel_id=1, source_target_pairs={{0,24},{4,28},{8,16},{12,20},{16,8},{20,12},{24,0},{28,4},{1,25},{... | collective-permute-start | bytes 245768 | tf_op jit(solution)/shard_map/ppermute | solution.py:25
  78.1 5.2 %collective-permute-start.10 = (f32[20,8,128]{2,1,0:T(8,128)S(1)}, f32[20,8,128]{2,1,0:T(8,128)S(1)}, u32[]{:S(2)}, u32[]{:S(2)}) collective-permute-start(f32[20,8,128]{2,1,0:T(8,128)S(1)} %add.73), channel_id=1, source_target_pairs={{0,8},{4,12},{8,0},{12,4},{16,24},{20,28},{24,16},{28,20},{1,9},{5... | collective-permute-start | bytes 245768 | tf_op jit(solution)/shard_map/ppermute | solution.py:25
  78.6 4.9 %collective-permute-start.9 = (f32[20,8,128]{2,1,0:T(8,128)S(1)}, f32[20,8,128]{2,1,0:T(8,128)}, u32[]{:S(2)}, u32[]{:S(2)}) collective-permute-start(f32[20,8,128]{2,1,0:T(8,128)S(1)} %add.73), channel_id=1, source_target_pairs={{0,16},{4,20},{8,24},{12,28},{16,0},{20,4},{24,8},{28,12},{1,17},{... | collective-permute-start | bytes 245768 | tf_op jit(solution)/shard_map/ppermute | solution.py:25
  84.5 9.2 %collective-permute-start.17 = (f32[20,8,128]{2,1,0:T(8,128)S(1)}, f32[20,8,128]{2,1,0:T(8,128)S(1)}, u32[]{:S(2)}, u32[]{:S(2)}) collective-permute-start(f32[20,8,128]{2,1,0:T(8,128)S(1)} %add_add_fusion), channel_id=1, source_target_pairs={{0,5},{1,4},{2,7},{3,6},{4,1},{5,0},{6,3},{7,2},{8,13},{9,12},{10,... | collective-permute-start | bytes 245768 | tf_op jit(solution)/shard_map/ppermute | solution.py:592
  85.8 7.9 %collective-permute-start.16 = (f32[20,8,128]{2,1,0:T(8,128)S(1)}, f32[20,8,128]{2,1,0:T(8,128)S(1)}, u32[]{:S(2)}, u32[]{:S(2)}) collective-permute-start(f32[20,8,128]{2,1,0:T(8,128)S(1)} %add_add_fusion), channel_id=1, source_target_pairs={{0,4},{4,0},{8,12},{12,8},{16,20},{20,16},{24,28},{28,24},{1,5},{5... | collective-permute-start | bytes 245768 | tf_op jit(solution)/shard_map/ppermute | solution.py:25
  87.6 6.1 %collective-permute-start.15 = (f32[20,8,128]{2,1,0:T(8,128)S(1)}, f32[20,8,128]{2,1,0:T(8,128)S(1)}, u32[]{:S(2)}, u32[]{:S(2)}) collective-permute-start(f32[20,8,128]{2,1,0:T(8,128)S(1)} %add_add_fusion), channel_id=1, source_target_pairs={{0,1},{1,0},{2,3},{3,2},{4,5},{5,4},{6,7},{7,6},{8,9},{9,8},{10,11... | collective-permute-start | bytes 245768 | tf_op jit(solution)/shard_map/ppermute | solution.py:25
  87.9 10.6 %collective-permute-start.14 = (f16[2,272,128]{2,1,0:T(8,128)(2,1)S(1)}, f16[2,272,128]{2,1,0:T(8,128)(2,1)S(1)}, u32[]{:S(2)}, u32[]{:S(2)}) collective-permute-start(f16[2,272,128]{2,1,0:T(8,128)(2,1)S(1)} %pad_maximum_fusion.4), channel_id=1, source_target_pairs={{0,18},{1,19},{2,16},{3,17},{4,22},{5,23},{6,20},{7,21},{8,26},{9,... | collective-permute-start | bytes 417800 | tf_op jit(solution)/shard_map/ppermute | solution.py:592
  (6 other events, 14.7 us)

commit v5 on v4

--- a/solution.py
+++ b/solution.py
@@ -12,9 +12,11 @@
 CLS_PAD = 32
 CHUNKS = ((0, 3), (1, 2))
 ZC = 16
-RUNS = 16
+RUNS = 64
 GROUP = 4
 ROWS = RUNS * 2 * ZC
+SPAN = 1024
+SEL_ROWS = SPAN // ZC
 STRIP = 32
 LEVEL_TOPS = tuple(2.0 ** e for e in (4, -7, -18, -29, -40))
 LEVEL_BITS = (11, 22, 33, 44, 55)
@@ -268,8 +270,8 @@
 
     groups = RUNS // GROUP
     n_ch = w_in_ref.shape[0]
-    sel_row = lax.broadcasted_iota(jnp.int32, (2 * RUNS, ROWS), 0)
-    sample = lax.broadcasted_iota(jnp.int32, (2 * RUNS, ROWS), 1)
+    sel_row = lax.broadcasted_iota(jnp.int32, (SEL_ROWS, ROWS), 0)
+    sample = jnp.bitwise_and(lax.broadcasted_iota(jnp.int32, (SEL_ROWS, ROWS), 1), SPAN - 1)
     sample_run = lax.shift_right_logical(sample, 7) * GROUP + lax.shift_right_logical(jnp.bitwise_and(sample, 63), 4)
     sample_row = 2 * sample_run + jnp.bitwise_and(lax.shift_right_logical(sample, 6), 1)
     select = jnp.where(sel_row == sample_row, 1.0, 0.0).astype(jnp.bfloat16)
@@ -332,10 +334,12 @@
 
     def back(b, out):
         left_ref, dpre_ref = out
-        dpre = dpre_ref[...]
-        sums = jnp.dot(left_ref[...], dpre, preferred_element_type=jnp.float32)
-        w_in_acc[...] += sums[0:n_ch]
-        hw_acc[pl.ds(pl.multiple_of(2 * RUNS * b, 2 * RUNS), 2 * RUNS), :] = sums[n_ch:]
+        for k in range(ROWS // SPAN):
+            cut = slice(SPAN * k, SPAN * (k + 1))
+            sums = jnp.dot(left_ref[:, cut], dpre_ref[cut, :], preferred_element_type=jnp.float32)
+            w_in_acc[...] += sums[0:n_ch]
+            at = pl.multiple_of(2 * RUNS * b, 2 * RUNS) + SEL_ROWS * k
+            hw_acc[pl.ds(at, SEL_ROWS), :] = sums[n_ch:]
         runs = read_runs(ids_ref, RUNS * b, RUNS)
         for g in range(groups):
             dfeat = jnp.dot(dpre_ref[g * 128:(g + 1) * 128, :], w_in_t_ref[...], preferred_element_type=jnp.float32)
@@ -535,7 +539,7 @@
     mid = wgt_rows // 2
     buf = [pltpu.VMEM((ROWS, channels), bf16), pltpu.VMEM((ROWS, hidden), bf16),
            pltpu.VMEM((ROWS, hidden), f32), pltpu.VMEM((CLS_ROWS, ROWS), f32)]
-    out_buf = [pltpu.VMEM((channels + 2 * RUNS, ROWS), bf16), pltpu.VMEM((ROWS, hidden), bf16)]
+    out_buf = [pltpu.VMEM((channels + SEL_ROWS, ROWS), bf16), pltpu.VMEM((ROWS, hidden), bf16)]
     work = [pltpu.VMEM((n_hw, channels), f32), pltpu.VMEM((2 * rows_blk, ZC, channels), f32),
             pltpu.VMEM((n_lab, 128), f32), pltpu.VMEM((n_hw, hidden), f32),
             pltpu.VMEM((channels, hidden), f32), pltpu.VMEM((CLS_PAD, hidden), f32),
@@ -549,7 +553,7 @@
             functools.partial(decode_kernel, chunk=CHUNKS[n], first=n == 0, rows_blk=rows_blk,
                               slots=slots, pair_cols=pair_cols), "decode%d" % n,
             (meta,) + sources + (wzf0, wzf1)[n:n + 1] + shared,
-            [smem] + [vmem] * (len(sources) + 8 - 1), outs, work, 22 * 10**9, 20)
+            [smem] + [vmem] * (len(sources) + 8 - 1), outs, work, 22 * 10**9, 28)
 
     wz0a, wz0b, zh0a, zh0b, hw0, wgt0 = decode(
         0, (own_hw, recv_hw, own0, recv0), sums + [((n_hw, channels), f32), ((wgt_rows, hidden), f32)])

time: 100 us -> 92.3 us (0.923)
  Pallas kernels: 57 us -> 49 us
    pallas_call x7, Pallas kernels: 57 us -> 49 us  [call(): pl.pallas_call(kernel, out_shape=[jax.ShapeDtypeStruct(shape, kind) for s...]
  transfers between devices with their start and end apart: 18 -> 18, of which waited for: 7 -> 7; matrix products, arithmetic and copies ran while one was open for 4% -> 4% of each run, Pallas kernels for 53% -> 49%
where the time goes in v5:
time: 92.3 us; the launch traced here: 92 us
  Pallas kernels  49 us (53%)
  starting transfers between devices  21.4 us (23%)
  waiting for transfers between devices  12.6 us (14%)
  other arithmetic  4.75 us (5%)
  local copies, waits for them, and re-layouts  2.37 us (3%)
  between operations  1.86 us (2%)
    pallas_call x7, Pallas kernels, call(): pl.pallas_call(kernel, out_shape=[jax.ShapeDtypeStruct(shape, kind) for s...  49 us
    ppermute x12, starting transfers between devices, ppermute_xor(): return lax.ppermute(value, axis, [(i, i ^ mask) for i in range(size)])  14.4 us
    ppermute x12, waiting for transfers between devices, ppermute_xor(): return lax.ppermute(value, axis, [(i, i ^ mask) for i in range(size)])  5.17 us
    ppermute x2, waiting for transfers between devices, corner(): return lax.ppermute(value, ('ha', 'wa'), pairs)  4.87 us
    ppermute x1, starting transfers between devices, local(): recv0 = lax.ppermute(send0, 'ha', swap_y)  3.03 us
    ppermute x1, waiting for transfers between devices, local(): recv_hw = lax.ppermute(send_hw, 'ha', swap_y)  2.51 us
  transfers between devices with their start and end apart: 18, of which 7 were waited for; matrix products, arithmetic and copies ran while one was open for 4% of the time, Pallas kernels for 49%

profile of v5, /device:TPU:0, one launch (start us, length us, event | category | flops | bytes accessed | tf_op | source)
XLA Modules:
  0.0 92.0 jit_solution(4668534539507075349)
XLA Ops:
  2.1 2.9 %pack_plane.1 = bf16[640,128]{1,0:T(8,128)(2,1)} custom-call(s32[10]{0:T(128)} %stack.48.meta_ref.refs_0_, bf16[2048,128]{1,0:T(8,128)(2,1)} %bitcast.67, s32[512,128]{1,0:T(8,128)} %bitcast.69), custom_call_target="tpu_custom_call" | custom-call | flops 2000000000 | bytes 1048576 | tf_op jit(solution)/shard_map/pack_plane/pallas_call | solution.py:502
  5.0 3.0 %collective-permute-start = (bf16[640,128]{1,0:T(8,128)(2,1)}, bf16[640,128]{1,0:T(8,128)(2,1)S(1)}, u32[]{:S(2)}, u32[]{:S(2)}) collective-permute-start(bf16[640,128]{1,0:T(8,128)(2,1)} %pack_plane.1), channel_id=1, source_target_pairs={{0,16},{4,20},{8,24},{12,28},{16,0},{20,4},{24,8},{28,12},{1,17},{... | collective-permute-start | bytes 491528 | tf_op jit(solution)/shard_map/ppermute | solution.py:517
  8.1 2.7 %pack_rows.1 = bf16[1040,128]{1,0:T(8,128)(2,1)S(1)} custom-call(s32[10]{0:T(128)S(1)} %copy-done, bf16[4096,128]{1,0:T(8,128)(2,1)S(1)} %bitcast.65, s32[1,512]{1,0:T(1,128)S(1)} %copy-done.7), custom_call_target="tpu_custom_call" | custom-call | flops 3000000000 | bytes 1048576 | tf_op jit(solution)/shard_map/pack_rows/pallas_call | solution.py:502
  10.9 1.6 %copy-done.1 = bf16[128,64,128]{2,1,0:T(8,128)(2,1)S(1)} copy-done((bf16[128,64,128]{2,1,0:T(8,128)(2,1)S(1)}, bf16[128,64,128]{2,1,0:T(8,128)(2,1)}, u32[]{:S(2)}) %copy-start.1) | copy-done | bytes 2097176
  12.5 3.6 %pack_own.1 = (bf16[1040,128]{1,0:T(8,128)(2,1)S(1)}, bf16[640,128]{1,0:T(8,128)(2,1)S(1)}, bf16[640,128]{1,0:T(8,128)(2,1)S(1)}, bf16[640,128]{1,0:T(8,128)(2,1...) custom-call(s32[10]{0:T(128)S(1)} %copy-done, ...), custom_call_target="tpu_custom_call" | custom-call | flops 3000000000 | bytes 1048576 | tf_op jit(solution)/shard_map/pack_own/pallas_call | solution.py:502
  16.2 2.5 %collective-permute-done.1.refs_2_ = bf16[1040,128]{1,0:T(8,128)(2,1)S(1)} collective-permute-done((bf16[1040,128]{1,0:T(8,128)(2,1)S(1)}, bf16[1040,128]{1,0:T(8,128)(2,1)S(1)}, u32[]{:S(2)}, u32[]{:S(2)}) %collective-permute-start.1) | collective-permute-done | bytes 266272 | tf_op jit(solution)/shard_map/ppermute | solution.py:522
  18.7 1.2 %collective-permute-start.2 = (bf16[640,128]{1,0:T(8,128)(2,1)S(1)}, bf16[640,128]{1,0:T(8,128)(2,1)S(1)}, u32[]{:S(2)}, u32[]{:S(2)}) collective-permute-start(bf16[640,128]{1,0:T(8,128)(2,1)S(1)} %get-tuple-element.73), channel_id=1, source_target_pairs={{0,16},{4,20},{8,24},{12,28},{16,0},{20,4},{24,8},{28,12},{1,17},{... | collective-permute-start | bytes 491528 | tf_op jit(solution)/shard_map/ppermute | solution.py:535
  19.9 17.6 %decode0.1 = (f32[128,8,128]{2,1,0:T(8,128)S(1)}, f32[128,8,128]{2,1,0:T(8,128)S(1)}, f32[64,8,128]{2,1,0:T(8,128)S(1)}, f32[64,8,128]{2,1,0:T(8,128)S(1)}, f32[...) custom-call(s32[10]{0:T(128)S(1)} %copy-done, bf16[1040,128]{1,0:T(8,128)(2,1)S(1)} %get-tuple-element.74.refs_1_, ...), custom_call_target="tpu_custom_call" | custom-call | flops 22000001024 | bytes 1048576 | tf_op jit(solution)/shard_map/decode0/pallas_call | solution.py:502
  37.5 1.6 %collective-permute-start.4 = (f32[512,128]{1,0:T(8,128)S(1)}, f32[512,128]{1,0:T(8,128)S(1)}, u32[]{:S(2)}, u32[]{:S(2)}) collective-permute-start(f32[512,128]{1,0:T(8,128)S(1)} %bitcast.71), channel_id=1, source_target_pairs={{0,1},{1,0},{2,3},{3,2},{4,5},{5,4},{6,7},{7,6},{8,9},{9,8},{10,11... | collective-permute-start | bytes 786440 | tf_op jit(solution)/shard_map/ppermute | solution.py:27
  39.2 17.7 %decode1.1 = (f32[128,8,128]{2,1,0:T(8,128)S(1)}, f32[148,8,128]{2,1,0:T(8,128)S(1)}, f32[64,8,128]{2,1,0:T(8,128)S(1)}, f32[64,8,128]{2,1,0:T(8,128)S(1)}, f32[...) custom-call(s32[10]{0:T(128)S(1)} %copy-done, bf16[1040,128]{1,0:T(8,128)(2,1)S(1)} %get-tuple-element.74.refs_1_, ...), custom_call_target="tpu_custom_call" | custom-call | flops 22000001024 | bytes 1048576 | tf_op jit(solution)/shard_map/decode1/pallas_call | solution.py:502
  59.7 2.7 %collective-permute-start.7 = (f32[20,8,128]{2,1,0:T(8,128)S(1)}, f32[20,8,128]{2,1,0:T(8,128)S(1)}, u32[]{:S(2)}, u32[]{:S(2)}) collective-permute-start(f32[20,8,128]{2,1,0:T(8,128)S(1)} %slice_add_fusion.1), channel_id=1, source_target_pairs={{0,2},{1,3},{2,0},{3,1},{4,6},{5,7},{6,4},{7,5},{8,10},{9,11},{10,... | collective-permute-start | bytes 245768 | tf_op jit(solution)/shard_map/ppermute | solution.py:27
  63.4 1.5 %collective-permute-start.12 = (f16[1,1040,128]{2,1,0:T(8,128)(2,1)}, f16[1,1040,128]{2,1,0:T(8,128)(2,1)}, u32[]{:S(2)}, u32[]{:S(2)}) collective-permute-start(f16[1,1040,128]{2,1,0:T(8,128)(2,1)} %pad_maximum_fusion), channel_id=1, source_target_pairs={{0,8},{4,12},{8,0},{12,4},{16,24},{20,28},{24,16},{28,20},{1,9},{5... | collective-permute-start | bytes 798728 | tf_op jit(solution)/shard_map/ppermute | solution.py:27
  65.9 2.4 %collective-permute-start.8 = (f16[2,272,128]{2,1,0:T(8,128)(2,1)S(1)}, f16[2,272,128]{2,1,0:T(8,128)(2,1)S(1)}, u32[]{:S(2)}, u32[]{:S(2)}) collective-permute-start(f16[2,272,128]{2,1,0:T(8,128)(2,1)S(1)} %pad_maximum_fusion.3), channel_id=1, source_target_pairs={{0,2},{1,3},{2,0},{3,1},{4,6},{5,7},{6,4},{7,5},{8,10},{9,11},{10,... | collective-permute-start | bytes 417800 | tf_op jit(solution)/shard_map/ppermute | solution.py:27
  68.3 1.8 %collective-permute-start.11 = (f32[20,8,128]{2,1,0:T(8,128)S(1)}, f32[20,8,128]{2,1,0:T(8,128)S(1)}, u32[]{:S(2)}, u32[]{:S(2)}) collective-permute-start(f32[20,8,128]{2,1,0:T(8,128)S(1)} %add.73), channel_id=1, source_target_pairs={{0,24},{4,28},{8,16},{12,20},{16,8},{20,12},{24,0},{28,4},{1,25},{... | collective-permute-start | bytes 245768 | tf_op jit(solution)/shard_map/ppermute | solution.py:27
  70.7 1.2 %collective-permute-start.9 = (f32[20,8,128]{2,1,0:T(8,128)S(1)}, f32[20,8,128]{2,1,0:T(8,128)}, u32[]{:S(2)}, u32[]{:S(2)}) collective-permute-start(f32[20,8,128]{2,1,0:T(8,128)S(1)} %add.73), channel_id=1, source_target_pairs={{0,16},{4,20},{8,24},{12,28},{16,0},{20,4},{24,8},{28,12},{1,17},{... | collective-permute-start | bytes 245768 | tf_op jit(solution)/shard_map/ppermute | solution.py:27
  71.9 3.0 %collective-permute-done.11 = f32[20,8,128]{2,1,0:T(8,128)S(1)} collective-permute-done((f32[20,8,128]{2,1,0:T(8,128)S(1)}, f32[20,8,128]{2,1,0:T(8,128)S(1)}, u32[]{:S(2)}, u32[]{:S(2)}) %collective-permute-start.11) | collective-permute-done | bytes 81952 | tf_op jit(solution)/shard_map/ppermute | solution.py:27
  75.6 0.9 add_add_fusion
  76.5 1.3 %collective-permute-start.17 = (f32[20,8,128]{2,1,0:T(8,128)S(1)}, f32[20,8,128]{2,1,0:T(8,128)S(1)}, u32[]{:S(2)}, u32[]{:S(2)}) collective-permute-start(f32[20,8,128]{2,1,0:T(8,128)S(1)} %add_add_fusion), channel_id=1, source_target_pairs={{0,5},{1,4},{2,7},{3,6},{4,1},{5,0},{6,3},{7,2},{8,13},{9,12},{10,... | collective-permute-start | bytes 245768 | tf_op jit(solution)/shard_map/ppermute | solution.py:596
  77.8 1.9 %collective-permute-start.16 = (f32[20,8,128]{2,1,0:T(8,128)S(1)}, f32[20,8,128]{2,1,0:T(8,128)S(1)}, u32[]{:S(2)}, u32[]{:S(2)}) collective-permute-start(f32[20,8,128]{2,1,0:T(8,128)S(1)} %add_add_fusion), channel_id=1, source_target_pairs={{0,4},{4,0},{8,12},{12,8},{16,20},{20,16},{24,28},{28,24},{1,5},{5... | collective-permute-start | bytes 245768 | tf_op jit(solution)/shard_map/ppermute | solution.py:27
  80.5 1.0 %convert_element_type.48 = f32[1,1040,128]{2,1,0:T(8,128)S(1)} convert(f16[1,1040,128]{2,1,0:T(8,128)(2,1)} %collective-permute-done.12) | non-fusion elementwise | flops 133120 | bytes 798720 | tf_op jit(solution)/shard_map/convert_element_type | solution.py:205
  81.6 1.0 %fusion.1 = f32[128,8,128]{2,1,0:T(8,128)} fusion(f32[1,1040,128]{2,1,0:T(8,128)S(1)} %convert_element_type.48, f32[128]{0:T(128)S(1)} %fusion.15, pred[]{:T(512)S(6)} %or.3, f32[128,8,128]{2,1,0:T(8,128)S(1)} %get-tuple-element.112, f32[128,8,128]{2,1,0:T(8,128)S(1)} %copy-done.11, f32[128,8,128]{2,1,0:T(8,128)S(1)} %get-tuple-element.111, ...), kind=kLoop, calls=%fused_computation.2 | loop fusion | flops 655360 | bytes 3146241 | tf_op jit(solution)/shard_map/add | solution.py:620
  82.5 3.1 %place.1 = f32[4096,128]{1,0:T(8,128)} custom-call(s32[10]{0:T(128)S(1)} %copy-done, s32[1,512]{1,0:T(1,128)S(1)} %copy-done.7, f32[1024,128]{1,0:T(8,128)S(1)} %get-tuple-element.102.mine_ref, f32[1024,128]{1,0:T(8,128)S(1)} %fusion.2.recv_ref), custom_call_target="tpu_custom_call" | custom-call | flops 3000000000 | bytes 1048576 | tf_op jit(solution)/shard_map/place/pallas_call | solution.py:502
  85.7 4.9 %collective-permute-done.14 = f16[2,272,128]{2,1,0:T(8,128)(2,1)S(1)} collective-permute-done((f16[2,272,128]{2,1,0:T(8,128)(2,1)S(1)}, f16[2,272,128]{2,1,0:T(8,128)(2,1)S(1)}, u32[]{:S(2)}, u32[]{:S(2)}) %collective-permute-start.14) | collective-permute-done | bytes 139296 | tf_op jit(solution)/shard_map/ppermute | solution.py:596
  90.7 1.3 %finish.1 = (f32[16,32,128]{2,1,0:T(8,128)}, f32[128,256]{1,0:T(8,128)}, f32[1,256]{1,0:T(1,128)}, f32[18,256]{1,0:T(8,128)}, f32[1,18]{1,0:T(1,128)}) custom-call(s32[10]{0:T(128)S(1)} %copy-done, f32[2,256,128]{2,1,0:T(8,128)S(1)} %slice_multiply_fusion.2.zh_ref, f32[20,8,128]{2,1,0:T(8,128)S(1)} %add.80.w_mine_ref, f32[20,8,128]{2,1,0:T(8,128)S(1)} %add.81.w_other_ref), custom_call_target="tpu_custom_call" | custom-call | flops 1000000000 | bytes 1048576 | tf_op jit(solution)/shard_map/finish/pallas_call | solution.py:502
  (94 shorter events, 7.7 us)
Async XLA Ops:
  2.1 5.9 %copy-start = (s32[10]{0:T(128)S(1)}, s32[10]{0:T(128)}, u32[]{:S(2)}) copy-start(s32[10]{0:T(128)} %stack.48.meta_ref.refs_0_) | copy-start | bytes 124
  2.1 5.9 %copy-start.2 = (bf16[32,128,128]{2,1,0:T(8,128)(2,1)S(1)}, bf16[32,128,128]{2,1,0:T(8,128)(2,1)}, u32[]{:S(2)}) copy-start(bf16[32,128,128]{2,1,0:T(8,128)(2,1)} %param.10) | copy-start | bytes 3145732
  2.1 5.9 %copy-start.7 = (s32[1,512]{1,0:T(1,128)S(1)}, s32[1,512]{1,0:T(1,128)}, u32[]{:S(2)}) copy-start(s32[1,512]{1,0:T(1,128)} %rid_ref.1) | copy-start | bytes 6148
  5.0 11.2 %collective-permute-start = (bf16[640,128]{1,0:T(8,128)(2,1)}, bf16[640,128]{1,0:T(8,128)(2,1)S(1)}, u32[]{:S(2)}, u32[]{:S(2)}) collective-permute-start(bf16[640,128]{1,0:T(8,128)(2,1)} %pack_plane.1), channel_id=1, source_target_pairs={{0,16},{4,20},{8,24},{12,28},{16,0},{20,4},{24,8},{28,12},{1,17},{... | collective-permute-start | bytes 491528 | tf_op jit(solution)/shard_map/ppermute | solution.py:517
  8.0 2.8 %copy-start.3 = (bf16[64,32,128]{2,1,0:T(8,128)(2,1)S(1)}, bf16[64,32,128]{2,1,0:T(8,128)(2,1)}, u32[]{:S(2)}) copy-start(bf16[64,32,128]{2,1,0:T(8,128)(2,1)} %param.11) | copy-start | bytes 1572868
  8.0 2.8 %copy-start.4 = (s32[1,512,128]{2,1,0:T(8,128)S(1)}, s32[1,512,128]{2,1,0:T(8,128)}, u32[]{:S(2)}) copy-start(s32[1,512,128]{2,1,0:T(8,128)} %param.19) | copy-start | bytes 786436
  10.7 7.9 %collective-permute-start.1 = (bf16[1040,128]{1,0:T(8,128)(2,1)S(1)}, bf16[1040,128]{1,0:T(8,128)(2,1)S(1)}, u32[]{:S(2)}, u32[]{:S(2)}) collective-permute-start(bf16[1040,128]{1,0:T(8,128)(2,1)S(1)} %pack_rows.1), channel_id=1, source_target_pairs={{0,16},{4,20},{8,24},{12,28},{16,0},{20,4},{24,8},{28,12},{1,17},{... | collective-permute-start | bytes 798728 | tf_op jit(solution)/shard_map/ppermute | solution.py:522
  18.7 18.8 %collective-permute-start.2 = (bf16[640,128]{1,0:T(8,128)(2,1)S(1)}, bf16[640,128]{1,0:T(8,128)(2,1)S(1)}, u32[]{:S(2)}, u32[]{:S(2)}) collective-permute-start(bf16[640,128]{1,0:T(8,128)(2,1)S(1)} %get-tuple-element.73), channel_id=1, source_target_pairs={{0,16},{4,20},{8,24},{12,28},{16,0},{20,4},{24,8},{28,12},{1,17},{... | collective-permute-start | bytes 491528 | tf_op jit(solution)/shard_map/ppermute | solution.py:535
  37.5 19.4 %collective-permute-start.4 = (f32[512,128]{1,0:T(8,128)S(1)}, f32[512,128]{1,0:T(8,128)S(1)}, u32[]{:S(2)}, u32[]{:S(2)}) collective-permute-start(f32[512,128]{1,0:T(8,128)S(1)} %bitcast.71), channel_id=1, source_target_pairs={{0,1},{1,0},{2,3},{3,2},{4,5},{5,4},{6,7},{7,6},{8,9},{9,8},{10,11... | collective-permute-start | bytes 786440 | tf_op jit(solution)/shard_map/ppermute | solution.py:27
  39.2 17.8 %collective-permute-start.3 = (f32[128,8,128]{2,1,0:T(8,128)S(1)}, f32[128,8,128]{2,1,0:T(8,128)S(1)}, u32[]{:S(2)}, u32[]{:S(2)}) collective-permute-start(f32[128,8,128]{2,1,0:T(8,128)S(1)} %get-tuple-element.89), channel_id=1, source_target_pairs={{0,4},{4,0},{8,12},{12,8},{16,20},{20,16},{24,28},{28,24},{1,5},{5... | collective-permute-start | bytes 1572872 | tf_op jit(solution)/shard_map/ppermute | solution.py:27
  56.9 5.6 %copy-start.10 = (f32[128,8,128]{2,1,0:T(8,128)}, f32[128,8,128]{2,1,0:T(8,128)S(1)}, u32[]{:S(2)}) copy-start(f32[128,8,128]{2,1,0:T(8,128)S(1)} %collective-permute-done.3) | copy-start | bytes 1572868
  57.2 7.7 %collective-permute-start.5 = (f16[1,528,128]{2,1,0:T(8,128)(2,1)S(1)}, f16[1,528,128]{2,1,0:T(8,128)(2,1)S(1)}, u32[]{:S(2)}, u32[]{:S(2)}) collective-permute-start(f16[1,528,128]{2,1,0:T(8,128)(2,1)S(1)} %pad_maximum_fusion.5), channel_id=1, source_target_pairs={{0,1},{1,0},{2,3},{3,2},{4,5},{5,4},{6,7},{7,6},{8,9},{9,8},{10,11... | collective-permute-start | bytes 405512 | tf_op jit(solution)/shard_map/ppermute | solution.py:27
  57.7 2.0 %collective-permute-start.6 = (f32[148,8,128]{2,1,0:T(8,128)S(1)}, f32[148,8,128]{2,1,0:T(8,128)S(1)}, u32[]{:S(2)}, u32[]{:S(2)}) collective-permute-start(f32[148,8,128]{2,1,0:T(8,128)S(1)} %get-tuple-element.108), channel_id=1, source_target_pairs={{0,4},{4,0},{8,12},{12,8},{16,20},{20,16},{24,28},{28,24},{1,5},{5... | collective-permute-start | bytes 1818632 | tf_op jit(solution)/shard_map/ppermute | solution.py:27
  58.1 12.6 %collective-permute-start.13 = (f16[1,1040,128]{2,1,0:T(8,128)(2,1)S(1)}, f16[1,1040,128]{2,1,0:T(8,128)(2,1)S(1)}, u32[]{:S(2)}, u32[]{:S(2)}) collective-permute-start(f16[1,1040,128]{2,1,0:T(8,128)(2,1)S(1)} %pad_maximum_fusion.1), channel_id=1, source_target_pairs={{0,16},{4,20},{8,24},{12,28},{16,0},{20,4},{24,8},{28,12},{1,17},{... | collective-permute-start | bytes 798728 | tf_op jit(solution)/shard_map/ppermute | solution.py:600
  59.7 5.9 %collective-permute-start.7 = (f32[20,8,128]{2,1,0:T(8,128)S(1)}, f32[20,8,128]{2,1,0:T(8,128)S(1)}, u32[]{:S(2)}, u32[]{:S(2)}) collective-permute-start(f32[20,8,128]{2,1,0:T(8,128)S(1)} %slice_add_fusion.1), channel_id=1, source_target_pairs={{0,2},{1,3},{2,0},{3,1},{4,6},{5,7},{6,4},{7,5},{8,10},{9,11},{10,... | collective-permute-start | bytes 245768 | tf_op jit(solution)/shard_map/ppermute | solution.py:27
  63.4 12.2 %collective-permute-start.12 = (f16[1,1040,128]{2,1,0:T(8,128)(2,1)}, f16[1,1040,128]{2,1,0:T(8,128)(2,1)}, u32[]{:S(2)}, u32[]{:S(2)}) collective-permute-start(f16[1,1040,128]{2,1,0:T(8,128)(2,1)} %pad_maximum_fusion), channel_id=1, source_target_pairs={{0,8},{4,12},{8,0},{12,4},{16,24},{20,28},{24,16},{28,20},{1,9},{5... | collective-permute-start | bytes 798728 | tf_op jit(solution)/shard_map/ppermute | solution.py:27
  65.9 9.7 %collective-permute-start.8 = (f16[2,272,128]{2,1,0:T(8,128)(2,1)S(1)}, f16[2,272,128]{2,1,0:T(8,128)(2,1)S(1)}, u32[]{:S(2)}, u32[]{:S(2)}) collective-permute-start(f16[2,272,128]{2,1,0:T(8,128)(2,1)S(1)} %pad_maximum_fusion.3), channel_id=1, source_target_pairs={{0,2},{1,3},{2,0},{3,1},{4,6},{5,7},{6,4},{7,5},{8,10},{9,11},{10,... | collective-permute-start | bytes 417800 | tf_op jit(solution)/shard_map/ppermute | solution.py:27
  68.3 6.6 %collective-permute-start.11 = (f32[20,8,128]{2,1,0:T(8,128)S(1)}, f32[20,8,128]{2,1,0:T(8,128)S(1)}, u32[]{:S(2)}, u32[]{:S(2)}) collective-permute-start(f32[20,8,128]{2,1,0:T(8,128)S(1)} %add.73), channel_id=1, source_target_pairs={{0,24},{4,28},{8,16},{12,20},{16,8},{20,12},{24,0},{28,4},{1,25},{... | collective-permute-start | bytes 245768 | tf_op jit(solution)/shard_map/ppermute | solution.py:27
  70.1 5.3 %collective-permute-start.10 = (f32[20,8,128]{2,1,0:T(8,128)S(1)}, f32[20,8,128]{2,1,0:T(8,128)S(1)}, u32[]{:S(2)}, u32[]{:S(2)}) collective-permute-start(f32[20,8,128]{2,1,0:T(8,128)S(1)} %add.73), channel_id=1, source_target_pairs={{0,8},{4,12},{8,0},{12,4},{16,24},{20,28},{24,16},{28,20},{1,9},{5... | collective-permute-start | bytes 245768 | tf_op jit(solution)/shard_map/ppermute | solution.py:27
  70.7 4.9 %collective-permute-start.9 = (f32[20,8,128]{2,1,0:T(8,128)S(1)}, f32[20,8,128]{2,1,0:T(8,128)}, u32[]{:S(2)}, u32[]{:S(2)}) collective-permute-start(f32[20,8,128]{2,1,0:T(8,128)S(1)} %add.73), channel_id=1, source_target_pairs={{0,16},{4,20},{8,24},{12,28},{16,0},{20,4},{24,8},{28,12},{1,17},{... | collective-permute-start | bytes 245768 | tf_op jit(solution)/shard_map/ppermute | solution.py:27
  76.5 9.2 %collective-permute-start.17 = (f32[20,8,128]{2,1,0:T(8,128)S(1)}, f32[20,8,128]{2,1,0:T(8,128)S(1)}, u32[]{:S(2)}, u32[]{:S(2)}) collective-permute-start(f32[20,8,128]{2,1,0:T(8,128)S(1)} %add_add_fusion), channel_id=1, source_target_pairs={{0,5},{1,4},{2,7},{3,6},{4,1},{5,0},{6,3},{7,2},{8,13},{9,12},{10,... | collective-permute-start | bytes 245768 | tf_op jit(solution)/shard_map/ppermute | solution.py:596
  77.8 7.9 %collective-permute-start.16 = (f32[20,8,128]{2,1,0:T(8,128)S(1)}, f32[20,8,128]{2,1,0:T(8,128)S(1)}, u32[]{:S(2)}, u32[]{:S(2)}) collective-permute-start(f32[20,8,128]{2,1,0:T(8,128)S(1)} %add_add_fusion), channel_id=1, source_target_pairs={{0,4},{4,0},{8,12},{12,8},{16,20},{20,16},{24,28},{28,24},{1,5},{5... | collective-permute-start | bytes 245768 | tf_op jit(solution)/shard_map/ppermute | solution.py:27
  79.6 6.0 %collective-permute-start.15 = (f32[20,8,128]{2,1,0:T(8,128)S(1)}, f32[20,8,128]{2,1,0:T(8,128)S(1)}, u32[]{:S(2)}, u32[]{:S(2)}) collective-permute-start(f32[20,8,128]{2,1,0:T(8,128)S(1)} %add_add_fusion), channel_id=1, source_target_pairs={{0,1},{1,0},{2,3},{3,2},{4,5},{5,4},{6,7},{7,6},{8,9},{9,8},{10,11... | collective-permute-start | bytes 245768 | tf_op jit(solution)/shard_map/ppermute | solution.py:27
  80.0 10.6 %collective-permute-start.14 = (f16[2,272,128]{2,1,0:T(8,128)(2,1)S(1)}, f16[2,272,128]{2,1,0:T(8,128)(2,1)S(1)}, u32[]{:S(2)}, u32[]{:S(2)}) collective-permute-start(f16[2,272,128]{2,1,0:T(8,128)(2,1)S(1)} %pad_maximum_fusion.4), channel_id=1, source_target_pairs={{0,18},{1,19},{2,16},{3,17},{4,22},{5,23},{6,20},{7,21},{8,26},{9,... | collective-permute-start | bytes 417800 | tf_op jit(solution)/shard_map/ppermute | solution.py:596
  (6 other events, 14.7 us)
